TPU v7x, 512 devices: a whole 4x8x8 slice. The times are simulated.
512 devices in a mesh: brow: 32 (over y, x_lo, core), bcol: 16 (over z, x_hi).
Axes of the slice: x: 4 (x_hi: 2, x_lo: 2; x = x_hi * 2 + x_lo), y: 8, z: 8, core: 2. Of those that a mesh axis runs over, the one named last changes fastest.
Arguments:
- upper_store: bfloat16 [12288, 12288], P('brow', 'bcol'), may hold values from -0.21875 to 0.21875
- block_mask: int32 [96, 96], P('brow', 'bcol'), may hold values from 0 to 1, as said below
Outputs:
- product: bfloat16 [12288, 12288], P('brow', 'bcol')
Inputs may be any that keep to these rules, and one draw needn't show every extreme that they name: block_mask is 1 on every diagonal block and 0 on every block below the diagonal.
All inputs are finite; a program needn't handle non-finite values.
Results may differ from a plain program's by a relative error of at most 0.001.
Values may be sent and summed in bfloat16 or wider, within the bound.
A program may use at most 64 MiB of HBM per device.

v0:
```python
import jax
import jax.numpy as jnp
from jax import lax
from jax.sharding import PartitionSpec as P


def passed_along(value, axis, steps):
    count = lax.axis_size(axis)
    leading, last = (max(0, -steps), min(count, count - steps))
    return lax.ppermute(value, axis, [(source, source + steps) for source in range(leading, last)])


def shifted(array, axis, by):
    devices = lax.axis_size(axis)
    return lax.ppermute(array, axis, [(i, (i + by) % devices) for i in range(devices)])


def partner_2(value, axis, bit):
    mask = 2**bit
    pairs = [(source, source ^ mask) for source in range(lax.axis_size(axis))]
    return lax.ppermute(value, axis, pairs)


def tile_product(left_tile, right_tile):
    return lax.dot_general(
        left_tile, right_tile, (((1,), (1,)), ((), ())), preferred_element_type=jnp.float32
    )


def per_device(upper_store, block_mask):
    tile_rows, tile_width = upper_store.shape
    row_blocks, col_blocks = block_mask.shape
    block_size = tile_width // col_blocks
    keep_flags = block_mask.astype(jnp.bfloat16)
    masked = (
        upper_store.reshape(row_blocks, block_size, col_blocks, block_size)
        * keep_flags[:, None, :, None]
    ).reshape(tile_rows, tile_width)
    column_index = lax.axis_index("bcol")
    half_index = lax.axis_index("brow") % 2
    bit_count = (lax.axis_size("bcol") - 1).bit_length()
    following = passed_along(masked, "bcol", -1)
    travelling = jnp.stack([masked, following])
    for bit_number in range(bit_count):
        arrived = shifted(travelling, "brow", -(2 << bit_number))
        travelling = jnp.where(column_index >> bit_number & 1 == 1, arrived, travelling)
    partner = partner_2(travelling, "brow", 0)
    first_half = jnp.where(half_index == 0, travelling, partner)
    second_half = jnp.where(half_index == 0, partner, travelling)
    whole_tiles = jnp.concatenate([first_half, second_half], axis=1)
    left_tiles = (masked, following)
    total = tile_product(left_tiles[0], whole_tiles[0]) + tile_product(
        left_tiles[1], whole_tiles[1]
    )
    return total.astype(jnp.bfloat16)


def solution(mesh):
    in_specs = (P("brow", "bcol"), P("brow", "bcol"))
    out_specs = P("brow", "bcol")
    return jax.shard_map(
        per_device, mesh=mesh, in_specs=in_specs, out_specs=out_specs, check_vma=False
    )
```

profile of v0, /device:TPU:223, one launch (start us, length us, event | category | flops | bytes accessed | tf_op | source)
XLA Modules:
  0.0 205.0 jit_solution(3975493783850453017)
XLA Ops:
  0.0 0.0 copy-start.1
  0.0 0.7 convert_element_type.6
  0.8 0.2 mul.15
  0.9 0.2 copy-done.1
  1.1 0.1 bitcast_multiply_fusion
  1.2 3.0 %collective-permute-start = (bf16[384,768]{1,0:T(8,128)(2,1)S(1)}, bf16[384,768]{1,0:T(8,128)(2,1)S(1)}, u32[]{:S(2)}, u32[]{:S(2)}) collective-permute-start(bf16[384,768]{1,0:T(8,128)(2,1)S(1)} %bitcast_multiply_fusion), channel_id=1, source_target_pairs={{1,0},{2,1},{3,2},{4,3},{5,4},{6,5},{7,6},{8,7},{9,8},{10,9},{11,1... | collective-permute-start | bytes 1769480 | tf_op jit(solution)/shard_map/ppermute | solution.py:10
  4.2 16.7 %collective-permute-done = bf16[384,768]{1,0:T(8,128)(2,1)S(1)} collective-permute-done((bf16[384,768]{1,0:T(8,128)(2,1)S(1)}, bf16[384,768]{1,0:T(8,128)(2,1)S(1)}, u32[]{:S(2)}, u32[]{:S(2)}) %collective-permute-start) | collective-permute-done | bytes 589856 | tf_op jit(solution)/shard_map/ppermute | solution.py:10
  20.9 0.1 pad_maximum_fusion.1
  21.0 2.5 %collective-permute-start.1 = (bf16[2,384,768]{2,1,0:T(8,128)(2,1)S(1)}, bf16[2,384,768]{2,1,0:T(8,128)(2,1)S(1)}, u32[]{:S(2)}, u32[]{:S(2)}) collective-permute-start(bf16[2,384,768]{2,1,0:T(8,128)(2,1)S(1)} %pad_maximum_fusion.1), channel_id=1, source_target_pairs={{0,480},{16,496},{32,0},{48,16},{64,32},{80,48},{96,64},{112,80},{... | collective-permute-start | bytes 3538952 | tf_op jit(solution)/shard_map/ppermute | solution.py:15
  23.5 27.4 %collective-permute-done.1 = bf16[2,384,768]{2,1,0:T(8,128)(2,1)S(1)} collective-permute-done((bf16[2,384,768]{2,1,0:T(8,128)(2,1)S(1)}, bf16[2,384,768]{2,1,0:T(8,128)(2,1)S(1)}, u32[]{:S(2)}, u32[]{:S(2)}) %collective-permute-start.1) | collective-permute-done | bytes 1179680 | tf_op jit(solution)/shard_map/ppermute | solution.py:15
  50.9 0.2 broadcast_select_fusion
  51.1 1.9 collective-permute-start.2
  53.0 26.3 %collective-permute-done.2 = bf16[2,384,768]{2,1,0:T(8,128)(2,1)} collective-permute-done((bf16[2,384,768]{2,1,0:T(8,128)(2,1)S(1)}, bf16[2,384,768]{2,1,0:T(8,128)(2,1)}, u32[]{:S(2)}, u32[]{:S(2)}) %collective-permute-start.2) | collective-permute-done | bytes 1179680 | tf_op jit(solution)/shard_map/ppermute | solution.py:15
  79.3 1.4 broadcast_select_fusion.1
  80.7 1.9 collective-permute-start.3
  82.6 53.7 %collective-permute-done.3 = bf16[2,384,768]{2,1,0:T(8,128)(2,1)} collective-permute-done((bf16[2,384,768]{2,1,0:T(8,128)(2,1)S(1)}, bf16[2,384,768]{2,1,0:T(8,128)(2,1)}, u32[]{:S(2)}, u32[]{:S(2)}) %collective-permute-start.3) | collective-permute-done | bytes 1179680 | tf_op jit(solution)/shard_map/ppermute | solution.py:15
  136.3 1.4 broadcast_select_fusion.2
  137.7 0.0 copy-start
  137.7 4.0 %collective-permute-start.4 = (bf16[2,384,768]{2,1,0:T(8,128)(2,1)S(1)}, bf16[2,384,768]{2,1,0:T(8,128)(2,1)S(1)}, u32[]{:S(2)}, u32[]{:S(2)}) collective-permute-start(bf16[2,384,768]{2,1,0:T(8,128)(2,1)S(1)} %broadcast_select_fusion.2), channel_id=1, source_target_pairs={{0,256},{16,272},{32,288},{48,304},{64,320},{80,336},{96,352},{112... | collective-permute-start | bytes 3538952 | tf_op jit(solution)/shard_map/ppermute | solution.py:15
  141.7 0.0 copy-done
  141.7 54.7 %collective-permute-done.4 = bf16[2,384,768]{2,1,0:T(8,128)(2,1)S(1)} collective-permute-done((bf16[2,384,768]{2,1,0:T(8,128)(2,1)S(1)}, bf16[2,384,768]{2,1,0:T(8,128)(2,1)S(1)}, u32[]{:S(2)}, u32[]{:S(2)}) %collective-permute-start.4) | collective-permute-done | bytes 1179680 | tf_op jit(solution)/shard_map/ppermute | solution.py:15
  196.5 1.4 broadcast_select_fusion.3
  197.9 2.4 %collective-permute-start.5 = (bf16[2,384,768]{2,1,0:T(8,128)(2,1)S(1)}, bf16[2,384,768]{2,1,0:T(8,128)(2,1)S(1)}, u32[]{:S(2)}, u32[]{:S(2)}) collective-permute-start(bf16[2,384,768]{2,1,0:T(8,128)(2,1)S(1)} %broadcast_select_fusion.3), channel_id=1, source_target_pairs={{0,16},{16,0},{32,48},{48,32},{64,80},{80,64},{96,112},{112,96},{1... | collective-permute-start | bytes 3538952 | tf_op jit(solution)/shard_map/ppermute | solution.py:21
  200.3 2.4 %collective-permute-done.5 = bf16[2,384,768]{2,1,0:T(8,128)(2,1)S(1)} collective-permute-done((bf16[2,384,768]{2,1,0:T(8,128)(2,1)S(1)}, bf16[2,384,768]{2,1,0:T(8,128)(2,1)S(1)}, u32[]{:S(2)}, u32[]{:S(2)}) %collective-permute-start.5) | collective-permute-done | bytes 1179680 | tf_op jit(solution)/shard_map/ppermute | solution.py:21
  202.7 0.2 broadcast_select_fusion.5
  202.9 0.7 fusion.11
  203.6 1.5 fusion.7
Async XLA Ops:
  0.0 1.1 copy-start.1
  1.2 19.7 %collective-permute-start = (bf16[384,768]{1,0:T(8,128)(2,1)S(1)}, bf16[384,768]{1,0:T(8,128)(2,1)S(1)}, u32[]{:S(2)}, u32[]{:S(2)}) collective-permute-start(bf16[384,768]{1,0:T(8,128)(2,1)S(1)} %bitcast_multiply_fusion), channel_id=1, source_target_pairs={{1,0},{2,1},{3,2},{4,3},{5,4},{6,5},{7,6},{8,7},{9,8},{10,9},{11,1... | collective-permute-start | bytes 1769480 | tf_op jit(solution)/shard_map/ppermute | solution.py:10
  21.0 29.9 %collective-permute-start.1 = (bf16[2,384,768]{2,1,0:T(8,128)(2,1)S(1)}, bf16[2,384,768]{2,1,0:T(8,128)(2,1)S(1)}, u32[]{:S(2)}, u32[]{:S(2)}) collective-permute-start(bf16[2,384,768]{2,1,0:T(8,128)(2,1)S(1)} %pad_maximum_fusion.1), channel_id=1, source_target_pairs={{0,480},{16,496},{32,0},{48,16},{64,32},{80,48},{96,64},{112,80},{... | collective-permute-start | bytes 3538952 | tf_op jit(solution)/shard_map/ppermute | solution.py:15
  51.1 28.2 %collective-permute-start.2 = (bf16[2,384,768]{2,1,0:T(8,128)(2,1)S(1)}, bf16[2,384,768]{2,1,0:T(8,128)(2,1)}, u32[]{:S(2)}, u32[]{:S(2)}) collective-permute-start(bf16[2,384,768]{2,1,0:T(8,128)(2,1)S(1)} %broadcast_select_fusion), channel_id=1, source_target_pairs={{0,448},{16,464},{32,480},{48,496},{64,0},{80,16},{96,32},{112,48}... | collective-permute-start | bytes 3538952 | tf_op jit(solution)/shard_map/ppermute | solution.py:15
  80.7 55.6 %collective-permute-start.3 = (bf16[2,384,768]{2,1,0:T(8,128)(2,1)S(1)}, bf16[2,384,768]{2,1,0:T(8,128)(2,1)}, u32[]{:S(2)}, u32[]{:S(2)}) collective-permute-start(bf16[2,384,768]{2,1,0:T(8,128)(2,1)S(1)} %broadcast_select_fusion.1), channel_id=1, source_target_pairs={{0,384},{16,400},{32,416},{48,432},{64,448},{80,464},{96,480},{112... | collective-permute-start | bytes 3538952 | tf_op jit(solution)/shard_map/ppermute | solution.py:15
  137.7 4.0 %copy-start = (bf16[2,384,768]{2,1,0:T(8,128)(2,1)}, bf16[2,384,768]{2,1,0:T(8,128)(2,1)S(1)}, u32[]{:S(2)}) copy-start(bf16[2,384,768]{2,1,0:T(8,128)(2,1)S(1)} %broadcast_select_fusion.2) | copy-start | bytes 3538948
  137.7 58.7 %collective-permute-start.4 = (bf16[2,384,768]{2,1,0:T(8,128)(2,1)S(1)}, bf16[2,384,768]{2,1,0:T(8,128)(2,1)S(1)}, u32[]{:S(2)}, u32[]{:S(2)}) collective-permute-start(bf16[2,384,768]{2,1,0:T(8,128)(2,1)S(1)} %broadcast_select_fusion.2), channel_id=1, source_target_pairs={{0,256},{16,272},{32,288},{48,304},{64,320},{80,336},{96,352},{112... | collective-permute-start | bytes 3538952 | tf_op jit(solution)/shard_map/ppermute | solution.py:15
  197.9 4.9 %collective-permute-start.5 = (bf16[2,384,768]{2,1,0:T(8,128)(2,1)S(1)}, bf16[2,384,768]{2,1,0:T(8,128)(2,1)S(1)}, u32[]{:S(2)}, u32[]{:S(2)}) collective-permute-start(bf16[2,384,768]{2,1,0:T(8,128)(2,1)S(1)} %broadcast_select_fusion.3), channel_id=1, source_target_pairs={{0,16},{16,0},{32,48},{48,32},{64,80},{80,64},{96,112},{112,96},{1... | collective-permute-start | bytes 3538952 | tf_op jit(solution)/shard_map/ppermute | solution.py:21
where the time goes:
time: 205 us
  waiting for transfers between devices  181 us (88%)
  starting transfers between devices  15.7 us (8%)
  other arithmetic  5.46 us (3%)
  matrix products  2.15 us (1%)
    ppermute x4, waiting for transfers between devices, shifted(): lax.ppermute(array, axis, [(i, (i + by) % devices) for i in range(devices)])  162 us
    ppermute x1, waiting for transfers between devices, passed_along(): lax.ppermute(value, axis, [(source, source + steps) for source in range(l...  16.7 us
    ppermute x4, starting transfers between devices, shifted(): lax.ppermute(array, axis, [(i, (i + by) % devices) for i in range(devices)])  10.3 us
    select_n x4, other arithmetic, per_device(): jnp.where(column_index >> bit_number & 1 == 1, arrived, travelling)  4.37 us
  transfers between devices with their start and end apart: 6, of which 6 were waited for; matrix products, arithmetic and copies ran while one was open for 0% of the time, Pallas kernels for 0%

commit v1 on v0

v1 whole, which is shorter than its diff:
```python
import jax
import jax.numpy as jnp
from jax import lax
from jax.experimental import pallas as pl
from jax.experimental.pallas import tpu as pltpu
from jax.sharding import PartitionSpec as P

CHUNKS = 6
SLOTS = 44
SIB = 32
PLAN = (
    ((1, 12, 14, 16, 17, 29, 31, 194, 240, 256), 8, (83894272, 83894529, 83894786, 83895043, 83895300, 83895557, 101717272, 117450258, 102632219, 106697241, 117450772, 105647642, 101717789, 117451029, 117451543, 70193435, 117450515, 71178011, 117451286, 103681052)),
    ((2, 3, 15, 17, 18, 30, 31, 33, 195, 225, 227, 243, 257), 12, (68163584, 79828996, 82843905, 68163842, 68164099, 117514252, 117516308, 68225044, 117514766, 117516822, 67114757, 68162060, 117515280, 105714201, 69010969, 68162574, 68225558, 117517079, 103746842, 33554441, 69076762, 117516051, 68225815, 33554442, 117514509, 117515537, 103683352, 33554438, 117515023, 71176986, 33554439, 33554440, 117515794, 33554443, 117516565)),
    ((3, 13, 18, 19, 32, 34, 48, 49, 50, 51, 130, 226, 258), 9, (79894529, 67312131, 81860868, 81992197, 117580559, 68228367, 67175936, 101844761, 33554440, 117580045, 117580302, 33554438, 67176450, 33554443, 33554442, 33554439, 117581073, 117581844, 117579788, 33554441, 117581330, 105649176, 117582358, 117580816, 117582101, 117581587, 117582615)),
    ((2, 4, 20, 21, 26, 29, 33, 35, 37, 53, 54, 227, 229, 259), 8, (81926144, 68294661, 81926401, 67241986, 81926659, 67242500, 106698265, 100731162, 109647640, 33554440, 117647123, 117646609, 72159257, 33554439, 33554442, 33554438, 117645581, 117646352, 117646866, 33554443, 117647894, 117647637, 117645324, 33554441, 117645838, 117647380, 117646095, 117648151)),
    ((5, 12, 20, 21, 36, 52, 64, 66, 68, 82, 83, 228, 260), 8, (81991680, 68491265, 68425733, 81991939, 67307522, 117711374, 106631704, 67308036, 117711631, 72092696, 101911065, 101975578, 33554439, 117712402, 101975835, 68359182, 33554440, 33554442, 68359439, 117713687, 33554443, 117712659, 117710860, 117713430, 117711888, 117711117, 33554438, 117713173, 117712916, 117712145, 33554441)),
    ((6, 20, 22, 23, 37, 39, 65, 69, 71, 83, 84, 85, 131, 229, 261), 6, (68425986, 82057728, 67372801, 117776653, 82057987, 67373572, 68424461, 117776910, 67373829, 101911320, 68424718, 33554438, 117778966, 102041113, 33554441, 33554440, 117778195, 117776396, 33554442, 117778452, 117777167, 33554439, 117777681, 117777424, 117777938, 117778709, 117779223, 33554443)),
    ((7, 22, 23, 38, 40, 56, 70, 87, 98, 102, 114, 166, 196, 230, 262), 7, (68622339, 68622852, 67438080, 69540609, 102107416, 67438594, 117841932, 82124293, 68489740, 102107673, 33554439, 33554438, 117842703, 33554442, 68490511, 33554441, 117843474, 117842446, 33554443, 117843217, 117844502, 33554440, 117842189, 117844245, 117842960, 117844759, 117843731, 117843988)),
    ((8, 9, 22, 23, 28, 29, 39, 41, 71, 73, 101, 103, 112, 117, 118, 119, 167, 199, 231, 263), 8, (68556801, 82188292, 68557058, 67503616, 105713177, 67504387, 117907725, 67504901, 68555533, 33554442, 117909267, 117907982, 33554438, 102041624, 73143321, 117907468, 33554440, 117908496, 117909524, 33554441, 117908239, 107681562, 33554443, 117910038, 117908753, 117909010, 117909781, 33554439, 117910295)),
    ((9, 12, 24, 25, 38, 40, 57, 72, 119, 134, 136, 168, 184, 198, 232, 264), 12, (83367939, 67704836, 70785029, 78125312, 82254337, 68623106, 69671173, 102237977, 67569152, 33554439, 78126337, 33554442, 33554440, 78126594, 67569923, 117974546, 117974803, 33554443, 78126852, 105647896, 117973518, 117974032, 117975317, 73078040, 117975831, 117975574, 33554438, 117973775, 117973261, 117973004, 117975060, 33554441, 117974289)),
    ((8, 10, 11, 43, 59, 73, 88, 89, 137, 153, 201, 216, 233, 251, 265), 11, (82319360, 68687876, 75043077, 81205504, 67634945, 83106305, 67635202, 69605379, 101124632, 81336578, 67635973, 33554441, 81336836, 33554439, 33554442, 70720515, 118038540, 68686348, 118040853, 33554443, 118041367, 118039825, 33554438, 118039054, 118040596, 118038797, 118039311, 118041110, 118040082, 33554440, 118040339, 118039568)),
    ((11, 26, 27, 42, 58, 106, 164, 168, 170, 196, 202, 217, 219, 234, 236, 266), 10, (67835905, 74059523, 82188802, 67700995, 74059780, 67836165, 83564544, 67701252, 78256897, 102303512, 102370073, 83564805, 107614726, 33554439, 82385154, 118104076, 33554440, 33554442, 118104847, 118105361, 118106903, 118105618, 33554443, 33554441, 118106646, 118104333, 118106132, 118106389, 118104590, 118105104, 118105875)),
    ((10, 12, 13, 31, 43, 45, 165, 167, 171, 185, 186, 187, 218, 235, 250, 267), 14, (67765760, 68622593, 68818947, 83236867, 70916100, 82057474, 68884482, 67766017, 69868037, 101254936, 70851584, 82451457, 101255961, 70982660, 33554438, 33554441, 73076483, 118171411, 33554442, 33554440, 118170897, 33554439, 118169869, 118170126, 118171154, 118171925, 118172439, 118170640, 118172182, 118169612, 33554443, 118170383, 118171668)),
    ((13, 28, 29, 74, 192, 200, 202, 204, 215, 221, 236, 252, 268), 15, (67377152, 67966976, 67639299, 69933060, 70064641, 68491522, 67967490, 71112961, 67115522, 67832067, 102500376, 118235148, 71113220, 69146885, 68882956, 72092929, 118235919, 33554438, 111807769, 72093700, 33554442, 118237204, 118235405, 33554441, 118237718, 68883727, 33554439, 33554443, 118235662, 118236176, 33554440, 118237975, 118236690, 118237461, 118236947, 118236433)),
    ((12, 15, 28, 29, 30, 61, 193, 197, 205, 207, 214, 220, 235, 237, 241, 269), 14, (69474304, 83105793, 69015553, 67246082, 68950020, 69016322, 71110403, 68950277, 67896832, 70916612, 101385752, 67897603, 82189061, 102499865, 72158233, 101386266, 71110917, 118301712, 118302740, 70983168, 33554439, 102434587, 118301198, 118302226, 33554441, 33554438, 118301969, 33554442, 33554440, 118301455, 118302997, 118300941, 118303511, 118300684, 118303254, 33554443, 118302483)),
    ((15, 30, 31, 224, 238, 252, 254, 255, 270), 9, (69081088, 69015809, 71111939, 69081602, 71112196, 70127106, 118366734, 67116032, 70126849, 118367248, 102631449, 102565656, 68229376, 70127363, 82909701, 102697990, 118366220, 69014542, 70127620, 118366991, 33554440, 118368276, 69015056, 70128134, 118367505, 33554441, 118366477, 118368790, 118368019, 33554443, 118368533, 33554442, 33554439, 118367762, 118369047)),
    ((17, 30, 31, 222, 239, 240, 242, 255, 271), 14, (68027904, 69081348, 71047173, 69144066, 67180547, 69867780, 81795585, 69144323, 105715225, 69144837, 101716760, 104731930, 69077274, 101519899, 69143809, 67177752, 70192922, 103747612, 118432270, 69011993, 118432013, 69079821, 118433041, 69080849, 118431756, 118432784, 118432527)),
    ((0, 1, 15, 30, 208, 272), 4, (100667928, 100668441, 100668698, 118499605, 104730139, 118499091, 118498834, 104729628, 118499862, 118499348, 118500119, 104730909, 72160283)),
    ((1, 2, 14, 32, 47, 49, 51, 209, 241, 243, 273), 10, (67177472, 68098049, 67115011, 67177986, 80746756, 81861379, 67178500, 67116293, 67178757, 118565141, 103679768, 33554440, 118564884, 33554438, 71240984, 33554441, 33554439, 33554442, 118564627, 33554443, 104665625, 118565398, 118565655, 72225560, 118564370)),
    ((2, 3, 19, 35, 48, 50, 54, 146, 210, 229, 242, 274), 8, (80812032, 67179522, 69277953, 83040259, 67180036, 82909185, 81861632, 67180293, 100797208, 33554441, 33554442, 118629906, 118630163, 118630934, 33554439, 33554440, 118630677, 118631191, 118630420, 33554438, 33554443)),
    ((4, 5, 21, 28, 66, 81, 83, 85, 211, 243, 275), 7, (67246337, 80877570, 68290819, 68291076, 82974976, 82975237, 118696727, 102434328, 118696470, 33554442, 33554443, 33554441, 33554440, 118695956, 33554438, 118696213, 74125848, 118695699, 33554439, 118695442)),
    ((4, 5, 21, 26, 28, 65, 84, 131, 212, 244, 276), 9, (80943106, 67377412, 67442693, 83040512, 68491779, 100927513, 83040769, 106695706, 33554443, 118761235, 100862744, 118761749, 33554440, 108663067, 118761492, 33554438, 33554439, 33554442, 118762006, 118762263, 33554441, 118760978)),
    ((4, 5, 6, 7, 12, 20, 40, 87, 113, 213, 245, 277), 8, (67377664, 67377921, 83106050, 81008900, 68422405, 100861720, 83106563, 101910810, 106632217, 33554439, 118826514, 33554442, 33554438, 118827285, 118826771, 118827028, 33554440, 33554441, 118827799, 33554443, 118827542)),
    ((6, 7, 23, 54, 73, 112, 117, 118, 212, 246, 278), 6, (83171329, 67573762, 67442944, 81074436, 83171587, 101058328, 83171845, 33554441, 33554438, 101058585, 33554442, 118892050, 118892307, 118892564, 118892821, 33554440, 118893335, 33554439, 33554443, 118893078)),
    ((6, 8, 11, 24, 25, 55, 57, 89, 119, 147, 183, 198, 247, 279), 9, (81008641, 67508227, 67508484, 70654213, 68552192, 106630425, 100993304, 83237634, 100993562, 33554442, 101124123, 118958357, 33554439, 118957586, 33554438, 118958614, 118958871, 33554441, 118957843, 33554443, 118958100, 33554440)),
    ((8, 9, 25, 28, 43, 56, 73, 88, 216, 248, 280), 8, (70850561, 68753412, 83302403, 101190168, 70720002, 83302661, 33554442, 68617728, 33554439, 119023636, 33554443, 106696985, 33554438, 119023122, 119024407, 119024150, 119023893, 33554440, 119023379, 33554441)),
    ((10, 24, 26, 57, 59, 106, 169, 183, 185, 217, 219, 233, 281), 12, (67639553, 78190593, 76091396, 69802240, 81139971, 68684292, 70785536, 83368192, 102173208, 83368450, 70786051, 68684549, 80288773, 82385410, 119089172, 33554439, 80289027, 119088915, 33554440, 119089429, 119088658, 33554442, 33554443, 119089943, 119089686, 33554438, 33554441)),
    ((10, 11, 27, 42, 58, 167, 180, 186, 218, 235, 250, 282), 14, (83237120, 67770369, 70719491, 67311621, 70982146, 70523139, 68426501, 82384896, 33554438, 75107842, 33554440, 79305473, 71899650, 68749828, 119155479, 33554443, 33554441, 79305732, 101320984, 70851843, 68750085, 119154708, 119154451, 33554442, 119154965, 119155222, 33554439, 119154194)),
    ((11, 12, 13, 19, 28, 31, 203, 215, 221, 251, 283), 13, (82057217, 68814336, 72030464, 83630338, 67770629, 68814850, 83499267, 69933828, 68815107, 82123779, 69605637, 101320728, 70916868, 33554440, 69868289, 119219730, 119221015, 73076248, 119219987, 119220758, 33554441, 33554443, 33554439, 33554438, 119220501, 33554442, 119220244)),
    ((12, 13, 29, 44, 60, 205, 208, 214, 220, 236, 237, 246, 284), 15, (68360192, 69539841, 82122755, 68426240, 73141762, 82253828, 67574277, 71178241, 67967745, 68880386, 69146628, 101452312, 82516482, 73142019, 68688133, 101452569, 68880643, 73142276, 33554440, 33554442, 119285523, 68881157, 33554438, 33554443, 119285266, 33554439, 119285780, 119286037, 119286551, 119286294, 33554441)),
    ((1, 13, 14, 15, 30, 91, 253, 255, 285), 14, (67967232, 69998593, 67901442, 67574018, 67311876, 67115264, 71047429, 72158465, 83237379, 68946436, 104664344, 101517081, 33554440, 67897112, 104664603, 112858650, 119350802, 119351059, 33554441, 71111449, 78319642, 119352087, 67897371, 33554439, 119351316, 33554438, 33554442, 119351573, 119351830, 33554443)),
    ((0, 1, 14, 15, 31, 62, 240, 242, 254, 286), 13, (71175425, 68032513, 68098308, 69011458, 71175939, 82123269, 67180800, 69011715, 71176196, 68164354, 68164608, 69278977, 101516824, 102699033, 68164869, 83696901, 104732170, 101517338, 33554440, 33554441, 68028953, 70065667, 33554438, 33554443, 119416852, 33554439, 119417366, 119416595, 119416338, 119417623, 119417109)),
    ((12, 14, 15, 28, 30, 287), 14, (68032770, 69998850, 68098563, 71176704, 69077508, 67115781, 67181057, 68099076, 119480846, 70128654, 68028430, 119481103, 68028687, 70192642, 119481617, 68029201, 102435352, 119480332, 119480589, 101387033, 72093977, 119481360, 73078553)),
    ((34, 35, 44, 45, 47), 5, (100797720, 100799513, 68227864, 100798490, 68228634, 107744795, 107745820, 105780765, 70126109)),
    ((18, 30, 51, 52, 59, 61), 6, (100864792, 100733721, 109776666, 100863004, 105714461, 100863774, 108795419, 74256411)),
    ((35, 41, 45), 7, (69212161, 70391810, 67243779, 70326274, 70392325, 70457856, 69212676, 70327045, 107746585, 107746842, 110694424, 100800283)),
    ((51, 52, 62), 9, (69212418, 70392576, 75634945, 70260995, 70326532, 69344005, 101847832, 67308824, 100864538, 100865307, 107812121, 100863516, 100865821)),
    ((13, 59, 69), 3, (100930330, 105648664, 100930587, 110761241)),
    ((6, 28, 52, 59, 86), 5, (109776409, 100992795, 107680536, 100865050, 77206553, 110761500, 100996893, 76222492)),
    ((9, 27, 103), 5, (109581592, 67635480, 101061658, 107680025, 75110169)),
    ((8, 61, 86, 120), 3, (100996632, 101124889, 101127962, 107811099)),
    ((42, 44, 102, 137), 7, (101060888, 101193497, 68491032, 110695708, 107745562, 109710619, 76156700, 75175706)),
    ((25, 60, 120), 7, (69343236, 77139201, 77139715, 70589186, 77140229, 109644825, 83433472, 109778458, 101127448)),
    ((11, 15, 27, 63), 11, (70457344, 82188549, 70457601, 70785792, 76156418, 76156932, 104728600, 69737217, 101321498, 74061594, 103683609, 69737475, 102369051, 73077018)),
    ((12, 27, 60, 153, 154), 12, (70981637, 70719746, 71833857, 70851332, 101386776, 71834115, 82451968, 70720256, 73079553, 101256473, 75173635, 101257754, 109778716, 68686617, 107679771)),
    ((29, 31, 45, 125), 9, (74189824, 82712577, 70588418, 74190595, 69212930, 74190852, 69736965, 102500120, 104731673, 106761498, 74191642, 112989211)),
    ((12, 30, 61, 62, 92, 157, 188), 15, (71112704, 70850818, 73208069, 69343491, 69999105, 69343748, 108794904, 69213184, 71113475, 70982404, 74255896, 101386010, 104663068, 73272860, 101389851, 74257436, 111875609, 115086877, 105714974, 80547869)),
    ((0, 1, 14, 17, 31, 32, 42, 47, 48, 60, 160, 224, 241, 302), 6, (72223744, 71243777, 70588675, 72224772, 72225029, 72224258, 70326786, 72224515, 120463886, 71111694, 105780232, 120463629, 120465428, 105780489, 120464143, 120466199, 120464400, 33554439, 120465942, 120464914, 33554443, 120465685, 120464657, 120465171, 33554438, 120463372, 33554442)),
    ((0, 1, 15, 31, 62, 63, 92, 126, 303), 12, (70125570, 77600773, 70125827, 68229121, 71241218, 71241475, 105843737, 70261504, 71241732, 71173657, 69213444, 106828056, 104729116, 72290332, 120529679, 111875098, 120529422, 120528908, 73273881, 120529936, 112006683, 120529165, 73274908, 120530193)),
    ((35, 47, 51, 60, 62), 8, (101847576, 108794138, 100799769, 104795163, 107811612, 72225307, 70125083, 73272604)),
    ((34, 35, 46, 63), 4, (101782552, 100800025, 106763290, 105843996, 101783323)),
    ((34, 35, 51, 62, 63, 93), 6, (100797976, 109907993, 100798746, 77338137, 100799003, 106828573, 101848092, 71173917, 106827550)),
    ((34, 42), 10, (70260736, 70653956, 82123013, 69408769, 76683267, 70392834, 69278720, 110694936, 69409794, 69279235, 110695193, 100797466, 68227610)),
    ((26, 58, 68), 8, (69277697, 69540354, 69409280, 69409539, 70589444, 69410053, 100929818, 110758936, 78189080, 108662553)),
    ((41, 44, 46, 52, 62), 5, (106763545, 104663322, 100865564, 108729368, 110693915)),
    ((23, 51, 61), 4, (101848600, 67309592, 102107929, 108795674)),
    ((9, 24, 26, 43), 5, (109712409, 109647128, 108727323, 102172698, 75173401, 108597020)),
    ((8, 25, 42, 58, 60, 103), 8, (109580568, 109710363, 102237722, 109777693, 101062425, 111744798, 102238492, 75238685, 77205790)),
    ((11, 24, 26, 43, 45, 136), 8, (107746329, 102172440, 108728347, 101191194, 106630172, 76158491, 68621338, 102304029, 73207321)),
    ((11, 13, 27, 91), 13, (77204994, 70522880, 83630595, 79304961, 72751364, 101321240, 70786565, 104665114, 72095258, 102369819, 75109915, 112857625, 74061336, 78318617)),
    ((11, 13, 26, 43, 45, 62, 154), 13, (73013249, 69540098, 69474563, 69278211, 69540868, 108728600, 102303770, 83302917, 106762267, 82517504, 106631196, 101258009, 104664094, 76158744, 104662557, 104663583)),
    ((15, 29, 125), 12, (75239171, 82516224, 69934085, 70786305, 70261253, 102501145, 103683864, 69802500, 72159513, 79436546, 75239428, 73144089, 112004890, 79435034)),
    ((12, 13, 14, 17, 29, 45, 46, 53, 58, 59, 63, 241, 317), 12, (82581505, 70064130, 69278468, 121448725, 79502080, 73275651, 121447183, 121448982, 72094991, 67963157, 70654469, 106631961, 67963414, 69671685, 121446669, 33554439, 106632730, 121446926, 121447697, 121448468, 33554443, 106761240, 121448211, 33554440, 121447440, 106762011, 33554441, 121449239, 121446412, 33554438, 121447954, 33554442)),
    ((0, 1, 15, 16, 28, 30, 31, 42, 44, 47, 50, 63, 94, 318), 15, (72292356, 70195205, 72161792, 71244033, 69409027, 73272320, 70588931, 82778629, 71244293, 121512205, 70065154, 105845003, 121512719, 73273348, 121512976, 121513490, 70192146, 106695960, 69076498, 70982912, 70261761, 121514261, 33554440, 70393347, 70983428, 73275147, 33554438, 121514004, 121514518, 33554441, 33554442, 121512462, 121511948, 121513747, 121513233, 121514775, 33554439)),
    ((17, 46, 47, 48, 62, 160, 319), 11, (69867522, 73274627, 71174917, 70195456, 72289794, 106763032, 70393089, 70196228, 104662809, 72224024, 70327297, 121577998, 104663834, 121578255, 121578512, 121577741, 121578769, 121577484)),
    ((69, 78, 79, 92), 4, (100931352, 110891289, 107876379, 105777946, 74323738)),
    ((85, 93, 94), 3, (100995352, 68425496, 109907481, 109909786)),
    ((68, 74, 77), 4, (111808536, 100928538, 100928795, 68358682, 109843481)),
    ((91, 93), 2, (111873560, 109907737)),
    ((69, 74, 75, 76, 91), 9, (67374594, 72685573, 67374851, 72554756, 72423681, 100930072, 109842713, 71440896, 70523397, 71441153, 111807514, 100931101, 112858140, 111810331)),
    ((78, 86), 6, (71571456, 71309317, 69474817, 72489219, 71572740, 100995864, 69475074, 105711641, 100996378)),
    ((74, 103), 2, (101061144, 111808025, 111808794)),
    ((86, 91, 92, 120), 4, (111874840, 100996122, 111875865, 112858395, 78319387, 101126684)),
    ((43, 136, 137), 2, (101192472, 109712153, 109712666, 101190683, 101191964)),
    ((26, 119, 153), 5, (102109720, 67570712, 102241817, 109646874, 67702809)),
    ((77, 93), 8, (71440388, 71571968, 67901697, 71702786, 105646616, 71703045, 78253827, 106694681, 76289560)),
    ((27, 78, 92, 108, 140), 12, (72620036, 73078785, 77270530, 71572229, 83696132, 73079301, 107678745, 72882435, 109775128, 83565056, 72948483, 107677467, 106629404, 105712410, 75108889)),
    ((0, 2, 4, 8, 12, 31, 36, 58, 61, 74, 77, 92, 93, 230, 244, 332), 11, (73209859, 71571717, 82581761, 72685829, 82450948, 106694937, 76286976, 106694426, 106629144, 76287490, 33554442, 72948738, 33554439, 33554441, 77337881, 33554440, 122429709, 122431765, 33554438, 122430480, 122429452, 33554443, 122430994, 122432022, 122430223, 122429966, 122430737, 122431508, 122432279, 122431251)),
    ((1, 3, 7, 13, 15, 16, 29, 33, 45, 60, 62, 69, 75, 79, 93, 94, 95, 101, 229, 246, 333), 13, (73144321, 71440642, 71964676, 73210112, 73144578, 75304450, 82582019, 72423427, 73079044, 73210373, 106695448, 72091907, 77338392, 106759961, 122495245, 122497558, 73143053, 107811354, 33554439, 122494988, 122495502, 33554441, 122496530, 122496273, 33554442, 76353816, 122496016, 122497815, 33554440, 122496787, 33554443, 33554438, 122497301, 122495759, 122497044)),
    ((17, 32, 46, 48, 63, 64, 79, 95, 126, 160, 334), 13, (73340928, 73275393, 73734147, 82778116, 73341185, 75438339, 72030725, 72292864, 71637250, 73341444, 74322181, 122560524, 73208332, 74321153, 72686338, 122561552, 73209360, 74321410, 71310084, 122561809, 106825752, 74321667, 122561038, 106826521, 107876870, 122561295, 122560781, 122563351, 73209617, 107877127, 122562580, 33554442, 33554440, 122562837, 33554441, 33554443, 122562066, 122562323, 122563094)),
    ((47, 49, 62, 63, 78, 94, 95, 335), 13, (72222208, 75372546, 72222465, 75373059, 72555010, 73338884, 107812376, 73337856, 71309829, 122626574, 73274382, 73338113, 72424197, 107941147, 73338627, 75371291, 122626060, 122627345, 122626831, 106759705, 122627088, 105711130, 76354073, 122626317)),
    ((93, 94, 95), 3, (110892056, 106825498, 108925209)),
    ((68, 77, 79, 94), 4, (108859160, 101913369, 109909274, 106893595)),
    ((69, 93, 95), 5, (110891800, 100930841, 106826010, 74387226, 75371802)),
    ((68, 79, 86), 4, (101914137, 106892826, 67375129, 100995608)),
    ((75, 85, 92), 4, (111810072, 101979418, 67440410, 100995099, 68425243, 110891033)),
    ((68, 76, 78, 94), 8, (75700224, 67439873, 67440130, 72620547, 71374853, 72620804, 101914392, 106760474, 108860443, 110827289)),
    ((58, 91), 9, (72554496, 69670916, 71636993, 71768578, 71637507, 69541125, 111873304, 79303448, 111744537, 77205529)),
    ((102,), 2, (101060632, 68490776)),
    ((75, 153), 3, (101257496, 68687640, 111809817)),
    ((75, 76, 92, 136, 154), 5, (102176536, 110692889, 67704345, 106629914, 110825243, 110826524)),
    ((59, 92, 93, 123), 6, (110760728, 76221720, 106695194, 108660507, 110890265, 73074457)),
    ((4, 8, 11, 21, 23, 27, 31, 42, 43, 57, 59, 61, 75, 76, 77, 89, 90, 92, 122, 347), 12, (71505922, 69016068, 70916352, 72751105, 71572482, 71768835, 110824728, 108859417, 123412749, 33554440, 108727579, 123414034, 82517765, 123414291, 110825754, 33554438, 123413263, 33554441, 123414548, 123412492, 123415062, 33554442, 123413006, 78254872, 123413520, 123414805, 33554443, 123413777, 123415319, 33554439)),
    ((0, 3, 7, 20, 24, 28, 60, 62, 74, 76, 77, 90, 93, 246, 348), 15, (71768065, 72095746, 72620292, 70064388, 75110656, 70195714, 71309573, 71768325, 73013505, 77336323, 108858648, 72091416, 72031235, 123478542, 105646105, 72948229, 33554441, 33554443, 77336066, 33554439, 123478799, 73075204, 123479056, 33554438, 123480598, 33554442, 123479827, 123478285, 123478028, 76288792, 123479570, 123480855, 33554440, 123479313, 123480084, 123480341)),
    ((44, 45, 49, 53, 57, 59, 61, 63, 76, 77, 78, 79, 85, 94, 95, 349), 17, (76352769, 72357890, 72096003, 70392068, 72161285, 82254080, 72096257, 72488961, 71964930, 71506179, 73013764, 109842200, 123544849, 77272344, 71375106, 109842969, 73139712, 123545363, 33554440, 72091161, 109844250, 123545106, 72092442, 75303961, 33554439, 123546134, 74192657, 123545877, 123544592, 75305242, 123543821, 123545620, 33554438, 123543564, 123546391, 33554441, 123544335, 33554442, 123544078, 33554443)),
    ((45, 47, 48, 50, 61, 62, 63, 78, 79, 80, 82, 110, 126, 350), 16, (72161537, 74389506, 72292608, 75370500, 75369472, 73205762, 72686083, 123611413, 105711384, 82647809, 75369986, 72423939, 73341700, 72290069, 83761665, 75370243, 71375365, 73341957, 123609100, 71174421, 72358149, 33554438, 123610128, 123611156, 33554440, 108795161, 33554442, 33554443, 123610385, 123611927, 74256153, 123610899, 123609614, 33554441, 123610642, 33554439, 123611670, 123609871, 123609357)),
    ((78, 79, 81, 83, 94, 351), 13, (74323968, 82843653, 81861125, 72293121, 72226818, 75372036, 108859928, 72489475, 72227077, 74320920, 83827458, 123675664, 108860185, 72223248, 72358401, 123674636, 105712154, 123674893, 74323472, 123675150, 123675407, 106760731, 106760988, 123675921)),
    ((111,), 2, (107873816, 76419608, 109974297)),
    ((110, 126, 127), 3, (107809049, 112005656, 110039066)),
    ((103, 109), 2, (111940120, 101061401)),
    ((), 0, ()),
    ((), 0, ()),
    ((78, 110, 120, 125), 4, (105711896, 112005145, 101127706, 107808283)),
    ((), 6, (74520577, 79960066, 69736453, 67505152, 81074690, 67505923, 72816644, 67505409)),
    ((120,), 7, (77993987, 74586116, 70785285, 71702528, 73537793, 101127192, 69605890)),
    ((153,), 1, (110626584,)),
    ((122, 138), 2, (108594713, 109644056, 108595226, 108595483, 108595996)),
    ((10, 42, 58, 107, 108, 109, 122, 123, 170, 187, 228, 230, 234, 246, 251, 362), 8, (107678232, 101321754, 124396303, 75044111, 107743257, 124396560, 75044368, 68751898, 78385176, 33554441, 79369752, 33554439, 33554438, 124397074, 33554443, 33554440, 124398359, 33554442, 78386201, 124397588, 124396046, 124397331, 124395532, 124397845, 124398102, 124396817, 124395789)),
    ((7, 19, 37, 38, 43, 75, 106, 108, 109, 122, 125, 228, 229, 231, 235, 252, 363), 8, (74913792, 79367939, 75110912, 74914306, 79367425, 75111170, 75176196, 108595736, 79368453, 74057473, 33554440, 33554438, 33554442, 74058501, 33554441, 124461068, 112004121, 33554443, 124463381, 124461325, 33554439, 124463638, 124463124, 124462867, 124461582, 124461839, 124463895, 124462096, 124462610, 124462353)),
    ((32, 34, 40, 44, 57, 93, 106, 109, 124, 125, 172, 238, 364), 11, (74258432, 76158976, 74061828, 74123266, 74782978, 78384899, 74258691, 72030977, 78385413, 74259205, 124526604, 82451713, 108791832, 124527375, 75174412, 108792089, 124527632, 33554442, 33554440, 75175183, 78384642, 33554439, 75175440, 33554438, 124528660, 33554441, 124528917, 33554443, 124529174, 124528403, 124529431, 124526861, 124527118, 124527889, 124528146)),
    ((33, 35, 39, 45, 48, 77, 79, 94, 97, 101, 108, 125, 126, 157, 189, 236, 239, 253, 365), 12, (73537536, 75307008, 78385921, 74062082, 75175938, 75438595, 75241475, 77402116, 74189316, 77402373, 107677208, 107677977, 107678491, 124594710, 77401345, 33554439, 33554443, 74189573, 112004378, 33554442, 124592654, 124593682, 124594967, 124594196, 124592397, 124594453, 33554441, 33554440, 124593939, 124592911, 124592140, 124593425, 124593168, 33554438)),
    ((64, 78, 95, 96, 111, 113, 126, 127, 142, 238, 366), 13, (77402881, 75438083, 75372805, 83695874, 77403652, 73734912, 82713346, 76419333, 107940888, 73270808, 74521088, 76418305, 75371032, 73472259, 76419076, 124658961, 33554443, 109974536, 124657933, 108922905, 33554438, 109974793, 124658190, 124657676, 124658447, 124659732, 33554439, 124659218, 124659989, 124660246, 124658704, 124659475, 124660503, 75306769, 33554442)),
    ((79, 82, 94, 110, 126, 127, 225, 255, 367), 10, (75435522, 76420869, 73406464, 82713092, 73406721, 74319874, 110038041, 74521345, 74320131, 112006170, 74521600, 75435779, 124723212, 109909016, 75436036, 124723469, 124724240, 124724497, 124723726, 124723983)),
    ((119, 124, 126, 127), 6, (101125912, 112987161, 68556056, 108923418, 111022363, 77469210, 78452507)),
    ((102, 110, 111, 159), 6, (102044440, 110957082, 107874075, 108989468, 75435291, 112136217, 76418074)),
    ((103, 125), 2, (101062168, 112989721)),
    ((), 0, ()),
    ((124,), 2, (112988184, 80418328)),
    ((108, 119, 124), 5, (101126170, 113971736, 75171352, 112923673, 68556314)),
    ((119, 120), 2, (101126937, 102110232, 102111002)),
    ((107, 136), 10, (71899136, 74848258, 78059522, 74455043, 67570945, 74783236, 74848773, 80156677, 102176025, 67637017, 112921624, 112922138)),
    ((123, 124), 9, (74848513, 69801987, 73734660, 73865218, 113972249, 71769088, 108661274, 108660760, 69671429, 79433241)),
    ((9, 55, 105, 106, 107, 122, 170, 215, 217, 230, 244, 251, 377), 2, (125379857, 76027665, 33554439, 33554442, 125380885, 125381142, 33554438, 125378572, 33554440, 125380114, 33554441, 125380371, 125378829, 33554443, 125379086, 125381399, 125380628, 125379600, 125379343)),
    ((20, 26, 38, 52, 58, 75, 90, 92, 107, 120, 123, 125, 186, 228, 246, 250, 252, 378), 10, (74127364, 75040513, 73996544, 108791320, 73996802, 110890009, 107611674, 73997059, 73074201, 107612187, 73997317, 33554438, 79434264, 33554442, 125444108, 125444622, 33554441, 33554440, 125446164, 33554443, 78320153, 33554439, 125445907, 125445393, 125446421, 125446678, 125445650, 125444365, 125445136, 125444879, 125446935)),
    ((40, 43, 53, 55, 57, 59, 91, 107, 108, 109, 117, 124, 125, 238, 379), 8, (74979330, 74979844, 75105792, 73014017, 75106563, 110956056, 125510929, 33554440, 75107077, 112922649, 33554439, 74058265, 33554441, 112004634, 33554442, 125511186, 125510672, 33554443, 125511957, 33554438, 125512214, 125509901, 125510415, 125511700, 125509644, 125511443, 125510158, 125512471)),
    ((33, 45, 48, 54, 56, 60, 94, 108, 109, 122, 125, 126, 139, 188, 189, 235, 236, 380), 10, (74782720, 79432961, 75307265, 74979586, 79433475, 74717188, 75307524, 74455296, 75171842, 75307781, 125575951, 76223759, 75172099, 79433989, 125577236, 33554438, 107743512, 33554440, 33554441, 33554443, 112988935, 125576465, 125576208, 125575180, 125577493, 125576722, 125576979, 125578007, 125575694, 33554442, 125577750, 125575437)),
    ((77, 81, 85, 91, 92, 93, 95, 109, 110, 124, 126, 127, 173, 237, 239, 381), 14, (75110400, 75237121, 74192898, 73734404, 74127616, 74258945, 74193155, 74586372, 76224773, 75176450, 71047683, 108726041, 69999362, 75373316, 125641230, 107742744, 108726810, 108727067, 125642258, 125640973, 33554439, 77401112, 125641487, 33554440, 125641744, 125642515, 125643286, 125643029, 125640716, 33554441, 33554438, 33554442, 125642001, 125642772, 33554443, 125643543)),
    ((79, 80, 82, 94, 95, 110, 112, 125, 127, 142, 158, 240, 254, 255, 382), 16, (78451457, 82647043, 77466624, 74390018, 75438848, 77466881, 70195972, 107809561, 73472000, 77467138, 75439108, 125707280, 75302914, 77467652, 74455813, 75439365, 125706252, 125708822, 73271830, 74387478, 33554443, 107877400, 125706766, 125707794, 72222744, 107877658, 125707023, 111022598, 72223002, 125709079, 33554441, 125708051, 33554440, 76355088, 33554442, 33554439, 108792347, 125706509, 125708308, 125708565, 125707537)),
    ((78, 109, 110, 111, 113, 126, 142, 383), 13, (74389760, 77469445, 74324226, 76421379, 83761409, 125772302, 110957848, 83827202, 74455556, 110956314, 75367936, 73472516, 76418840, 108860697, 125772559, 108856859, 125772816, 125773073, 108857884, 78386458, 125771788, 125772045, 108858141)),
    ((140, 142, 143), 3, (114037017, 112071704, 112070171, 112072474, 76417818)),
    ((158, 159), 3, (114103064, 112135962, 113121049, 78582041)),
    ((35, 139, 143), 4, (112071450, 100799257, 109709848, 76416794)),
    ((85, 158), 3, (100994072, 114102809, 68424216)),
    ((140, 141), 1, (114036760, 114038041)),
    ((157, 158), 2, (114103577, 114102040, 81532184)),
    ((137, 139), 2, (101192984, 109709593)),
    ((), 0, ()),
    ((38, 56, 121, 137, 152, 153, 168, 184, 217, 232, 244, 248, 392), 11, (76748800, 74914051, 79173636, 80091137, 70851074, 79108356, 72947717, 71834368, 71834629, 110627608, 33554443, 101193226, 126363154, 126364439, 126361612, 126362897, 33554441, 33554438, 126362383, 33554439, 126363925, 126363668, 126361869, 126362126, 126363411, 126364182, 126362640, 33554440)),
    ((3, 25, 41, 55, 73, 105, 138, 153, 154, 169, 186, 201, 233, 393), 11, (78125056, 71833601, 76024324, 77076485, 82319618, 75896835, 69736709, 78125825, 79174146, 126428176, 77075984, 33554438, 76024067, 33554440, 101258264, 126427405, 33554439, 33554442, 77137944, 33554443, 126427148, 33554441, 126429975, 126428690, 126429461, 126428947, 126429204, 126427662, 126427919, 126429718, 126428433)),
    ((40, 42, 55, 56, 57, 59, 72, 108, 130, 134, 139, 154, 155, 230, 234, 394), 7, (77142017, 77207557, 76088832, 73996291, 76089346, 112923160, 76089860, 110757401, 78384152, 110758682, 33554438, 126493198, 77141006, 33554443, 33554439, 126493712, 77141520, 33554440, 126493969, 126494483, 126492684, 126494997, 126494740, 33554442, 126495254, 33554441, 126495511, 126494226, 126492941, 126493455)),
    ((33, 37, 41, 43, 56, 75, 90, 124, 125, 140, 141, 154, 157, 188, 235, 247, 395), 9, (75634692, 77207813, 76154368, 75897091, 76154625, 108792601, 33554440, 76154882, 33554438, 33554442, 78450969, 110692120, 33554443, 126560533, 126558734, 33554439, 79435545, 33554441, 126558477, 126560019, 126558991, 126559762, 126560790, 126561047, 126560276, 126558220, 126559505, 126559248)),
    ((66, 68, 74, 76, 92, 93, 141, 154, 156, 157, 234, 236, 396), 10, (80481280, 76355584, 72030211, 75765764, 76220418, 76355845, 77404417, 76220932, 110888728, 80481537, 75503877, 110889497, 80481794, 33554440, 126624527, 33554438, 33554442, 126623756, 77271564, 80482051, 126624270, 126625041, 126625298, 33554439, 126626583, 126624784, 33554441, 33554443, 126626326, 126625555, 126624013, 126625812, 126626069)),
    ((50, 65, 67, 77, 79, 81, 93, 111, 126, 140, 143, 156, 158, 159, 173, 189, 231, 237, 397), 9, (77404160, 77273089, 77338626, 75766019, 77208065, 77338884, 79499268, 109774360, 126689549, 77404677, 109775641, 79498754, 79499011, 110823450, 33554441, 76286211, 33554443, 126691348, 126690320, 126689292, 126691605, 33554439, 126689806, 126690577, 126691862, 126690063, 33554440, 126690834, 33554438, 33554442, 126691091, 126692119)),
    ((96, 110, 111, 113, 127, 128, 130, 143, 158, 159, 238, 398), 16, (77535232, 77469698, 79500547, 77535489, 76879874, 77469956, 78452997, 76487424, 78515457, 76749060, 126757655, 74320663, 78515971, 110954520, 111023385, 76618241, 78516485, 126756113, 75368729, 76484377, 75504386, 112072202, 126755085, 75436311, 111020570, 77403921, 79566362, 126756370, 126755856, 33554438, 33554440, 126756884, 126757398, 126755599, 126756627, 126757141, 33554441, 126755342, 33554439, 126754828, 33554443)),
    ((97, 111, 142, 158, 159, 254, 255, 399), 11, (77532160, 77470210, 75503618, 75635201, 77470467, 76417540, 114103832, 77532417, 75504133, 77533188, 110955289, 111019546, 78580762, 126820364, 77533445, 126821649, 79564824, 79565338, 126821135, 80549657, 109905435, 126820621, 126821392, 126820878)),
    ((158, 159), 2, (113119000, 111020825)),
    ((142, 157, 158), 4, (115086104, 80547096, 113054490, 110954265, 110954779)),
    ((51,), 1, (101848344,)),
    ((136, 142), 3, (102175256, 112070681, 79500825)),
    ((), 0, ()),
    ((142, 157), 3, (114102553, 113054744, 81532697)),
    ((153, 157), 3, (115085848, 110627097, 110627354, 80546840)),
    ((), 0, ()),
    ((104, 136, 137, 150, 155, 169, 184, 201, 214, 216, 248, 408), 3, (109579032, 110757913, 127412758, 33554440, 33554441, 33554443, 127411987, 110758426, 127412501, 33554442, 127411730, 127412244, 33554439, 33554438, 127413015)),
    ((34, 40, 41, 51, 53, 89, 137, 138, 139, 154, 185, 230, 249, 409), 11, (69933313, 81270786, 81271043, 76945667, 72882181, 76027909, 67701760, 71899396, 76945924, 109643544, 73930753, 33554438, 127475981, 79174400, 127476495, 127477009, 127477266, 127477780, 33554441, 33554439, 127477523, 127478294, 33554440, 33554442, 127476752, 127476238, 127478037, 127475724, 127478551, 33554443)),
    ((36, 37, 52, 56, 58, 86, 90, 138, 139, 141, 152, 155, 186, 235, 247, 252, 410), 12, (70981889, 76224513, 76093442, 80287747, 69933568, 77137408, 80288005, 79239427, 127541774, 109710105, 72947972, 79239685, 78189582, 109644568, 33554439, 127543059, 109840154, 33554438, 33554441, 33554440, 33554443, 127541517, 33554442, 127541260, 127543316, 127543573, 127543830, 127542288, 127542545, 127542031, 127544087, 127542802)),
    ((75, 85, 89, 91, 93, 140, 141, 156, 157, 234, 236, 251, 253, 411), 7, (76159232, 77076738, 76159493, 77203201, 77076996, 113052952, 33554438, 77203715, 127607310, 78255118, 33554439, 33554442, 127607053, 127609109, 80483096, 127608595, 33554440, 127608338, 33554441, 33554443, 127608081, 127607567, 127607824, 127609366, 127606796, 127609623, 127608852)),
    ((50, 64, 76, 77, 80, 82, 84, 90, 92, 122, 140, 141, 157, 173, 231, 412), 7, (77268480, 77268737, 76356098, 77269508, 109840408, 80483352, 109840921, 77404931, 33554439, 127673103, 33554438, 33554442, 127675159, 127674388, 78320911, 127672332, 77269765, 33554441, 127672846, 33554443, 127673617, 127674902, 33554440, 127674645, 127674131, 127672589, 127673360, 127673874)),
    ((109, 110, 113, 123, 125, 127, 140, 141, 142, 143, 145, 156, 158, 159, 253, 413), 15, (76945408, 76290049, 78452738, 75831299, 76290308, 76880133, 77334016, 76617729, 114037272, 127739667, 74254099, 79498264, 76285464, 127738896, 127740438, 74254870, 78386704, 109774617, 77334787, 127739153, 127740181, 70065412, 78386961, 77335301, 33554440, 127738639, 113053978, 33554443, 127738382, 110823707, 33554442, 76286746, 127738125, 127739410, 127740695, 80484122, 127737868, 33554438, 33554439, 127739924, 33554441)),
    ((112, 126, 127, 142, 143, 144, 159, 190, 237, 254, 255, 414), 14, (76421122, 75831555, 76486660, 75700480, 79564290, 76486917, 79563776, 75569153, 77535748, 127806231, 75369239, 76484887, 79564033, 76617985, 127803404, 111087130, 76552195, 79565061, 127803661, 76417050, 33554439, 112071963, 76618499, 127803918, 77532955, 127805717, 33554440, 113120521, 127804432, 76417307, 33554438, 77399552, 33554442, 127804946, 109905944, 127805460, 127804689, 109906457, 127804175, 127805974, 33554443, 127805203)),
    ((142, 143, 158, 415), 12, (79565569, 76487168, 79565826, 74520836, 112069656, 77465859, 76421636, 75569413, 127868940, 79499800, 76416524, 75569667, 78516748, 110955034, 76552453, 127869197, 127869454, 127869968, 127870225, 109905689, 127869711)),
    ((47, 175), 5, (105781016, 71242008, 70126360, 112069145, 80614937)),
    ((174, 190, 191), 3, (116200728, 114232858, 112002841)),
    ((175,), 1, (114168344, 114169625)),
    ((191,), 1, (114232600,)),
    ((170, 171), 1, (101322520, 101324313)),
    ((172, 174, 188), 3, (112003609, 101389336, 111872794)),
    ((103,), 1, (101061912,)),
    ((119, 187), 3, (101125656, 101387545, 68817689, 101387290)),
    ((8, 137, 171), 4, (101192216, 109579289, 101324570, 78252826, 76023320, 109578011, 109579549, 109579806, 109580319, 111807004)),
    ((25, 52, 56, 86, 154, 170, 183, 185, 186, 201, 252, 425), 4, (109645080, 77075224, 102307595, 33554441, 128526356, 33554439, 128526099, 33554442, 33554438, 128526870, 33554440, 128527127, 128525842, 128526613)),
    ((10, 12, 66, 68, 70, 74, 84, 88, 91, 155, 168, 171, 186, 187, 202, 251, 426), 13, (74062336, 81467394, 77862915, 81336321, 79108099, 80288257, 78187269, 112854552, 112854809, 67768581, 79239940, 112855578, 82582788, 79240192, 33554443, 108598043, 79240450, 128591892, 128592406, 128590864, 33554438, 33554440, 128590093, 33554439, 33554441, 128589836, 128590607, 74059035, 128592149, 128592663, 128590350, 33554442, 128591121, 128591635, 128591378)),
    ((29, 45, 47, 58, 67, 71, 86, 122, 156, 165, 172, 173, 188, 189, 235, 427), 10, (79960322, 77863172, 82450688, 79304704, 78125573, 82451201, 79305217, 33554441, 80353795, 78126084, 33554442, 112920088, 67834392, 78252034, 128657171, 33554438, 128658199, 128656400, 33554439, 128655629, 128657685, 128655886, 33554440, 128657428, 128656143, 128656914, 128657942, 33554443, 128655372, 128656657)),
    ((98, 106, 108, 109, 127, 138, 157, 174, 184, 188, 189, 234, 428), 10, (78317827, 79501313, 78318084, 78453248, 79501570, 77928965, 128722707, 74188563, 112986136, 128721679, 112002585, 33554440, 128722193, 80612377, 128720908, 33554441, 79369487, 128723478, 81596953, 128721936, 128722450, 33554443, 128721422, 79370001, 128723735, 33554438, 33554439, 128722964, 128723221, 33554442, 128721165)),
    ((47, 60, 97, 101, 107, 109, 111, 112, 123, 126, 139, 142, 157, 161, 165, 172, 175, 190, 205, 237, 429), 11, (79435778, 81595906, 79436035, 81596163, 79501824, 79173892, 81596420, 79436293, 128788243, 75302675, 115086360, 79502337, 109906713, 81596677, 111871514, 80547352, 33554441, 33554440, 128788500, 79501081, 77334552, 33554443, 128788757, 33554438, 128787729, 128787472, 128786701, 128786444, 128786958, 128787215, 128789014, 33554442, 128787986, 128789271, 33554439)),
    ((128, 130, 142, 147, 158, 159, 160, 175, 190, 191, 206, 430), 12, (79566850, 80549891, 79632388, 78977029, 80612609, 77928708, 78584069, 78387456, 80612866, 78715138, 80613123, 77666561, 80613380, 113184521, 128852237, 128851980, 80613637, 113051416, 128852751, 33554439, 33554440, 80614665, 113051673, 128853265, 128853522, 128854550, 128854293, 128853779, 128853008, 33554442, 33554438, 33554443, 128854036, 128852494, 128854807)),
    ((113, 129, 143, 174, 190, 191, 431), 10, (79629569, 77731840, 80614402, 78514435, 79629312, 77732101, 77601028, 79630597, 79629826, 115215896, 112003865, 128917773, 79630340, 82646040, 128918030, 114233114, 128917516, 128918287, 128918544, 128918801)),
    ((189, 190, 191), 2, (112985880, 112986649, 115215386, 115216156, 115217435)),
    ((174, 190), 3, (116199960, 115151897, 79496728)),
    ((191,), 2, (113116952, 81662744)),
    ((), 0, ()),
    ((187, 190), 2, (116200985, 102371864)),
    ((174,), 1, (115152664,)),
    ((), 0, ()),
    ((136, 170), 3, (111741208, 68752664, 102176281)),
    ((136, 137, 153, 173), 4, (101191704, 110626331, 109578266, 111938073)),
    ((154, 170, 188), 5, (112920856, 67835160, 110692633, 111741467, 68752923, 111740444, 111740957, 110693146)),
    ((26, 29, 58, 68, 71, 86, 170, 171, 187, 218, 235, 442), 8, (102373131, 67834123, 33554438, 110759193, 111805976, 78189337, 33554439, 33554441, 33554440, 111806234, 33554442, 129640982, 109646619, 109647388, 129640211, 129640468, 129640725, 75107611, 129639954, 75108380, 129641239)),
    ((106, 107, 117, 119, 123, 138, 171, 172, 185, 188, 189, 219, 234, 443), 10, (78911488, 78256128, 83499012, 79301381, 78059777, 78256385, 81401858, 78060032, 78256644, 129704719, 74057999, 79300867, 82516995, 129704205, 129705490, 33554441, 129705233, 101390091, 33554439, 33554438, 33554440, 129704976, 129706518, 129706261, 129706004, 129706775, 33554442, 129703948, 129704462, 129705747)),
    ((44, 60, 112, 114, 116, 120, 122, 124, 139, 172, 173, 176, 189, 444), 13, (82515969, 77928450, 79239171, 81467649, 79366917, 78321664, 70064900, 111937560, 129769741, 79502596, 129770255, 80418063, 79366146, 111937817, 80417549, 111938330, 33554440, 33554438, 129770769, 80418577, 33554439, 33554441, 33554443, 129770512, 129769484, 109777947, 129771026, 33554442, 75238939, 129771283, 129772311, 129772054, 129769998, 129771797, 129771540)),
    ((61, 141, 142, 145, 147, 149, 155, 157, 159, 172, 173, 174, 177, 188, 191, 213, 445), 11, (78649345, 78387202, 78649604, 129837333, 76351765, 79431168, 129836048, 80483856, 79431939, 115149850, 129835277, 79432453, 129835020, 115150108, 129836562, 108794395, 111871768, 78382618, 129835534, 33554441, 111872025, 78382876, 129835791, 33554439, 33554442, 33554443, 112921117, 129837847, 129836305, 33554440, 74255387, 129837590, 129837076, 129836819, 33554438)),
    ((129, 142, 143, 144, 158, 159, 174, 178, 191, 206, 222, 446), 14, (78518273, 78583810, 81074181, 81661185, 78518530, 78911748, 78714880, 79632643, 81661956, 129902355, 77465363, 78581011, 112003096, 79764225, 77666307, 79632900, 129901070, 129902612, 77465620, 78581268, 80548878, 78649856, 129900556, 33554438, 78650371, 81662213, 129900813, 33554439, 33554442, 115217673, 129901841, 33554440, 33554443, 129901584, 129902869, 129903126, 129902098, 129903383, 129901327)),
    ((174, 175, 190, 447), 12, (80615424, 78780417, 81663492, 79563011, 81663749, 129966349, 80614157, 77797377, 78584323, 78513933, 115152408, 79562754, 78650114, 129966092, 113051929, 77666818, 129967377, 113052186, 129966606, 129966863, 78513676, 129967120, 78514961)),
    ((205, 206, 207), 3, (101455384, 116263961, 116265754, 80611098, 116266779, 80612123)),
    ((190, 206, 221, 222), 3, (116200219, 101518361, 114101016, 101520154)),
    ((1, 207), 2, (116266009, 100668952)),
    ((2,), 1, (100730648,)),
    ((102, 171, 205), 3, (101060120, 114035226, 101323801)),
    ((206, 222, 223), 3, (114099736, 116330266, 114099995, 101521177)),
    ((136,), 2, (102175512, 67636504)),
    ((119,), 1, (101126424,)),
    ((205,), 2, (114034968, 67900696)),
    ((25, 154, 170, 204), 5, (101258520, 101259033, 111740698, 110630684, 113969947, 109645597, 76091676)),
    ((171, 205), 4, (101454872, 80480280, 101455641, 111806746, 67769626, 80481049)),
    ((116, 117, 120, 188, 201, 204, 205, 219, 221, 459), 2, (102437639, 33554442, 130754580, 130754837, 130754323, 33554440, 33554438, 130754066, 130755351, 130755094, 33554441, 33554443)),
    ((128, 132, 140, 155, 156, 157, 189, 196, 200, 202, 218, 221, 460), 11, (67898368, 81598468, 81205253, 80414465, 83630850, 80550146, 67899139, 130818060, 67898625, 80288517, 115083544, 81468160, 115083801, 130819602, 130820116, 33554440, 83565314, 81468419, 130818317, 130820630, 130818574, 130819088, 33554442, 33554441, 130818831, 33554438, 33554443, 130819345, 33554439, 130819859, 130820887, 130820373)),
    ((45, 129, 131, 133, 143, 145, 149, 150, 173, 174, 190, 193, 197, 204, 206, 207, 221, 222, 461), 14, (80353282, 79697924, 80222211, 79960580, 83631104, 80353541, 112003352, 81597720, 81402368, 101518874, 81402625, 81528858, 68949018, 33554441, 130886166, 113969177, 82583041, 33554440, 33554442, 130885909, 130885652, 33554438, 130884110, 130885138, 130884881, 130885395, 130884367, 33554439, 130883853, 130886423, 33554443, 130883596, 130884624)),
    ((160, 162, 172, 174, 175, 191, 192, 207, 222, 223, 462), 12, (80025600, 82709761, 81664002, 82710018, 80681476, 79763461, 80026369, 82710275, 80546051, 113116696, 80677912, 79698176, 82710532, 130949389, 81597197, 130951188, 78514196, 82710789, 130949646, 115149337, 81662488, 115281673, 82711817, 130949903, 130950931, 130950160, 33554438, 33554442, 130950674, 130950417, 33554440, 130949132, 130951959, 130951445, 130951702, 33554439, 33554443)),
    ((161, 163, 175, 206, 222, 223, 463), 11, (81664256, 81727492, 79829250, 80611587, 101520408, 79698433, 81726978, 116330009, 114100762, 81726721, 79698693, 131014668, 80812293, 81659929, 131015696, 83760153, 131015953, 116330779, 131015439, 131014925, 131015182)),
    ((17, 221, 223), 5, (102502936, 101717529, 116329754, 83759898, 81659674)),
    ((18, 207), 2, (101778968, 115282201)),
    ((19, 223), 3, (101845016, 115214617, 83760409)),
    ((20,), 1, (101910552,)),
    ((21, 23), 2, (101976601, 102106904)),
    ((22, 102, 190), 3, (116201240, 102042137, 79498008, 102044698)),
    ((25, 221), 4, (101519640, 68949784, 81529624, 110630169)),
    ((9, 204), 3, (102438680, 108596249, 67899672)),
    ((153,), 3, (102241304, 77072408, 67702296, 101256985, 68687129)),
    ((9, 170), 4, (102306584, 67767576, 109581337, 75042329, 109581850, 75042842)),
    ((187, 205, 221), 5, (112855064, 67833368, 68817944, 115082777, 114034202, 114034459)),
    ((170, 188, 204, 222), 5, (102306840, 112920345, 115148314, 113968667, 67767832, 113969436)),
    ((45, 133, 145, 149, 150, 173, 204, 205, 214, 218, 221, 476), 3, (102503175, 33554441, 131868692, 33554440, 33554442, 131868178, 67964167, 33554443, 33554438, 131868435, 131868949, 131869206, 131869463)),
    ((172, 173, 177, 181, 189, 191, 204, 205, 206, 219, 222, 223, 477), 14, (80746496, 81528577, 80484355, 82647300, 81139717, 80550402, 80484612, 81402112, 79763712, 82582275, 131932686, 113969688, 82516739, 131932943, 33554439, 68883992, 131933200, 33554440, 67899416, 131934485, 131933971, 131934999, 131933457, 131934742, 131932172, 33554442, 33554438, 131932429, 33554441, 33554443, 131933714, 131934228)),
    ((175, 176, 178, 190, 191, 206, 207, 208, 210, 223, 238, 254, 478), 14, (80680962, 81729538, 68098816, 81594113, 80615684, 80025861, 81467904, 79763969, 82647555, 81729797, 114100248, 115280921, 131997965, 82711065, 132000278, 79563286, 80678934, 80610841, 131998736, 132000535, 79563543, 80679191, 81594627, 117315339, 131999507, 33554438, 33554442, 131998222, 82648068, 131999250, 131998993, 33554440, 132000021, 33554441, 131997708, 131998479, 131999764, 33554439)),
    ((206, 207, 209, 222, 479), 10, (82712832, 80681218, 80026115, 83760644, 132064272, 115148824, 80877827, 81660677, 82712080, 80611856, 80747009, 80681733, 132063758, 80611342, 132063244, 132063501, 132064015, 115149593, 132064529)),
    ((15, 238, 239), 3, (116263705, 101584152, 101582618, 68032281, 70128410)),
    ((2, 17, 18, 95, 238), 3, (116197144, 100731417, 107942170, 100732699, 100733468)),
    ((3,), 1, (100795928, 100796185, 100796698)),
    ((2, 4), 2, (100861464, 100731674, 100862233)),
    ((5, 11, 27), 4, (107679000, 75109144, 107615257, 100927002, 100927771)),
    ((6, 27, 28, 30, 51, 238), 6, (100864281, 107681048, 105715482, 116197403, 68294425, 116197917, 107679516, 100993822)),
    ((7, 10, 13, 42), 6, (101059096, 109711641, 107613722, 75043866, 105649947, 77141785)),
    ((8, 28, 93), 4, (107681304, 109906969, 101123866, 77337113)),
    ((9, 137), 2, (109580824, 67634712, 101192729)),
    ((10, 25, 26), 3, (109646360, 68748824, 101255193, 109645338)),
    ((11, 43, 76, 108, 171, 255), 8, (117312280, 101323289, 109842458, 107615004, 101323547, 77272602, 109711902, 111938845, 79368989)),
    ((28, 59, 60, 91, 187, 188, 221, 238), 10, (101389080, 108792857, 107680794, 101519131, 76223001, 102372636, 116196893, 67833628, 109775902, 112858911, 78319903, 77206046)),
    ((61, 76, 77, 170, 205, 221, 255), 8, (110826265, 102503707, 117311260, 107810072, 75240216, 101322781, 101454622, 76287257, 109843738)),
    ((94, 126, 161, 175, 177, 180, 193, 213, 221, 222, 225, 229, 235, 253, 255, 493), 7, (101519385, 112006424, 75303192, 33554439, 68949529, 101520666, 33554443, 132983575, 77467416, 33554441, 132982804, 132983318, 33554440, 132982547, 101520924, 33554442, 33554438, 132983061, 109908763, 132982290)),
    ((44, 110, 111, 192, 194, 206, 222, 223, 224, 239, 252, 254, 255, 494), 15, (83695616, 81860609, 83826689, 68029954, 81795073, 68030468, 83826949, 68029440, 82123522, 83696387, 133046541, 117314073, 68030211, 82124036, 133046798, 81659417, 82517248, 68030725, 133047055, 117378311, 109975066, 82775065, 68031239, 133047312, 133047826, 109973019, 33554443, 101586185, 133047569, 133048854, 33554442, 107744536, 133048597, 33554438, 33554440, 133048340, 75174680, 133046284, 74320410, 133048083, 133049111)),
    ((62, 78, 197, 207, 208, 238, 254, 255, 495), 11, (83823616, 83761154, 83630084, 81795333, 82708225, 82708739, 82909445, 101649945, 83696644, 108860952, 83824387, 107812634, 133112334, 133112848, 133112591, 133111820, 101650459, 133113105, 133112077)),
    ((1, 95, 255), 5, (108926744, 100668185, 101650202, 83757338, 69080346)),
    ((14, 18, 239), 5, (101779224, 117379353, 104666906, 70127898, 67963674)),
    ((19, 255), 4, (117311000, 68095000, 69079576, 101844505, 101845786)),
    ((18, 20), 3, (101779736, 101910041, 67179800, 101910298)),
    ((9, 13, 21), 4, (101976089, 108596506, 76026650, 101976347, 105648920)),
    ((22,), 1, (102041368, 102041881, 102042394)),
    ((11, 23, 26, 29), 6, (108661785, 102500634, 102107163, 107615512, 72159002, 73143578)),
    ((24, 59), 3, (102172952, 102173465, 109777178, 77207322)),
    ((8, 25), 3, (109580056, 110629401, 110629914, 68683802)),
    ((41,), 1, (110693400,)),
    ((27, 187), 3, (101388312, 108664089, 68818456)),
    ((10, 75, 204), 6, (101254680, 75043352, 108599065, 74058776, 102437915, 74060057, 110824474, 78254618)),
    ((27, 58, 204, 205, 239), 7, (108663833, 101586456, 82709016, 101453339, 74124825, 101454364, 111744282, 77205274)),
    ((30, 75, 110, 238, 239), 6, (102568472, 116197659, 69014811, 117379100, 107808793, 102566685, 110825498, 77403161)),
    ((94, 127, 207, 208, 210, 222, 223, 234, 236, 238, 239, 240, 242, 255, 510), 10, (117378584, 68031512, 134097430, 81660438, 82776086, 134096402, 82708504, 102634504, 108922649, 33554443, 102635018, 108924186, 33554438, 134097687, 76483865, 33554439, 134096916, 134097173, 77468441, 134096659, 33554441)),
    ((95, 127, 238, 239, 241, 253, 254, 511), 16, (82778370, 82450437, 82974720, 134160396, 102568728, 82582529, 83757058, 82844163, 102569753, 83757572, 68095233, 134160910, 82643737, 82707980, 82778884, 68096261, 111023130, 134161167, 68030988, 134160653, 108925979, 134161681, 74386971, 134161424, 76484122)),
)

LEFT, RIGHT0, RIGHT1 = CHUNKS, 2 * CHUNKS, 3 * CHUNKS
SIZE = 384 // CHUNKS
MAX_SENDS = max(len(p[2]) for p in PLAN)
MAX_FROM = max(1, max(len(p[0]) for p in PLAN))
MESH = pl.DeviceIdType.MESH


def nt_dot(left, right):
    return lax.dot_general(left, right, (((1,), (1,)), ((), ())), preferred_element_type=jnp.float32)


def choose(index, low, high, leaf):
    if all(PLAN[i] == PLAN[low] for i in range(low, high)):
        leaf(PLAN[low])
        return
    middle = (low + high) // 2

    @pl.when(index < middle)
    def _():
        choose(index, low, middle, leaf)

    @pl.when(index >= middle)
    def _():
        choose(index, middle, high, leaf)


def kernel(upper_ref, mask_ref, out_ref, buf, acc, table, origin, count, in_sem, send_sem, recv_sem):
    brow, column = lax.axis_index("brow"), lax.axis_index("bcol")
    row, half = brow // 2, brow % 2
    own = buf.at[pl.ds(0, 384)]
    load = pltpu.make_async_copy(upper_ref, own, in_sem)
    load.start()

    def leaf(plan):
        origins, targets, sends = plan
        count[0] = len(origins)
        count[1] = targets
        count[2] = len(sends)
        for i, v in enumerate(origins):
            origin[i] = v
        for i, v in enumerate(sends):
            table[i] = v

    choose(row * 16 + column, 0, 256, leaf)
    sends = count[2]
    barrier = pltpu.get_barrier_semaphore()

    @pl.loop(0, count[0])
    def _(i):
        v = origin[i]
        chip, flip = v % 256, v // 256
        there = (chip // 16) * 2 + (half + flip) % 2
        pl.semaphore_signal(barrier, inc=1, device_id=(there, chip % 16), device_id_type=MESH)

    load.wait()
    for i in range(3):
        for j in range(6):
            keep = mask_ref[i, j].astype(jnp.float32)
            at = (pl.ds(i * 128, 128), pl.ds(j * 128, 128))
            buf[at] = (buf[at].astype(jnp.float32) * keep).astype(jnp.bfloat16)

    @pl.when(count[1] > 0)
    def _():
        pl.semaphore_wait(barrier, count[1])

    def slot(index):
        return buf.at[pl.ds(pl.multiple_of(index * SIZE, SIZE), SIZE)]

    def copy(v, i):
        chip = (v // 65536) % 256
        there = (chip // 16) * 2 + (half + (v // 2**24) % 2) % 2
        return pltpu.make_async_remote_copy(
            src_ref=slot(v % 256),
            dst_ref=slot((v // 256) % 256),
            send_sem=send_sem.at[i],
            recv_sem=recv_sem.at[(v // 256) % 256],
            device_id=(there, chip % 16),
            device_id_type=MESH,
        )

    def arrived(index):
        pltpu.make_async_copy(slot(index), slot(index), recv_sem.at[index]).wait()

    @pl.loop(0, sends)
    def _(i):
        v = table[i]

        @pl.when((v // 2**25) % 2 == 1)
        def _():
            arrived(v % 256)

        @pl.when((v // 2**26) % 2 == 1)
        def _():
            copy(v, i).start()

    has0 = (row == 0) | ((column >= row) & (row + column >= 16))
    has1 = (column < 15) & ((row <= 1) | ((column + 1 >= row) & (row + column >= 16)))
    here = pl.ds(pl.multiple_of(half * 384, 128), 384)
    other = pl.ds(pl.multiple_of(384 - half * 384, 128), 384)
    acc[...] = jnp.zeros_like(acc)

    def rows(index):
        return buf[pl.ds(pl.multiple_of(index * SIZE, SIZE), 384), :]

    @pl.when(has0)
    def _():
        @pl.loop(0, CHUNKS)
        def _(j):
            arrived(SIB + j)

        right = jnp.where(row + column == 0, 0, RIGHT0)
        acc[:, here] = nt_dot(rows(0), rows(right))
        acc[:, other] = nt_dot(rows(0), rows(SIB))

    @pl.when(has1)
    def _():
        @pl.loop(0, CHUNKS)
        def _(j):
            arrived(SIB + CHUNKS + j)

        left = jnp.where(column == 0, RIGHT1, LEFT)
        acc[:, here] += nt_dot(rows(left), rows(RIGHT1))
        acc[:, other] += nt_dot(rows(left), rows(SIB + CHUNKS))

    out_ref[...] = acc[...].astype(jnp.bfloat16)

    @pl.loop(0, sends)
    def _(i):
        v = table[i]

        @pl.when((v // 2**26) % 2 == 1)
        def _():
            copy(v, i).wait_send()


def per_device(upper_store, block_mask):
    return pl.pallas_call(
        kernel,
        out_shape=jax.ShapeDtypeStruct((384, 768), jnp.bfloat16),
        in_specs=[pl.BlockSpec(memory_space=pl.ANY), pl.BlockSpec(memory_space=pltpu.SMEM)],
        out_specs=pl.BlockSpec(memory_space=pltpu.VMEM),
        scratch_shapes=[
            pltpu.VMEM((SLOTS * SIZE, 768), jnp.bfloat16),
            pltpu.VMEM((384, 768), jnp.float32),
            pltpu.SMEM((MAX_SENDS,), jnp.int32),
            pltpu.SMEM((MAX_FROM,), jnp.int32),
            pltpu.SMEM((3,), jnp.int32),
            pltpu.SemaphoreType.DMA,
            pltpu.SemaphoreType.DMA((MAX_SENDS,)),
            pltpu.SemaphoreType.DMA((SLOTS,)),
        ],
        compiler_params=pltpu.CompilerParams(
            collective_id=0, has_side_effects=True, vmem_limit_bytes=48 * 2**20
        ),
        name="cannon_steps",
    )(upper_store, block_mask)


def solution(mesh):
    spec = P("brow", "bcol")
    return jax.shard_map(per_device, mesh=mesh, in_specs=(spec, spec), out_specs=spec, check_vma=False)
```

time: 205 us -> 46.9 us (0.23)
  the two profiles are of different devices: /device:TPU:223 before, /device:TPU:19 now
where the time goes in v1:
time: 46.9 us; the launch traced here: 46.7 us
  Pallas kernels  44.1 us (94%)
  local copies, waits for them, and re-layouts  2.56 us (5%)
    pallas_call x1, Pallas kernels, per_device(): pl.pallas_call(kernel, out_shape=jax.ShapeDtypeStruct((384, 768), jnp.bfl...  44.1 us
    unnamed x5, local copies, waits for them, and re-layouts  2.56 us

profile of v1, /device:TPU:19, one launch (start us, length us, event | category | flops | bytes accessed | tf_op | source)
XLA Modules:
  0.0 46.7 jit_solution(12777461976398508506)
XLA Ops:
  0.0 0.0 copy-start
  0.0 1.1 %copy-done = bf16[384,768]{1,0:T(8,128)(2,1)S(1)} copy-done((bf16[384,768]{1,0:T(8,128)(2,1)S(1)}, bf16[384,768]{1,0:T(8,128)(2,1)}, u32[]{:S(2)}) %copy-start) | copy-done | bytes 589848
  1.1 0.0 copy-start.1
  1.1 0.7 %copy-done.1 = s32[3,6]{1,0:T(4,128)S(1)} copy-done((s32[3,6]{1,0:T(4,128)S(1)}, s32[3,6]{1,0:T(4,128)}, u32[]{:S(2)}) %copy-start.1) | copy-done | bytes 96
  1.7 44.1 %cannon_steps.1 = bf16[384,768]{1,0:T(8,128)(2,1)S(1)} custom-call(bf16[384,768]{1,0:T(8,128)(2,1)S(1)} %copy-done, s32[3,6]{1,0:T(4,128)S(1)} %copy-done.1), custom_call_target="tpu_custom_call" | custom-call | tf_op jit(solution)/shard_map/cannon_steps/pallas_call | solution.py:406
  45.9 0.8 %copy.4 = bf16[384,768]{1,0:T(8,128)(2,1)} copy(bf16[384,768]{1,0:T(8,128)(2,1)S(1)} %cannon_steps.1) | data formatting | bytes 1179648
Async XLA Ops:
  0.0 1.1 %copy-start = (bf16[384,768]{1,0:T(8,128)(2,1)S(1)}, bf16[384,768]{1,0:T(8,128)(2,1)}, u32[]{:S(2)}) copy-start(bf16[384,768]{1,0:T(8,128)(2,1)} %upper_ref.1) | copy-start | bytes 1769476
  1.1 0.7 %copy-start.1 = (s32[3,6]{1,0:T(4,128)S(1)}, s32[3,6]{1,0:T(4,128)}, u32[]{:S(2)}) copy-start(s32[3,6]{1,0:T(4,128)} %mask_ref.1) | copy-start | bytes 220

commit v2 on v0

v2 whole, which is shorter than its diff:
```python
import jax
import jax.numpy as jnp
from jax import lax
from jax.experimental import pallas as pl
from jax.experimental.pallas import tpu as pltpu
from jax.sharding import PartitionSpec as P

CHUNKS = 6
SLOTS = 45
SIB = 33
PLAN = (
    ((1, 14, 16, 17, 31, 48, 224, 256), 5, (83894528, 83894785, 83895042, 83895299, 83895556, 83895813, 101717528, 103681305, 117451285, 101719578, 71178010, 117450514, 117450771, 117451028, 101583131, 117451542, 117451799, 103683612)),
    ((2, 3, 15, 16, 17, 18, 31, 33, 225, 257), 10, (70260738, 81795329, 68163584, 117516050, 82909458, 68163844, 67114243, 67114757, 117517335, 68225815, 117516307, 117514765, 68162317, 117516564, 68225044, 33554441, 117515279, 33554438, 33554443, 103682840, 117514508, 68162060, 33554440, 33554439, 33554442, 117515793, 68163345, 104731929, 70192921, 117515022, 117515536, 117516821, 117517078)),
    ((3, 18, 19, 32, 34, 48, 50, 51, 52, 96, 194, 226, 258), 8, (69277697, 81860613, 81860868, 68229122, 67311619, 67175936, 101845016, 101845274, 33554439, 101845785, 117580558, 68360718, 33554440, 33554443, 33554438, 117580815, 68228367, 117581329, 68228881, 117582100, 33554442, 117581072, 117581843, 117582357, 117582614, 117580301, 117581586, 33554441, 117582871, 117580044)),
    ((2, 17, 18, 19, 20, 33, 35, 37, 49, 51, 53, 131, 195, 227, 243, 259), 8, (79828994, 70391813, 81926147, 81926404, 68294657, 67241472, 101914649, 67179289, 100731160, 101910554, 100731931, 117646865, 68294417, 117646608, 68294160, 117648150, 33554440, 33554442, 117645837, 68293389, 117646351, 117647893, 33554438, 117646094, 117647636, 117648407, 117645580, 33554443, 117647122, 33554439, 117647379, 33554441)),
    ((5, 12, 20, 21, 36, 66, 68, 84, 130, 132, 228, 244, 260), 9, (33554442, 79894528, 117711887, 69409029, 81991681, 81991939, 68360450, 68425988, 68622351, 33554438, 117711630, 68359182, 33554441, 101976600, 33554439, 101976345, 105647131, 72949531, 117711373, 117711116, 68358668, 101975578, 117712401, 68359953, 33554443, 33554440, 117712658, 117712144, 117713943, 117713686, 117713172, 117712915, 117713429)),
    ((20, 21, 22, 23, 37, 39, 53, 65, 69, 71, 85, 87, 197, 229, 231, 261), 8, (82057217, 82057474, 83105797, 68425731, 67373572, 67372544, 101911321, 102107928, 117777423, 68424975, 102042394, 33554440, 117776652, 68424204, 33554442, 102042139, 117777166, 68424718, 33554438, 33554439, 117777680, 33554443, 117777937, 68425489, 33554441, 117778708, 117778965, 117779222, 117776909, 117779479, 117778194, 117778451)),
    ((7, 21, 22, 23, 25, 36, 38, 40, 54, 70, 98, 102, 166, 246, 262), 6, (69671170, 82122756, 68491265, 68556805, 68557059, 82253824, 102106904, 117842702, 68490254, 33554442, 117843473, 68491025, 117842445, 68489997, 117843216, 68490768, 33554443, 117844758, 117844244, 117843987, 33554438, 117844501, 117843730, 33554440, 117845015, 33554441, 33554439, 117842959, 117842188)),
    ((8, 22, 24, 27, 39, 69, 73, 99, 103, 119, 151, 167, 183, 231, 263), 9, (70654464, 83237634, 68557571, 68753921, 67504644, 67504901, 104471320, 74125336, 113645833, 117908495, 70654735, 117909009, 68556561, 33554440, 117909523, 117910037, 117908752, 68556304, 33554443, 117909780, 117910294, 117908238, 117909266, 117907724, 33554438, 117910551, 117907981, 33554439, 33554442)),
    ((9, 11, 23, 24, 25, 40, 72, 88, 89, 136, 164, 166, 232, 264), 11, (72882436, 67569923, 78125056, 82319361, 68688386, 68688645, 82188549, 76025346, 102237721, 33554441, 33554442, 117974545, 68622097, 107614744, 67765784, 117973517, 33554438, 117975316, 117975573, 33554443, 117974802, 117973260, 117976087, 117973774, 117975059, 117975830, 117974031, 117974288, 33554439, 33554440)),
    ((11, 24, 25, 26, 27, 41, 43, 73, 89, 105, 197, 199, 201, 233, 265), 12, (68687876, 69671936, 69736709, 70850561, 68688128, 75042563, 83433474, 67635459, 102173464, 102172953, 33554438, 115809306, 68750106, 33554440, 33554442, 114891291, 68749595, 118039567, 68687119, 33554443, 118039053, 68686605, 118040081, 68687633, 118039824, 118040338, 118040852, 118038796, 118041623, 118041366, 118040595, 118041109, 118039310, 33554441, 33554439)),
    ((8, 11, 12, 25, 26, 27, 29, 42, 168, 170, 184, 198, 202, 230, 234, 266), 11, (83237377, 82057733, 68753408, 82450435, 68753669, 74059266, 67835906, 68884740, 74059780, 105647640, 102370073, 102369306, 33554439, 118104846, 68885006, 101451803, 118104589, 68752141, 33554442, 118104332, 68751884, 118105617, 33554441, 118105874, 118106645, 118105103, 33554440, 118106388, 118106131, 118105360, 118106902, 33554443, 118107159, 33554438)),
    ((10, 13, 26, 28, 29, 43, 45, 165, 169, 171, 180, 187, 188, 213, 221, 235, 250, 267), 10, (82188291, 68491521, 67639296, 73076226, 70981637, 73076740, 68818945, 67766788, 101255192, 118170125, 68817677, 118172181, 33554440, 33554442, 118170382, 68817934, 33554439, 118170896, 118169868, 68817420, 33554438, 101520665, 118172438, 118171667, 118170639, 118172695, 33554443, 118171153, 118171410, 118171924, 33554441)),
    ((10, 14, 27, 29, 42, 44, 76, 192, 204, 206, 218, 232, 236, 250, 268), 14, (67377920, 82516229, 72093443, 67770370, 68032516, 71047429, 68950020, 67967489, 67967744, 72092929, 69016066, 102500120, 104537114, 70127130, 102501145, 118235661, 68883213, 118235404, 69016332, 33554438, 33554440, 118236689, 68884241, 33554441, 118237717, 33554439, 118237974, 80480790, 118236175, 68883727, 33554443, 118235918, 118236946, 118238231, 33554442, 118237460, 118237203, 118236432)),
    ((11, 12, 15, 28, 29, 30, 31, 45, 61, 111, 193, 201, 205, 207, 220, 237, 253, 269), 11, (71110403, 68884481, 71047172, 69146629, 69015554, 69015808, 115808793, 71047705, 68880409, 105713688, 68946456, 103750940, 69011740, 33554443, 33554439, 101386010, 118301197, 68948749, 101385755, 118302225, 118301711, 68949263, 118302996, 33554442, 118303510, 118301454, 33554441, 118301968, 118303767, 118300940, 33554438, 33554440, 118302739, 118303253, 118302482)),
    ((0, 12, 15, 30, 31, 46, 224, 236, 238, 240, 254, 255, 270), 11, (68098565, 67901954, 70127363, 69081348, 67115265, 70126592, 68098818, 69146881, 104798744, 118366733, 72093720, 69014285, 100670474, 118366476, 103682566, 69143558, 118367504, 118368532, 82708500, 118367761, 118366990, 118369046, 118369303, 82709271, 118368789, 82708757, 33554440, 33554443, 118367247, 33554441, 118368275, 118368018, 33554439)),
    ((14, 17, 29, 30, 239, 254, 255, 271), 13, (68229379, 67180545, 69144837, 68028932, 69081600, 69081858, 69144580, 69144066, 104666906, 67963674, 100733209, 104471580, 69011996, 70065436, 105712920, 105714205, 118432526, 101517339, 118432783, 118432269, 83756813, 118433040, 69080592, 118432012, 118433297)),
    ((0, 1, 28, 30, 208, 240, 272), 10, (100667928, 115677466, 83434010, 73142554, 100668953, 118500118, 67178518, 111221275, 71175451, 118499347, 105454876, 71175708, 102632222, 104729629, 118499090, 118499861, 118500375, 118499604)),
    ((1, 2, 15, 19, 31, 49, 51, 224, 241, 273), 10, (67312384, 81861122, 67115012, 80746499, 68098309, 67177729, 67178243, 100730904, 102767897, 67115801, 69144345, 100734217, 100734474, 33554439, 33554440, 118564883, 33554443, 103683866, 33554438, 118565397, 118565911, 118565140, 118565654, 118564626)),
    ((2, 3, 48, 50, 82, 210, 242, 274), 6, (81795076, 82909187, 67179008, 67311873, 67180293, 67179522, 100796184, 33554440, 33554441, 33554438, 33554443, 33554442, 118631447, 33554439, 118630162, 67308562, 118630676, 118631190, 118630419, 118630933)),
    ((2, 3, 4, 5, 23, 49, 83, 211, 243, 245, 275), 6, (80877568, 67246082, 67246341, 67246595, 82974724, 82974977, 101779224, 100861977, 33554443, 118696212, 33554440, 33554439, 33554442, 101782554, 33554441, 118696469, 118695698, 118695955, 33554438, 118696983, 118696726)),
    ((4, 5, 52, 80, 212, 242, 244, 276), 8, (70326273, 80943108, 67312130, 83040259, 67442949, 83171328, 100927768, 100862489, 33554442, 118761491, 67439891, 118762005, 33554441, 118761234, 33554440, 33554438, 118761748, 33554439, 118762519, 118762262, 33554443)),
    ((5, 6, 11, 53, 55, 113, 117, 245, 277), 9, (82975234, 81008641, 67377156, 67377411, 67377664, 83106565, 100992792, 105519129, 73075993, 118827284, 118826770, 67505170, 118828055, 33554443, 118827541, 118827798, 33554442, 33554438, 33554439, 118827027, 33554441, 33554440)),
    ((5, 6, 7, 26, 39, 54, 114, 118, 246, 278), 10, (70588672, 70720002, 67443205, 67443460, 83171841, 83172099, 100993816, 100993305, 101058843, 117120026, 75107354, 71900186, 33554442, 33554440, 33554443, 33554439, 33554438, 33554441, 118892306, 67570706, 118892563, 67570963, 118893591, 118892820, 118893334, 118893077)),
    ((4, 8, 9, 24, 89, 135, 147, 183, 215, 245, 247, 279), 8, (67442693, 70653956, 69670915, 67508225, 83236866, 83237120, 33554439, 101913880, 33554438, 33554443, 118957842, 67636242, 33554440, 33554441, 118958099, 118958356, 118958613, 67637013, 118959127, 118958870, 33554442)),
    ((8, 9, 56, 150, 152, 214, 244, 248, 280), 8, (83171586, 83302404, 67704837, 67705091, 68617985, 68617728, 116857112, 80222232, 67635736, 101124122, 101189145, 101124891, 33554438, 33554441, 33554439, 119023378, 67701778, 119024149, 33554440, 119023892, 67702292, 119023635, 119024663, 119024406, 33554443, 33554442)),
    ((7, 9, 10, 26, 27, 185, 217, 247, 249, 251, 281), 12, (83106049, 83106307, 80287749, 70785027, 70785282, 67639552, 83367940, 71899392, 82385154, 108597784, 67700248, 101255961, 101058330, 119089685, 67768085, 33554443, 119089942, 67768342, 33554441, 119089171, 33554440, 119089428, 33554442, 119088914, 119090199, 33554438, 33554439)),
    ((10, 11, 27, 56, 58, 90, 186, 250, 282), 11, (68557312, 82384898, 82254081, 67705349, 75108356, 69867523, 67705603, 73144581, 68749828, 101320472, 108664073, 33554443, 119155478, 67833878, 119154707, 33554440, 119155221, 33554438, 119154964, 33554442, 119154450, 33554439, 119155735)),
    ((10, 12, 13, 28, 29, 59, 219, 249, 251, 283), 12, (67573764, 69868033, 73013504, 68815107, 81401861, 67770629, 67770882, 74124802, 101255705, 103422744, 71109912, 33554441, 33554440, 119220243, 119220500, 67898900, 102306842, 119221014, 67899414, 33554442, 33554439, 119219986, 119221271, 119220757, 33554438, 33554443)),
    ((12, 13, 29, 30, 60, 216, 220, 252, 284), 9, (68164101, 70523136, 67967234, 69933060, 82647041, 68880643, 73142019, 106697993, 101386776, 33554442, 33554443, 119285779, 33554439, 33554438, 33554440, 119286550, 119286293, 119286807, 119286036, 119285522)),
    ((12, 13, 14, 15, 30, 31, 77, 241, 253, 285), 12, (69539845, 69081090, 68098049, 68946179, 70064128, 67901441, 67901701, 67966980, 101325592, 71110168, 104664089, 67896857, 101386266, 33554439, 119351058, 33554442, 33554440, 33554441, 119351829, 102437403, 119351315, 119351572, 119352343, 119352086, 33554438, 33554443)),
    ((14, 15, 16, 29, 31, 46, 62, 240, 254, 286), 12, (68164353, 68164610, 71176453, 68164864, 68099076, 68099328, 67968003, 69011458, 69011201, 83696133, 106697752, 68945944, 103682073, 67963417, 101582362, 103683099, 68028443, 104732170, 33554439, 33554443, 119417879, 33554438, 119416594, 119417622, 83757590, 33554441, 119417108, 119417365, 33554440, 119416851)),
    ((13, 14, 15, 17, 46, 238, 287), 13, (67115525, 67180803, 70129665, 69077508, 70192128, 70192642, 103554328, 101517081, 71110936, 71111449, 119481873, 68229649, 116071962, 68029201, 69014042, 119481359, 119481102, 119481616, 119480588, 119480845)),
    ((17, 34, 45, 46, 47), 6, (105778968, 116464409, 67244057, 103881498, 67243034, 103881756, 72225820, 103683357, 107746587)),
    ((2, 52, 59, 61, 62), 4, (100730648, 107811353, 100865818, 100864795, 109776668, 107812381)),
    ((35, 47, 63), 8, (69212420, 69212672, 67243522, 70523393, 67244293, 67243779, 70457601, 104864536, 71375384, 73274904, 100800025, 104012570, 72226074)),
    ((4, 51, 62), 8, (73406464, 70260997, 81926657, 69343492, 70392066, 70457347, 100864024, 100862745, 100863258, 105715483)),
    ((42, 69, 102), 4, (101060632, 108337945, 76156185, 100930074)),
    ((29, 41, 51, 52, 56, 86), 7, (100865562, 103947033, 67309337, 106437144, 72159512, 100996892, 110694171, 109777693)),
    ((44, 59, 61, 103), 3, (101062168, 101062425, 107745562, 105649435, 107746844)),
    ((6, 9, 23, 59, 120), 5, (100993049, 102107416, 108596252, 101126938, 109776157, 101127963)),
    ((9, 41, 57, 117, 136), 4, (101191960, 110694682, 109582105, 67635993, 101060379, 101192476, 101189405)),
    ((59, 137, 154), 8, (69540611, 72816896, 69736965, 83433730, 75044868, 72948993, 101257752, 109776921, 101258778)),
    ((26, 27, 59, 91, 170), 11, (69474561, 70654211, 70719492, 82319616, 70981893, 78256130, 104341018, 75109146, 108662552, 101321753, 101451547, 72094491, 101320732, 101321501)),
    ((28, 61, 91, 154, 171), 13, (70719749, 70588932, 82451202, 79305728, 83564803, 73210625, 111873817, 106437400, 70983448, 74126872, 107809819, 101389852, 101258522)),
    ((31, 46, 61, 74), 11, (70326784, 70392322, 69605893, 83564548, 73145091, 74190081, 106763544, 111808281, 108795418, 108794907, 101452060, 101452573, 72095517)),
    ((15, 29, 46, 61, 76, 78, 124), 13, (70457861, 69212931, 70982404, 70850816, 73207298, 71112961, 71113219, 104602392, 72158232, 112988441, 80418585, 107810586, 101517596, 105711387, 101386526, 105715229)),
    ((0, 1, 12, 14, 17, 30, 31, 32, 50, 61, 62, 63, 78, 302), 11, (69212163, 71243777, 69998595, 72223744, 72225029, 72224772, 72224258, 120464399, 70065167, 71244047, 120463628, 71111180, 102631192, 71176984, 120463885, 120464656, 71112208, 120465684, 120465427, 69143827, 68028179, 120464142, 105779975, 71240967, 120465170, 120466455, 120465941, 33554440, 120464913, 120466198, 33554443, 33554438, 33554442, 33554441)),
    ((1, 13, 31, 62, 63, 126, 143, 303), 10, (69213186, 69343747, 71241732, 71241989, 71178241, 71240704, 104471064, 72289304, 104729369, 72290585, 112006682, 112006427, 120529164, 71176716, 114103068, 120529678, 71177230, 105714973, 71175965, 120529421, 120529935, 120530449, 120530192)),
    ((1, 35, 51, 60), 4, (100668440, 101847578, 108794139, 100800281)),
    ((20, 32, 44, 51), 6, (101910296, 100863513, 108271642, 75174426, 101782043, 104795676)),
    ((3, 35, 37, 44, 63), 6, (100797208, 100799513, 104405530, 74190362, 101848347, 105780764, 70126108)),
    ((34, 35, 45), 11, (70261248, 69540099, 69408772, 69409281, 72488962, 70326530, 67309829, 101782297, 100799768, 107092506, 73208090, 104795931)),
    ((28, 34, 85), 10, (75700226, 69278213, 69278465, 83040512, 70588419, 69540356, 101978904, 100797722, 107288857, 70983193, 73141273)),
    ((22, 43, 52, 86), 4, (100865304, 102041113, 100995867, 108728346)),
    ((7, 23, 42), 4, (102107672, 101058074, 110565913, 76156697, 102110491)),
    ((22, 42, 43), 5, (104995609, 75174169, 102041626, 105388568, 77141528)),
    ((25, 42, 58, 59, 60), 7, (106175258, 77205018, 102238488, 103095580, 75238684, 102238233, 113843227, 77205531, 110760477, 102369054)),
    ((9, 45, 50), 5, (103292184, 75042072, 107745817, 70983705, 108729370)),
    ((7, 15, 47, 60, 91), 8, (70785538, 79304709, 82385409, 70785796, 77204480, 79305219, 112858136, 108793369, 72030745, 104728090, 102369819, 104730652)),
    ((11, 12, 42, 43, 45, 52, 57, 60, 107), 14, (69278723, 69672193, 82320389, 70786304, 69802244, 83499266, 110696217, 103423256, 73077016, 103160859, 73207835, 112922906, 102435359, 104666140, 104665117, 106761248, 102434334)),
    ((12, 13, 45), 10, (70786049, 70261509, 70916354, 82516997, 79435779, 75238400, 75239428, 105649688, 70982936, 105648409, 102499867, 106696218)),
    ((13, 15, 27, 29, 31, 45, 46, 59, 62, 63, 79, 109, 157, 235, 317), 13, (69933824, 69999108, 69999362, 70064643, 72161797, 72162049, 121447439, 69606159, 69999631, 102833418, 33554443, 106761497, 121447182, 72094734, 33554439, 106762010, 121446668, 72094220, 33554441, 114101272, 121449495, 70127895, 121448981, 121448210, 67962386, 106632987, 121446925, 121447953, 33554440, 121449238, 121448467, 121448724, 33554438, 121447696)),
    ((0, 1, 16, 30, 46, 47, 58, 64, 94, 318), 9, (81861381, 71109124, 69277952, 71108353, 71108867, 71109381, 73272834, 73272577, 73273091, 73273348, 121513489, 69409553, 103679768, 106829579, 121514003, 70192403, 121512461, 121513746, 69076498, 121515031, 70193431, 33554441, 121514774, 70193174, 121514517, 69077269, 33554442, 33554438, 121512204, 121514260, 69077012, 33554440, 121512718, 121512975, 33554439, 121513232)),
    ((14, 46, 47, 49, 51, 319), 11, (78649345, 69343236, 70195200, 72226819, 72289794, 70195461, 106763032, 121578768, 70392848, 104666393, 121579025, 72226577, 121577740, 72225292, 70125068, 106632730, 121578254, 121577997, 121578511)),
    ((34, 79, 93, 95), 4, (110891800, 104729115, 108923930, 107878169)),
    ((34, 85, 94), 4, (105912856, 67440664, 100995353, 105844762, 107941659)),
    ((55, 69, 77, 79), 4, (107877657, 100930586, 109843480, 109713179)),
    ((76,), 1, (111875864,)),
    ((69,), 5, (75634693, 75765760, 72554500, 67374851, 67374594, 72554753, 72620033, 100931096, 100930841)),
    ((81, 86, 88, 91), 8, (71440898, 69474816, 71571460, 71571715, 72620293, 72620545, 100996121, 111874328, 101124634, 105712155)),
    ((74, 103), 2, (111808794, 101061144, 111808537, 111807515)),
    ((86, 92), 4, (100995608, 110237977, 78320409, 72949785)),
    ((55, 76, 137), 3, (101192728, 109842201, 109711386)),
    ((16, 22, 25, 75, 120, 153), 6, (106175515, 77270043, 101256986, 101127704, 109644825, 109646364, 105714717)),
    ((21, 91), 6, (72751106, 71702788, 71703045, 71703296, 69998851, 78253313, 105646873, 107615000, 107615770)),
    ((58, 92, 93), 10, (71899904, 75175937, 72948484, 72948739, 77271301, 73079298, 106568216, 76353816, 111875609, 73075225, 109777946, 107681051)),
    ((4, 10, 12, 14, 38, 42, 44, 60, 61, 74, 78, 92, 93, 108, 125, 332), 15, (72423428, 71833859, 74062337, 73144322, 76286976, 76288261, 106695448, 105060377, 72358681, 73075481, 108860442, 72157210, 122430479, 70065679, 73210895, 106629403, 33554442, 107746332, 122429965, 73077517, 122430222, 73077774, 122432278, 67897878, 33554438, 33554441, 122431507, 122430993, 122430736, 122431764, 122429708, 122431250, 33554439, 33554443, 33554440, 122432535, 122432021)),
    ((13, 15, 35, 37, 45, 47, 61, 69, 73, 76, 92, 93, 94, 108, 125, 161, 333), 9, (71440386, 73079045, 75303936, 73209859, 75304193, 73144836, 73210114, 73210372, 106695193, 76353561, 106760984, 76355352, 107811098, 106628636, 122495244, 73142796, 107810075, 33554440, 122496272, 73143824, 122496786, 69010962, 122495758, 122495501, 73143053, 122496529, 33554439, 33554441, 122498071, 33554438, 122497557, 33554442, 122496015, 122497814, 33554443, 122497043, 122497300)),
    ((32, 34, 46, 50, 63, 93, 94, 95, 110, 334), 10, (72423940, 70064897, 74321667, 72096258, 74322181, 122560780, 73341184, 73208332, 74321153, 74321924, 106829080, 122562065, 73209617, 116202777, 73205785, 106826523, 122561294, 73341454, 122561551, 106760730, 122561808, 73341712, 107877127, 107877898, 33554440, 122562836, 70125588, 122563607, 70126359, 122561037, 33554438, 122562322, 122562579, 122563093, 70125845, 33554441, 122563350, 33554443)),
    ((47, 63, 65, 94, 95, 177, 335), 11, (71440643, 71309573, 72423685, 74322946, 73337856, 73275393, 73338884, 73338370, 73338113, 109909272, 122626316, 73273868, 104663066, 74257434, 122626830, 73274382, 122627601, 107811611, 106826265, 74387481, 107812124, 122627087, 122627344, 122626573)),
    ((65, 76, 92, 95), 3, (101979674, 110890009, 108925464, 110891291)),
    ((76, 78, 79), 4, (110827032, 105192218, 75306522, 106893593)),
    ((51, 91, 94), 3, (101848088, 112857625, 108926234)),
    ((68, 95), 4, (115612440, 68359704, 101913369, 108141082, 74387738)),
    ((56, 68, 69, 73), 3, (100928792, 100931353, 100930330, 111809052, 111744027)),
    ((), 4, (71374852, 71375109, 80025602, 70522881, 67440387, 67439616)),
    ((74,), 7, (80026372, 70589185, 72817155, 69540869, 71637250, 71768064, 111808024)),
    ((41, 86, 122), 3, (100996378, 110693401, 108595992)),
    ((8, 37, 43, 137), 4, (105191961, 76025881, 101192984, 106698522, 106696731)),
    ((4, 41, 71, 75, 92, 136, 153, 154), 6, (102175768, 67636760, 101257497, 110825244, 110825499, 101259034, 110693661, 106629150, 106631711, 106628896)),
    ((27, 75, 93), 4, (110892312, 73140504, 102368793, 75108889, 110892826)),
    ((11, 21, 59, 61, 63, 75, 76, 77, 89, 93, 94, 106, 181, 347), 13, (72489216, 71636997, 70916098, 69933315, 82516740, 77142785, 123413262, 69868558, 74060814, 106759960, 105519385, 75305241, 110824986, 123413776, 71965200, 33554443, 33554441, 33554438, 123414033, 74061585, 123413005, 33554442, 123414547, 33554440, 123415575, 123414804, 123413519, 123415061, 123412748, 123414290, 123415318, 33554439)),
    ((16, 26, 28, 30, 44, 52, 60, 76, 77, 88, 90, 107, 144, 156, 348), 13, (72096005, 71768321, 72358144, 83565058, 72949250, 72030468, 72096515, 83630339, 72162304, 77336066, 109841944, 109843994, 72092186, 107745051, 33554443, 33554442, 108663065, 123480340, 72158740, 33554441, 123479055, 72030991, 123479569, 123479826, 123480597, 72158997, 123478284, 123480854, 123478798, 123481111, 33554439, 123478541, 123479312, 33554440, 123480083, 33554438)),
    ((43, 44, 45, 51, 59, 61, 63, 76, 77, 78, 91, 95, 141, 349), 13, (82843648, 71309313, 82581506, 73013251, 72030213, 72095749, 72161540, 107747608, 75304728, 123544334, 72096782, 123545619, 72224019, 108727579, 123545362, 33554439, 33554438, 123544077, 74191629, 105646105, 75304473, 123546647, 33554443, 33554440, 123545876, 108859418, 106632476, 123544848, 123546390, 33554442, 33554441, 123544591, 123545105, 123546133, 123543820)),
    ((34, 62, 78, 79, 95, 109, 112, 126, 160, 176, 350), 10, (73340928, 75369729, 72227074, 73078785, 72292355, 72227332, 72161285, 75370500, 75370243, 75370757, 75369986, 123609870, 72292878, 123609613, 72293133, 105776920, 123610127, 72293391, 123611669, 71174421, 72290069, 106043913, 71375625, 33554443, 123610898, 123610384, 123611412, 71174164, 123612183, 123611155, 71173907, 123611926, 108926474, 123610641, 123609356, 33554440, 33554439, 33554438)),
    ((78, 79, 81, 94, 110, 351), 12, (72555013, 73271555, 72357888, 74386946, 74323969, 72227589, 72292612, 104864280, 76487704, 73205272, 123674892, 74322444, 108859929, 123675920, 72223248, 123675406, 106763290, 123675149, 106763803, 123676177, 123675663)),
    ((35, 109, 111), 3, (100799000, 111940122, 109974297)),
    ((127,), 2, (111023128, 76484120)),
    ((51, 103, 111), 3, (101061912, 109974553, 107747098)),
    ((120, 126), 2, (101126680, 109908761)),
    ((123,), 1, (111809304,)),
    ((52, 124), 3, (112335384, 80417560, 107680281)),
    ((103,), 5, (74520576, 69474308, 74782723, 77993985, 67506437, 67505666, 101061400)),
    ((120,), 6, (73537539, 77994242, 69605380, 69605637, 71702528, 73799681, 101127192)),
    ((107, 121, 122), 4, (108468760, 74058008, 109647385, 109581594)),
    ((122, 123, 138, 228, 246), 4, (109644313, 108661272, 108595738, 101254939, 75043611, 108599068)),
    ((8, 10, 74, 76, 91, 104, 107, 108, 121, 122, 123, 124, 228, 230, 234, 246, 362), 10, (111938584, 75176472, 124396302, 75043854, 108661019, 108595486, 111939353, 74123545, 124396816, 75176720, 79369497, 108661532, 109841690, 77271834, 33554438, 124397844, 33554441, 33554442, 108660253, 33554440, 124396559, 75044111, 124395788, 33554443, 124397330, 73075730, 33554439, 124396045, 124397073, 124397587, 124398615, 124398101, 124398358)),
    ((7, 27, 43, 75, 101, 106, 109, 122, 123, 124, 187, 229, 231, 237, 363), 12, (73930755, 74914048, 70982149, 75241989, 74057216, 75110914, 75111172, 79367682, 79368196, 75176193, 110955544, 108726041, 33554438, 33554441, 124463123, 73141523, 124461838, 75109390, 109777434, 33554440, 124462095, 124462352, 75109904, 33554439, 124462609, 124463894, 124463380, 124461581, 124464151, 33554443, 124461324, 124463637, 124462866, 33554442)),
    ((32, 38, 44, 50, 57, 76, 92, 93, 98, 110, 116, 123, 124, 125, 140, 172, 364), 12, (74651652, 74782981, 76158978, 74061824, 74062083, 75241473, 108791576, 111941130, 105646361, 76289305, 124527117, 75174669, 105711898, 75306266, 124527631, 75175183, 105645851, 76288795, 124528145, 75175697, 33554441, 124527374, 33554440, 124528659, 124528916, 33554438, 124529173, 124527888, 33554443, 124529687, 124526860, 124528402, 124529430, 33554439)),
    ((33, 43, 45, 77, 79, 111, 124, 125, 126, 157, 225, 365), 13, (73406976, 83630085, 75307010, 75241732, 74127360, 75307267, 75307524, 77402373, 77401345, 108665880, 78450200, 108727066, 108726811, 108927513, 78450969, 124593938, 71108114, 73272338, 33554440, 124593681, 75241233, 110957062, 107677468, 124593167, 75240719, 124594452, 124592396, 75239948, 124592653, 75240205, 124595223, 33554439, 124594966, 33554443, 124593424, 124594709, 33554441, 124592910, 124594195, 33554442)),
    ((64, 66, 78, 79, 95, 125, 126, 127, 142, 366), 10, (74651905, 75372546, 74389504, 75438082, 75438339, 76418048, 76419076, 76418819, 76419333, 124658703, 74193423, 124659988, 72222740, 124659217, 75306769, 109975307, 108925720, 124658189, 75305741, 124659474, 72222226, 124660245, 73338645, 72222997, 124658960, 108990474, 109974793, 124659731, 124660759, 72223511, 124660502, 33554440, 124658446, 33554439, 124657932, 33554438)),
    ((65, 79, 83, 95, 110, 126, 127, 223, 367), 12, (76552704, 73537794, 73406721, 76420612, 75372805, 75435779, 75435265, 75436293, 75435522, 107808280, 108923161, 76484377, 124723982, 74455310, 75371534, 109909530, 101519899, 124724753, 124724496, 124723725, 124724239, 124723468)),
    ((111, 125), 2, (112988696, 106825753)),
    ((102, 124, 127), 4, (102044184, 113711385, 75171353, 110038298)),
    ((83, 119, 125), 3, (102110233, 112989464, 108926746)),
    ((108, 110), 3, (110957337, 113252888, 79369752)),
    ((49,), 1, (107744280,)),
    ((36, 102, 108, 126), 6, (103291672, 68490520, 111483418, 75302426, 112924441, 110695195)),
    ((119,), 1, (102109720, 102109977)),
    ((104, 107, 122), 6, (74586370, 67571459, 74848256, 74848513, 67571973, 67571716, 77011202, 108594712, 112921625, 112922394)),
    ((123, 153), 7, (73603072, 78059523, 69671425, 69671685, 73865218, 71899140, 108660760, 110627609)),
    ((9, 25, 39, 41, 57, 87, 105, 106, 119, 122, 123, 136, 247, 249, 377), 5, (33554440, 110694424, 125380370, 74058770, 33554439, 125378828, 76026380, 33554441, 125379599, 73931279, 33554438, 125379342, 125381398, 125380884, 125379085, 76026637, 33554442, 125380113, 125379856, 125380627, 125381141, 33554443, 125381655)),
    ((22, 26, 42, 90, 92, 105, 106, 107, 109, 120, 123, 124, 218, 246, 250, 378), 11, (72816645, 74913792, 75040513, 75040770, 74063363, 73996804, 33554439, 113972504, 125445392, 73931024, 79433496, 107612699, 112987161, 33554441, 107612186, 33554440, 108791836, 125446677, 74125077, 125444364, 125447191, 74125591, 125446163, 74124563, 33554442, 33554443, 125445649, 33554438, 125446420, 125445906, 74124306, 125444878, 125445135, 125444621, 125446934)),
    ((49, 53, 55, 57, 75, 93, 106, 107, 108, 109, 113, 125, 127, 138, 251, 379), 12, (74979330, 73996292, 75106049, 74062595, 74062853, 74063104, 107677210, 107223064, 77270296, 108598811, 107611929, 79367449, 33554440, 33554443, 33554438, 33554439, 125511699, 125512470, 74190870, 125510157, 76157709, 125511185, 33554442, 125512213, 125510671, 125511442, 125510928, 76158480, 125512727, 33554441, 125510414, 125511956, 125509900)),
    ((44, 48, 56, 58, 60, 107, 108, 109, 122, 125, 126, 188, 380), 14, (74520832, 73734145, 70064389, 75110403, 79433732, 75439107, 75110656, 79433218, 74127617, 74258949, 74259204, 75307778, 111938840, 74259480, 107743769, 125575436, 74127884, 107612954, 125576464, 76224016, 33554439, 33554441, 125576721, 125576207, 125575950, 125578006, 74256406, 125578263, 125575693, 125577492, 74255892, 125577749, 33554440, 33554443, 125576978, 125577235, 33554438, 33554442)),
    ((76, 77, 81, 91, 93, 95, 108, 109, 110, 117, 124, 126, 127, 173, 381), 15, (74455040, 74586115, 82582276, 74258434, 75237635, 74192897, 74258693, 76356097, 111940632, 77401624, 33554439, 125640972, 72091148, 76288524, 108726299, 125641229, 74193677, 33554443, 125641743, 107743513, 77401881, 33554438, 125643028, 74321428, 110956570, 125642514, 72156690, 74320914, 125643799, 72157975, 125642257, 76289809, 125642771, 33554442, 125641486, 125643285, 33554441, 125642000, 125643542, 33554440)),
    ((64, 80, 82, 94, 109, 110, 111, 114, 143, 158, 382), 12, (74783232, 70195716, 70195971, 77467138, 75438597, 75302657, 75438850, 77466624, 77467652, 77467909, 77466881, 125706765, 73603341, 107808792, 107875097, 125707793, 125707536, 74390032, 125707279, 111023369, 125707022, 125708564, 125708307, 73271059, 74386707, 108792602, 33554442, 125706508, 125708050, 73270802, 74386450, 125709078, 33554438, 125708821, 33554439, 33554440, 125709335, 33554443)),
    ((110, 111, 124, 126, 145, 383), 10, (73472002, 74521089, 74389763, 76484612, 76484869, 76483584, 110957592, 125772815, 74320143, 116203034, 75303706, 108857371, 125772301, 110957849, 125773329, 108726556, 125772558, 125773072, 125772044)),
    ((143, 159), 2, (112071449, 113120024)),
    ((138, 158, 159), 5, (110172442, 80548890, 109644056, 113120793, 78581785)),
    ((68, 141), 2, (100929816, 114037785)),
    ((52, 157), 3, (100865048, 115086361, 80547353)),
    ((68, 141), 4, (100928536, 111156249, 78845977, 80483097)),
    ((158,), 2, (114103832, 112006169)),
    ((137, 139, 141), 3, (109578520, 109709850, 114037273)),
    ((136,), 2, (111417368, 68621848)),
    ((8, 40, 88, 104, 121, 134, 137, 150, 153, 168, 184, 198, 200, 230, 232, 249, 392), 10, (76748803, 75962372, 79108096, 69736453, 81205249, 72947714, 67636481, 103291911, 101192198, 126362382, 110627096, 33554443, 33554441, 126361868, 126362896, 126362125, 33554442, 126364695, 75043095, 126363153, 126363924, 126362639, 126364438, 126363410, 33554440, 126364181, 126363667)),
    ((73, 104, 105, 129, 152, 153, 154, 201, 217, 231, 233, 393), 11, (79173637, 71833602, 72882179, 76023553, 76023296, 79173892, 75896835, 76945410, 113711128, 77137944, 103356953, 77138457, 33554443, 33554442, 126429460, 33554439, 33554438, 126428689, 77076241, 126429203, 33554440, 126427404, 77074956, 33554441, 126429974, 126427661, 126427918, 77075470, 126430231, 126429717, 126428946, 126428175, 126428432)),
    ((36, 54, 66, 72, 108, 123, 134, 139, 153, 154, 155, 170, 186, 232, 234, 394), 8, (75569155, 73996548, 77142021, 77142274, 77142528, 77207553, 110757401, 112923672, 78384664, 33554443, 33554441, 110758427, 33554440, 33554442, 110758682, 33554439, 33554438, 126494996, 75173396, 126492940, 77140492, 126494482, 75172882, 126493454, 77141006, 126494225, 126493197, 126494739, 126495767, 126493711, 126495253, 126495510, 126493968)),
    ((33, 37, 39, 41, 75, 107, 124, 141, 154, 155, 156, 157, 171, 172, 203, 219, 235, 395), 8, (75897348, 78256898, 76155653, 76155139, 77207809, 77208064, 113053976, 111872794, 110823961, 33554438, 33554443, 126561303, 33554439, 126558733, 77206285, 33554442, 126561046, 126559247, 77206799, 126559504, 77207056, 126560789, 126560018, 126559761, 126560532, 126558990, 126560275, 126558476, 33554440, 33554441)),
    ((66, 72, 76, 92, 106, 108, 125, 155, 156, 157, 160, 204, 396), 12, (76814338, 76552452, 77273089, 80482051, 80481280, 76421125, 76355589, 76355844, 77404160, 115087128, 77335320, 126624012, 77271564, 110888473, 126625297, 77405201, 114038025, 107743002, 78385946, 126624526, 77272078, 126626325, 126625554, 126624269, 33554443, 126625811, 33554438, 126626068, 126626582, 126624783, 77272335, 126625040, 33554440, 126626839, 33554439, 33554442)),
    ((75, 77, 79, 99, 111, 125, 140, 143, 154, 156, 189, 237, 397), 12, (75766017, 75634946, 75897088, 77338627, 79499268, 76224517, 77273344, 77338885, 77339138, 77404418, 109775640, 110693147, 112004378, 126691861, 73206037, 109775385, 113055242, 126690576, 77338128, 126690833, 113054728, 33554443, 126689805, 126692118, 126692375, 33554441, 126690062, 126691347, 126690319, 126691604, 126691090, 33554438, 126689548, 33554439)),
    ((96, 98, 110, 111, 140, 144, 157, 158, 159, 174, 191, 398), 11, (76617731, 79632645, 78516228, 78516485, 78515457, 76486916, 76487170, 77469698, 77535232, 126755084, 111019545, 126756369, 77403921, 126756112, 77403664, 126757654, 74320406, 126755855, 110954266, 114037016, 112071174, 113119259, 126757140, 74319892, 126757911, 33554440, 126755598, 126756883, 74319635, 126755341, 126756626, 74319378, 33554441, 126757397, 33554439, 33554443, 33554442)),
    ((95, 97, 111, 113, 127, 142, 158, 159, 399), 11, (75503873, 79632384, 77532674, 77533188, 77532931, 77533445, 113121048, 78582040, 103750683, 79564059, 126821648, 77469200, 109906457, 109905946, 126821391, 126820620, 77468172, 112005917, 126821905, 77469457, 126820877, 75368205, 77468429, 109908508, 126821134)),
    ((111, 140, 159, 240), 5, (113120536, 110172698, 76419610, 114036761, 106694171)),
    ((129, 142, 144, 161), 4, (112204312, 79500568, 110954521, 108989466, 113052187)),
    ((71, 155), 2, (110757656, 110890265)),
    ((136, 159), 2, (102176024, 112135193)),
    ((140,), 2, (114036248, 80419096)),
    ((156,), 1, (113053464,)),
    ((137, 153), 3, (102241305, 77072409, 109578264)),
    ((54, 119, 156), 3, (101125657, 110823704, 110695706)),
    ((120, 136, 137, 150, 153, 168, 244, 248, 408), 4, (102240774, 112857880, 33554440, 33554441, 127412243, 76090643, 33554443, 127412757, 76091157, 127413014, 76091414, 127413271, 33554442, 33554439, 127411986, 127412500)),
    ((37, 40, 55, 59, 87, 89, 91, 117, 121, 137, 138, 141, 151, 155, 185, 249, 409), 13, (80025857, 76945666, 71899651, 72947973, 77071872, 80288260, 74979589, 78125825, 76027907, 109644568, 111873307, 77076507, 109643290, 109643801, 33554440, 33554441, 33554439, 33554442, 127477265, 127478807, 76157207, 33554443, 127477779, 127476494, 127477008, 127475980, 127477522, 127478550, 33554438, 127476751, 127476237, 127478036, 127478293)),
    ((56, 58, 138, 139, 146, 155, 186, 216, 232, 250, 410), 10, (72948229, 76093442, 69801984, 69933571, 79239681, 76093700, 79239936, 76356357, 77273603, 33554441, 109643544, 33554440, 127541516, 79240204, 109709081, 33554438, 109708826, 127542030, 33554439, 127542801, 33554442, 127544343, 76222743, 127542544, 127543572, 76221972, 33554443, 127543315, 127543058, 76221458, 127543829, 127542287, 127541773, 127544086)),
    ((73, 75, 81, 89, 91, 106, 123, 139, 140, 141, 151, 154, 156, 157, 189, 411), 9, (76683265, 77203715, 77203458, 76159232, 76159493, 76159748, 110692634, 33554438, 127608337, 78255889, 113908760, 76220184, 109839897, 33554439, 127608594, 127607309, 127607823, 78255375, 127607052, 127609622, 76288022, 127608080, 78255632, 33554442, 33554440, 127607566, 78255118, 33554443, 127608851, 33554441, 127609108, 127609365, 127609879)),
    ((64, 80, 90, 92, 140, 141, 146, 157, 171, 220, 236, 240, 252, 412), 12, (77010947, 77268480, 79501314, 76224772, 77404673, 77404933, 110434328, 76286232, 115086858, 33554441, 33554443, 109841177, 33554438, 109840410, 127674387, 73139987, 76352787, 127672588, 78320140, 127674644, 73140244, 76353044, 127675158, 127674901, 76353301, 33554439, 127674130, 76352530, 127675415, 127673102, 127673873, 127672845, 127673616, 127673359, 33554440)),
    ((107, 109, 115, 125, 127, 140, 141, 142, 145, 156, 158, 159, 205, 413), 13, (75700482, 71112704, 80418819, 80547073, 76290053, 77335044, 77334787, 76290304, 109774360, 113053209, 110823194, 127739409, 127740180, 76418580, 33554438, 127738381, 76290573, 127739923, 74254099, 127738638, 76418323, 127740951, 74255127, 110824219, 127740437, 74254613, 127738895, 78386447, 127738124, 127740694, 74254870, 33554441, 127739152, 127739666, 33554439, 33554440, 110827292, 33554443, 33554442)),
    ((97, 126, 142, 143, 173, 190, 414), 10, (75831300, 75569666, 79563776, 76487425, 77399552, 79565061, 79564547, 77535493, 77535747, 76421633, 76421892, 79564290, 127804174, 75831566, 127803917, 76487949, 127803660, 112070168, 127804688, 127806230, 75368982, 113119750, 127804945, 127805973, 33554441, 127805202, 75367954, 33554443, 127805716, 75368468, 127806487, 75369239, 33554440, 127804431, 33554442, 127805459, 33554439)),
    ((142, 143, 158, 174, 191, 415), 11, (76552195, 75503617, 75569412, 76749056, 78581250, 76421376, 76486661, 127869710, 78517262, 113054232, 127869967, 78517519, 110955289, 110954778, 127870481, 78518033, 127870224, 78517776, 127869196, 127869453)),
    ((132, 174, 175, 191, 225), 5, (114168344, 112531737, 77797401, 80613145, 106828058, 114168859, 109840156)),
    ((16, 190), 5, (110172952, 82646552, 81661976, 105714458, 114102809)),
    ((165, 173), 3, (114759960, 78382616, 114167833)),
    ((160,), 1, (112003352,)),
    ((135,), 1, (101191704,)),
    ((117, 174, 188), 4, (111286553, 78449177, 101388824, 78977560, 112005658)),
    ((102, 103, 184), 2, (101059864, 101061657, 101193498)),
    ((120, 172), 2, (101127448, 111872537)),
    ((8, 153, 171, 187), 6, (112662808, 76024856, 101323546, 78251802, 112854809, 110626587)),
    ((84, 170, 173, 185, 186, 187, 201, 217, 233, 425), 3, (33554442, 112794891, 101390104, 33554438, 33554439, 33554441, 33554440, 128526869, 128526098, 128526355, 128526612, 128527383, 128527126)),
    ((42, 44, 70, 74, 84, 86, 100, 139, 155, 168, 184, 186, 187, 189, 202, 426), 10, (69867776, 81336323, 67767810, 79239172, 67767553, 67768581, 78187269, 78186241, 79239426, 79304963, 79370240, 112855066, 109709339, 112985881, 33554439, 128590863, 128590349, 101324555, 109710872, 128592919, 128591377, 128590606, 128590092, 33554442, 33554440, 128592405, 128591120, 33554438, 128592662, 128591634, 128591891, 128592148, 33554441)),
    ((43, 67, 69, 71, 75, 139, 153, 156, 167, 172, 173, 186, 187, 188, 189, 235, 251, 427), 12, (80091139, 78125569, 79174148, 82450688, 80353282, 79305477, 79174400, 103488537, 79366681, 101387288, 33554440, 33554441, 128655885, 33554442, 33554438, 33554443, 109778202, 128656399, 79303951, 33554439, 128656913, 79304465, 128658198, 77336598, 128656142, 128656656, 128657684, 128657170, 128657427, 128658455, 128657941, 128655628)),
    ((96, 106, 108, 124, 125, 138, 140, 157, 162, 173, 187, 189, 192, 202, 206, 220, 221, 252, 428), 10, (78059780, 76225029, 78317570, 78452992, 78453249, 79502083, 112986648, 115150601, 128721164, 79368716, 128721421, 79368973, 128723220, 74188820, 128722706, 74188306, 128723991, 74189591, 128721935, 128723734, 33554438, 33554443, 33554439, 128722963, 128721678, 128723477, 128722192, 33554442, 128722449, 33554440)),
    ((47, 109, 133, 141, 143, 163, 165, 172, 175, 188, 190, 205, 221, 237, 429), 13, (77731840, 81468161, 81596420, 81532933, 78383363, 81595906, 81596677, 111745048, 79366936, 113051931, 111871513, 128787214, 79434766, 111871770, 128789270, 75303446, 128786957, 79434509, 128789013, 75303189, 77467413, 128787985, 79435537, 115152394, 33554443, 128786700, 128788499, 33554438, 128788242, 128787728, 128787471, 33554441, 128789527, 33554440, 128788756, 33554439)),
    ((128, 142, 158, 159, 176, 189, 190, 191, 206, 430), 11, (77928708, 78715136, 77601027, 80612609, 81729794, 78584069, 80613637, 80612866, 128853521, 128853264, 113184007, 128854292, 76417044, 128854035, 77532435, 76416787, 128852493, 79500045, 33554440, 128854549, 76417301, 128852750, 114169611, 33554438, 128855063, 76417815, 128853778, 33554441, 128853007, 128854806, 76417558, 128852236, 33554442)),
    ((129, 143, 147, 159, 174, 190, 191, 431), 11, (77600768, 78714884, 79629826, 79567105, 79567362, 79630083, 79630597, 115217176, 80678168, 117251354, 83761690, 82645530, 112003865, 128918286, 79565838, 128919057, 128918543, 128918800, 128917772, 128918029)),
    ((63, 145, 191), 4, (112269848, 73274136, 115217433, 112070426)),
    ((174, 175, 176), 5, (112335129, 81596953, 114169368, 81730840, 105843994)),
    ((101, 177, 191), 3, (115216920, 114166809, 112987418)),
    ((132,), 1, (113052952,)),
    ((188,), 1, (101389080,)),
    ((160, 165, 230), 3, (106630936, 112920090, 115152153)),
    ((187,), 2, (117053976, 79301400, 112854553)),
    ((136, 168), 2, (102175256, 101123609)),
    ((137, 171), 5, (111548952, 76024600, 115875353, 76024345, 101324314, 78252570, 111805979)),
    ((154, 169, 170), 4, (102307352, 78187032, 115940634, 77137690, 110691867, 111740953, 102307613, 111743516)),
    ((43, 58, 82, 152, 168, 170, 171, 182, 187, 190, 218, 442), 9, (102372874, 111741209, 102372617, 111807259, 114891032, 77205784, 33554440, 33554443, 109711900, 114104093, 111744282, 77205274, 33554439, 129640724, 78319124, 129640210, 78318610, 129640467, 129640981, 129641495, 129641238, 33554438)),
    ((59, 106, 107, 115, 117, 119, 123, 138, 170, 171, 172, 173, 181, 189, 219, 443), 11, (79042565, 67833089, 79301124, 79042816, 82515970, 79300867, 78321664, 82516483, 78125313, 78256642, 111740440, 129704718, 129706260, 74123284, 33554442, 33554440, 33554439, 33554443, 129705232, 129704204, 129705746, 33554441, 129707031, 74124055, 78385431, 129706517, 129705489, 129706774, 74123798, 129706003, 129704975, 33554438, 129704461)),
    ((45, 60, 112, 114, 122, 124, 170, 172, 173, 178, 189, 190, 236, 444), 11, (78911489, 81467906, 77928448, 67835139, 78321924, 78452741, 79501569, 79501827, 33554443, 129770768, 80288528, 33554441, 129770254, 80417806, 108793624, 78322200, 33554438, 33554442, 129771025, 33554439, 129771282, 75236882, 78449682, 129771796, 129769740, 129772310, 75237910, 78450710, 129770511, 129771539, 129772053, 78450453, 129772567, 33554440, 129769997)),
    ((139, 141, 145, 149, 156, 157, 159, 172, 173, 174, 179, 188, 191, 204, 219, 253, 445), 11, (78256385, 79566850, 79432453, 79431939, 79431168, 78387204, 129836304, 80483856, 111872283, 112920345, 129835790, 129838103, 76352279, 110823448, 33554441, 33554443, 112920858, 129836561, 80484113, 129837589, 76351765, 129836818, 78515218, 129837846, 76350994, 129837075, 76351251, 129836047, 129837332, 33554438, 129835276, 33554442, 129835533, 33554440, 33554439)),
    ((128, 129, 142, 143, 144, 158, 175, 189, 222, 446), 13, (77666308, 81661699, 81468418, 79632901, 81661185, 78584320, 78453507, 81661442, 114168601, 78513945, 129900812, 77666572, 112068634, 129902097, 79306001, 112986136, 129901583, 80549135, 129903125, 77465877, 78581525, 129903639, 77466391, 129901326, 33554441, 129901069, 33554439, 129902868, 77465620, 129902354, 129901840, 33554438, 129903382, 77466134, 129902611, 77465363, 78581011, 33554443, 33554440, 33554442)),
    ((142, 143, 174, 175, 190, 206, 223, 447), 12, (78780416, 78649602, 80678659, 80678916, 80679173, 78583809, 129966862, 77601550, 113055513, 109970968, 77532184, 115216666, 79498010, 129967119, 80614671, 129967633, 78514961, 129966605, 129966348, 129967376)),
    ((115, 204, 206, 207, 223), 5, (114366745, 82711833, 101453592, 116266524, 116266011, 80611355, 111939610)),
    ((222,), 3, (114628632, 67966488, 116200729)),
    ((3, 207), 2, (100796440, 116266777)),
    ((4,), 1, (100861464,)),
    ((), 0, ()),
    ((85, 86, 153, 206), 3, (100994584, 101256473, 114100762, 100996635)),
    ((7, 171), 3, (101324056, 80353816, 109580057)),
    ((113, 137), 2, (101258264, 113971737)),
    ((24,), 1, (109581848,)),
    ((25, 56, 153, 188, 221), 8, (101519129, 81271065, 116922906, 67702810, 114694168, 76091672, 113972763, 111744540)),
    ((155, 171, 198, 205, 221), 4, (114034201, 101323800, 78252056, 111806746, 111938075, 114035996)),
    ((45, 101, 122, 148, 157, 188, 199, 201, 204, 219, 221, 234, 459), 5, (114956824, 80547608, 33554440, 33554438, 33554441, 130755093, 33554442, 130755607, 33554443, 116200474, 130755350, 130754836, 109774873, 130754579, 33554439, 130754322)),
    ((12, 130, 132, 134, 140, 142, 144, 148, 189, 202, 205, 220, 221, 236, 460), 12, (79697923, 80615429, 67898625, 81467394, 81467652, 67898368, 82450945, 80415493, 80414208, 81598467, 115083800, 130819087, 81468687, 114956555, 130818316, 115084057, 101455113, 33554439, 101454342, 130820886, 76286486, 130820629, 130819601, 130819858, 79498258, 130818830, 130821143, 33554440, 130819344, 130820115, 33554442, 130820372, 130818573)),
    ((47, 61, 129, 131, 133, 157, 161, 186, 190, 197, 203, 206, 207, 220, 221, 223, 237, 461), 11, (82320130, 83499012, 80481029, 80353536, 82582529, 81533187, 80480001, 114825240, 67964440, 33554439, 130884109, 81531661, 33554440, 33554441, 130884623, 101520154, 130885908, 33554442, 130885137, 130883852, 81531404, 33554443, 130886422, 77400598, 112002841, 33554438, 130884366, 130886165, 130885651, 130886679, 130885394, 130884880)),
    ((160, 162, 174, 177, 178, 190, 191, 192, 204, 207, 221, 223, 238, 462), 13, (80026116, 80545537, 82710789, 80680963, 82709761, 82710532, 82710275, 81664000, 81730050, 81730304, 115215129, 130949645, 80550157, 81597197, 101454104, 113253386, 130949902, 130950930, 79629330, 78513682, 130950673, 81730577, 130951187, 130950159, 33554441, 130951701, 78514453, 33554440, 111937562, 33554443, 130950416, 130951958, 78514710, 130952215, 33554439, 130949388, 130951444, 33554438)),
    ((175, 191, 206, 222, 463), 11, (79698179, 79829253, 80746752, 80812033, 80611844, 81726978, 81727492, 81727749, 81726464, 131015695, 81663247, 101521177, 83696665, 131016209, 81663761, 114100504, 131015952, 81663504, 131014924, 131015181, 131015438)),
    ((17, 207, 223), 3, (101717272, 117314331, 117314074, 116265497)),
    ((192, 207), 3, (115281689, 116265752, 83826712)),
    ((19, 223), 2, (101844504, 117315097)),
    ((20,), 1, (101911064,)),
    ((21,), 1, (101975832,)),
    ((193, 219), 2, (115149336, 101389337)),
    ((201,), 1, (102239000,)),
    ((136, 162), 2, (102175512, 115149849)),
    ((201, 205, 233), 3, (115083545, 102503448, 81528856, 110759194)),
    ((9, 170, 186), 3, (102307096, 109647130, 111744793)),
    ((27, 203, 204, 235), 4, (108664600, 101455641, 115086618, 112858651)),
    ((173, 188, 190, 204), 7, (102437912, 80414744, 114628890, 79366170, 115150107, 102438425, 80415257, 113051676, 80419356, 109775133)),
    ((131, 140, 156, 173, 204, 205, 216, 218, 252, 476), 7, (114034969, 101519370, 68949514, 111938328, 131869719, 80548119, 131868691, 77334291, 102504203, 33554439, 33554441, 131869462, 80547862, 131868948, 77334548, 33554438, 131868434, 33554440, 131869205)),
    ((172, 173, 177, 181, 204, 206, 213, 215, 219, 222, 223, 253, 477), 11, (80288003, 80549890, 82647297, 80484356, 80484613, 82647557, 82647808, 113969432, 101390601, 114104839, 131933456, 80354064, 33554440, 33554438, 131932942, 80615950, 131934227, 131932685, 78382861, 131933970, 78448146, 131933713, 131933199, 33554442, 33554443, 131934484, 78448660, 131935255, 131934998, 131932428, 131934741)),
    ((161, 175, 176, 178, 190, 191, 206, 207, 236, 242, 254, 478), 9, (79763460, 81594627, 81729536, 83695874, 80681221, 81594113, 131998735, 79763727, 116263960, 33554443, 132000277, 79563029, 131998221, 83697165, 131999763, 79562515, 131999506, 79562258, 80677906, 131999249, 82646801, 132000020, 79562772, 80678420, 132000791, 79563543, 33554442, 131998478, 33554441, 132000534, 79563286, 33554439, 33554438, 131998992, 131997964, 33554440)),
    ((174, 177, 206, 207, 209, 222, 255, 479), 13, (81861635, 80877828, 80747008, 80747265, 82319874, 82776325, 80615685, 116264474, 80545818, 132064014, 79698702, 107944728, 81593880, 132064785, 115151897, 132064528, 114099739, 132063500, 132064271, 115152668, 113184797, 132063757)),
    ((1, 18, 238, 239), 5, (101779992, 100668185, 116464667, 82385691, 68030747, 101586202)),
    ((2, 17, 62, 223), 7, (100731672, 100731417, 116398362, 67178010, 111155739, 74258203, 116529948, 83368220, 82775836)),
    ((3, 35), 1, (100796953, 100796696, 100799258)),
    ((4,), 1, (100862233, 100861720)),
    ((5, 10, 83), 3, (100927256, 100927513, 107551770, 74060058, 100929563)),
    ((6, 16, 241), 3, (100993560, 107681561, 116197658)),
    ((8, 11), 4, (112531480, 74061080, 67766552, 109580569)),
    ((6, 9, 13, 26, 232), 6, (100992536, 117054233, 83302937, 76092185, 107680794, 101123867, 109647644)),
    ((8, 42, 59, 184, 205, 223, 249), 8, (115809048, 76025112, 110761756, 109710361, 101454875, 82582811, 101193246, 117314586, 82583066, 101189661)),
    ((25, 26, 58, 185, 224, 234), 7, (116792344, 83434264, 76092440, 114825754, 78189338, 109645337, 116198171, 101258013, 101255452)),
    ((10, 43, 171, 204, 251), 5, (107613976, 82385944, 109712411, 101323289, 113968922, 109712668)),
    ((12, 31, 60, 91, 187, 236, 252), 6, (104667929, 67832601, 101387800, 109778716, 101388058, 116197917, 114957083, 78319643, 116196894, 111875359)),
    ((93, 125, 205, 232, 238, 255), 9, (101584922, 82517274, 117312281, 83696410, 110892056, 112989723, 101454620, 114034717, 115214366)),
    ((28, 78, 127, 161, 175, 193, 203, 221, 222, 229, 233, 235, 238, 253, 493), 8, (107680536, 83565336, 101518617, 83630617, 101519642, 33554439, 101518363, 83630875, 114101020, 112006942, 109909021, 33554442, 33554440, 132983317, 33554443, 132983574, 132983831, 33554441, 132982803, 132982546, 132983060, 33554438)),
    ((14, 192, 194, 206, 208, 209, 222, 223, 254, 255, 494), 11, (81795845, 82909699, 69147136, 68029697, 82582020, 68030211, 68029440, 68029954, 82642689, 83695618, 117311000, 133047825, 82648081, 117311769, 133047311, 117378311, 133047568, 117379082, 133048853, 80611605, 133047054, 133046540, 133046797, 101585414, 133049367, 80612119, 33554440, 133049110, 33554443, 133048339, 80611091, 133048596, 33554441, 133048082, 80610834)),
    ((223, 225, 254, 255, 495), 6, (81795587, 83761153, 83761412, 83824130, 83824901, 83823616, 83824387, 116398872, 68095512, 101650202, 101650713, 133112847, 133113361, 83760913, 133113104, 133112333, 133112076, 133112590)),
    ((93, 225, 239, 254), 6, (101717017, 101585690, 110107416, 77337112, 102634523, 83757083)),
    ((1, 18, 32, 224, 238), 3, (101779736, 101778969, 115677722, 69014810, 101783067, 102569756)),
    ((19, 21, 225), 3, (101845528, 101844761, 101976090, 115214619)),
    ((20, 52), 2, (101910808, 100864537)),
    ((5, 21, 25), 4, (100928280, 102237977, 77075225, 110630170, 101976859)),
    ((20, 22, 24), 3, (102172697, 101910040, 102041370, 102041883)),
    ((7, 10, 23, 233), 5, (102107160, 102106649, 107551514, 74059034, 101058587, 108662300)),
    ((24, 231), 3, (102173208, 108597273, 102303514)),
    ((25, 201, 225), 3, (102238744, 77075992, 102241818, 77072922, 117314841)),
    ((9, 16, 41, 233), 6, (108596760, 82320664, 76026904, 110693913, 102303771, 102435610)),
    ((59, 182, 205, 231), 5, (101455384, 110760985, 101388570, 68818714, 108662043)),
    ((22, 43, 44, 92, 237), 5, (108729880, 108728089, 82451481, 111875098, 102434587, 102303260)),
    ((92, 109, 237), 5, (111941400, 115083034, 110890777, 82517785, 102502939, 81528347)),
    ((30, 175, 207, 222, 236, 238), 5, (101520409, 81594393, 102566682, 102568984, 82642968, 115149596, 102569499, 113051165, 113051422, 82645790)),
    ((15, 30, 175, 208, 210, 232, 236, 238, 239, 240, 248, 510), 8, (116398616, 82708248, 101586457, 82709017, 101649414, 69079558, 102635275, 134097686, 81660438, 82776086, 102634761, 134096915, 81659667, 82775315, 134097943, 134096658, 81659410, 82775058, 102634247, 134097172, 82775572, 115215386, 33554440, 134097429, 33554442)),
    ((209, 238, 239, 511), 7, (82778114, 68095233, 68096004, 82581765, 82712576, 82712835, 82778373, 82778627, 134161166, 68031502, 134161937, 68032273, 134160652, 82707980, 134161423, 134160909, 134161680, 115281176)),
)

LEFT, RIGHT0, RIGHT1 = CHUNKS, 2 * CHUNKS, 3 * CHUNKS
SIZE = 384 // CHUNKS
MAX_SENDS = max(len(p[2]) for p in PLAN)
MAX_FROM = max(1, max(len(p[0]) for p in PLAN))
MESH = pl.DeviceIdType.MESH


def nt_dot(left, right):
    return lax.dot_general(left, right, (((1,), (1,)), ((), ())), preferred_element_type=jnp.float32)


def choose(index, low, high, leaf):
    if all(PLAN[i] == PLAN[low] for i in range(low, high)):
        leaf(PLAN[low])
        return
    middle = (low + high) // 2

    @pl.when(index < middle)
    def _():
        choose(index, low, middle, leaf)

    @pl.when(index >= middle)
    def _():
        choose(index, middle, high, leaf)


def kernel(upper_ref, mask_hbm, out_ref, buf, acc, mask_ref, table, origin, count, in_sem, send_sem, recv_sem):
    brow, column = lax.axis_index("brow"), lax.axis_index("bcol")
    row, half = brow // 2, brow % 2
    own = buf.at[pl.ds(0, 384)]
    load = pltpu.make_async_copy(upper_ref, own, in_sem.at[0])
    load.start()
    load_mask = pltpu.make_async_copy(mask_hbm, mask_ref, in_sem.at[1])
    load_mask.start()

    def leaf(plan):
        origins, targets, sends = plan
        count[0] = len(origins)
        count[1] = targets
        count[2] = len(sends)
        for i, v in enumerate(origins):
            origin[i] = v
        for i, v in enumerate(sends):
            table[i] = v

    choose(row * 16 + column, 0, 256, leaf)
    sends = count[2]
    barrier = pltpu.get_barrier_semaphore()

    @pl.loop(0, count[0])
    def _(i):
        v = origin[i]
        there = ((v >> 4) & 15) * 2 + (half ^ (v >> 8))
        pl.semaphore_signal(barrier, inc=1, device_id=(there, v & 15), device_id_type=MESH)

    load_mask.wait()
    load.wait()
    for i in range(3):
        for j in range(6):
            keep = mask_ref[i, j].astype(jnp.float32)
            at = (pl.ds(i * 128, 128), pl.ds(j * 128, 128))
            buf[at] = (buf[at].astype(jnp.float32) * keep).astype(jnp.bfloat16)

    @pl.when(count[1] > 0)
    def _():
        pl.semaphore_wait(barrier, count[1])

    def slot(index):
        return buf.at[pl.ds(pl.multiple_of(index * SIZE, SIZE), SIZE)]

    def copy(v, i):
        there = ((v >> 20) & 15) * 2 + (half ^ ((v >> 24) & 1))
        return pltpu.make_async_remote_copy(
            src_ref=slot(v & 255),
            dst_ref=slot((v >> 8) & 255),
            send_sem=send_sem.at[i],
            recv_sem=recv_sem.at[(v >> 8) & 255],
            device_id=(there, (v >> 16) & 15),
            device_id_type=MESH,
        )

    def arrived(index):
        pltpu.make_async_copy(slot(index), slot(index), recv_sem.at[index]).wait()

    @pl.loop(0, sends)
    def _(i):
        v = table[i]

        @pl.when((v & (1 << 25)) != 0)
        def _():
            arrived(v & 255)

        @pl.when((v & (1 << 26)) != 0)
        def _():
            copy(v, i).start()

    has0 = (row == 0) | ((column >= row) & (row + column >= 16))
    has1 = (column < 15) & ((row <= 1) | ((column + 1 >= row) & (row + column >= 16)))
    here = pl.ds(pl.multiple_of(half * 384, 128), 384)
    other = pl.ds(pl.multiple_of(384 - half * 384, 128), 384)

    def rows(index):
        return buf[pl.ds(pl.multiple_of(index * SIZE, SIZE), 384), :]

    @pl.when(has0)
    def _():
        @pl.loop(0, CHUNKS)
        def _(j):
            arrived(SIB + j)

        right = jnp.where(row + column == 0, 0, RIGHT0)
        acc[:, here] = nt_dot(rows(0), rows(right))
        acc[:, other] = nt_dot(rows(0), rows(SIB))

    @pl.when(has1)
    def _():
        @pl.loop(0, CHUNKS)
        def _(j):
            arrived(SIB + CHUNKS + j)

        left = jnp.where(column == 0, RIGHT1, LEFT)
        for columns, right in ((here, RIGHT1), (other, SIB + CHUNKS)):
            term = nt_dot(rows(left), rows(right))

            @pl.when(has0)
            def _():
                out_ref[:, columns] = (acc[:, columns] + term).astype(jnp.bfloat16)

            @pl.when(jnp.logical_not(has0))
            def _():
                out_ref[:, columns] = term.astype(jnp.bfloat16)

    @pl.when(has0 & jnp.logical_not(has1))
    def _():
        out_ref[...] = acc[...].astype(jnp.bfloat16)

    @pl.when(jnp.logical_not(has0 | has1))
    def _():
        out_ref[...] = jnp.zeros_like(out_ref)

    @pl.loop(0, sends)
    def _(i):
        v = table[i]

        @pl.when((v & (1 << 26)) != 0)
        def _():
            copy(v, i).wait_send()


def per_device(upper_store, block_mask):
    return pl.pallas_call(
        kernel,
        out_shape=jax.ShapeDtypeStruct((384, 768), jnp.bfloat16),
        in_specs=[pl.BlockSpec(memory_space=pl.ANY)] * 2,
        out_specs=pl.BlockSpec(memory_space=pltpu.VMEM),
        scratch_shapes=[
            pltpu.VMEM((SLOTS * SIZE, 768), jnp.bfloat16),
            pltpu.VMEM((384, 768), jnp.float32),
            pltpu.SMEM((3, 6), jnp.int32),
            pltpu.SMEM((MAX_SENDS,), jnp.int32),
            pltpu.SMEM((MAX_FROM,), jnp.int32),
            pltpu.SMEM((3,), jnp.int32),
            pltpu.SemaphoreType.DMA((2,)),
            pltpu.SemaphoreType.DMA((MAX_SENDS,)),
            pltpu.SemaphoreType.DMA((SLOTS,)),
        ],
        compiler_params=pltpu.CompilerParams(
            collective_id=0, has_side_effects=True, vmem_limit_bytes=60 * 2**20
        ),
        name="cannon_steps",
    )(upper_store, block_mask)


def solution(mesh):
    spec = P("brow", "bcol")
    return jax.shard_map(per_device, mesh=mesh, in_specs=(spec, spec), out_specs=spec, check_vma=False)
```

time: 205 us -> 40.9 us (0.20)
  the two profiles are of different devices: /device:TPU:223 before, /device:TPU:353 now
where the time goes in v2:
time: 40.9 us; the launch traced here: 40.8 us
  Pallas kernels  38.8 us (95%)
  local copies, waits for them, and re-layouts  1.92 us (5%)
    pallas_call x1, Pallas kernels, per_device(): pl.pallas_call(kernel, out_shape=jax.ShapeDtypeStruct((384, 768), jnp.bfl...  38.8 us
    unnamed x1, local copies, waits for them, and re-layouts  1.92 us

profile of v2, /device:TPU:353, one launch (start us, length us, event | category | flops | bytes accessed | tf_op | source)
XLA Modules:
  0.0 40.8 jit_solution(7452659400882164605)
XLA Ops:
  0.0 38.8 %cannon_steps.1 = bf16[384,768]{1,0:T(8,128)(2,1)} custom-call(bf16[384,768]{1,0:T(8,128)(2,1)} %upper_ref.1, s32[3,6]{1,0:T(4,128)} %mask_hbm.1), custom_call_target="tpu_custom_call" | custom-call | tf_op jit(solution)/shard_map/cannon_steps/pallas_call | solution.py:420
  38.8 1.9 %copy.4 = bf16[384,768]{1,0:T(8,128)(2,1)} copy(bf16[384,768]{1,0:T(8,128)(2,1)} %cannon_steps.1) | data formatting | bytes 1179648

commit v3 on v0

v3 whole, which is shorter than its diff:
```python
import jax
import jax.numpy as jnp
from jax import lax
from jax.experimental import pallas as pl
from jax.experimental.pallas import tpu as pltpu
from jax.sharding import PartitionSpec as P

CHUNKS = 6
SLOTS = 46
SIB = 34
PLAN = (
    ((1, 10, 14, 16, 17, 18, 19, 31, 224, 240, 241, 256), 6, (83894784, 83895041, 83895298, 83895555, 83895812, 83896069, 102630937, 115808792, 74059032, 103682075, 101717274, 117452055, 103683612, 117451284, 117451798, 103683101, 117451541, 117451027, 117450770)),
    ((2, 3, 13, 15, 17, 18, 33, 48, 65, 225, 227, 257), 12, (68295428, 81795586, 67114757, 68360707, 82843649, 82909696, 117517334, 68225558, 117516049, 68163345, 117516820, 68225044, 117515278, 68162574, 103683353, 117515021, 68162317, 100863514, 117515792, 68163088, 104665112, 117515535, 117516306, 68224530, 117514764, 117517077, 117517591, 117516563, 33554439, 33554440, 33554443, 33554442, 33554441, 33554438)),
    ((3, 18, 19, 32, 34, 50, 51, 130, 194, 226, 258), 7, (81860610, 68294661, 67176193, 81860868, 117580300, 68360460, 81991683, 117580557, 68227853, 81991936, 101845272, 117580814, 68228110, 117581328, 117581071, 68228624, 68228367, 117581585, 117581842, 117582099, 117583127, 117582356, 117582613, 117582870, 33554440, 33554441, 33554438, 33554439, 33554442, 33554443)),
    ((1, 5, 17, 18, 19, 20, 33, 35, 36, 49, 51, 53, 195, 242, 259), 7, (79828996, 68294912, 67241986, 81926149, 68295169, 67242243, 100731928, 101911065, 117647121, 68294417, 117645836, 117648663, 68293132, 117648149, 117647892, 117646607, 68293903, 117648406, 117646093, 117647378, 117646864, 117647635, 117646350, 33554441, 33554442, 33554440, 33554438, 33554443, 33554439)),
    ((5, 19, 21, 23, 54, 66, 68, 84, 86, 96, 164, 180, 226, 228, 260), 8, (79894530, 68360196, 68425731, 82974721, 68426240, 117711886, 70457614, 67442693, 101976344, 102107417, 117712400, 68359696, 117712657, 68359953, 117711372, 117712143, 117713428, 117713171, 117714199, 117713685, 117713942, 117711629, 117712914, 33554443, 33554440, 33554441, 33554439, 33554442, 33554438)),
    ((4, 7, 20, 21, 37, 67, 69, 71, 73, 82, 83, 197, 229, 245, 261), 8, (78911488, 67373829, 81926401, 67373058, 82057732, 67373315, 101910041, 100862744, 117777679, 68424975, 117778193, 68425489, 117777422, 117777165, 68424461, 117778450, 117779735, 117778707, 117779221, 117778964, 117776908, 117779478, 117777936, 33554440, 33554438, 33554441, 33554439, 33554442, 33554443)),
    ((7, 12, 21, 22, 23, 38, 55, 56, 87, 100, 102, 113, 118, 130, 134, 228, 230, 262), 10, (80025600, 69540353, 68491266, 82123523, 102041368, 82123780, 102107930, 83171589, 117843472, 68490768, 117842444, 68489740, 105647385, 67574553, 73077529, 117842958, 117843215, 117844500, 117844757, 117844243, 117845271, 117845014, 117843986, 117842701, 117843729, 33554442, 33554441, 33554443, 33554440, 33554439, 33554438)),
    ((6, 9, 22, 23, 24, 27, 39, 73, 86, 87, 101, 103, 119, 231, 263), 11, (82057472, 69605634, 68556805, 70720257, 67504644, 67504387, 106567960, 102172953, 117909008, 74124568, 68556304, 100995866, 117907980, 68555276, 117909265, 68556561, 117908751, 117910550, 117909522, 101386011, 117910036, 117910293, 117908237, 117910807, 117909779, 117908494, 33554439, 33554443, 33554438, 33554441, 33554440, 33554442)),
    ((10, 23, 24, 25, 40, 42, 70, 89, 104, 120, 136, 166, 232, 248, 264), 13, (82253824, 68622853, 68688129, 69474563, 82254084, 67705091, 105520152, 67700760, 78125570, 68623106, 113842713, 75043864, 68684569, 117974030, 68753678, 78126084, 104406299, 102237978, 68753947, 74059803, 117973773, 68621069, 117975058, 117975829, 117974287, 117975315, 117976086, 117974544, 117975572, 117974801, 117973516, 117976343, 33554441, 33554442, 33554440, 33554438, 33554439, 33554443)),
    ((8, 11, 24, 25, 26, 27, 41, 43, 89, 105, 135, 137, 153, 231, 233, 235, 265), 13, (68753411, 68622594, 81139713, 75041792, 68688388, 83302661, 72947972, 80222469, 69737217, 68688896, 69737733, 107679512, 68815128, 101124377, 102304282, 118039052, 102303259, 102304540, 118039823, 118039566, 68686862, 118040080, 118040594, 118041622, 118040851, 118041879, 118040337, 118041365, 118041108, 118039309, 33554443, 33554441, 33554440, 33554438, 33554439, 33554442)),
    ((11, 26, 27, 42, 168, 170, 186, 187, 196, 200, 202, 230, 236, 266), 11, (82188288, 67115009, 69736451, 67639298, 67835909, 68884483, 82450693, 67640068, 102369048, 104537611, 118105102, 68752398, 118104845, 118107415, 118104588, 68751884, 118105616, 118106130, 118106644, 118106901, 118106387, 118107158, 118105873, 118105359, 33554440, 33554438, 33554439, 33554441, 33554442)),
    ((7, 10, 26, 27, 28, 43, 75, 163, 169, 171, 173, 182, 185, 187, 216, 218, 235, 267), 9, (70719746, 68818945, 67767045, 82450436, 70981888, 68819203, 67766274, 70589188, 67765760, 101255960, 70851075, 82451461, 118170895, 68818191, 118171666, 118171923, 118170638, 118172437, 118172180, 118170381, 118172694, 118170124, 118172951, 118171409, 118171152, 33554438, 33554442, 33554443, 33554441, 33554440, 33554439)),
    ((13, 24, 29, 44, 204, 205, 215, 218, 222, 234, 238, 252, 268), 10, (67508481, 72093186, 68950016, 68884740, 69868035, 68884997, 70982400, 70720517, 102500120, 118236945, 72093700, 102500633, 69016081, 72093957, 118237973, 80480533, 118236688, 118236174, 68883470, 118238230, 118237459, 118238487, 118237202, 118235660, 118236431, 118237716, 118235917, 33554443, 33554439, 33554442, 33554441, 33554440, 33554438)),
    ((15, 28, 29, 43, 45, 192, 193, 203, 205, 207, 219, 221, 222, 223, 237, 269), 14, (71047682, 69015555, 67180548, 68688644, 71109632, 69015809, 69146882, 69998597, 116333080, 67898117, 68880152, 71110917, 102636057, 72159513, 105713690, 68946458, 118302738, 118301453, 68948749, 118301967, 68949263, 118303252, 118301196, 68948492, 118303509, 118302995, 118302481, 118303766, 118304023, 118301710, 118302224, 33554439, 33554442, 33554438, 33554441, 33554440, 33554443)),
    ((15, 16, 30, 31, 46, 224, 238, 239, 240, 252, 255, 270), 9, (70126592, 69146626, 68098305, 70127363, 67115780, 68098820, 70127877, 102631960, 70126849, 102565913, 71244292, 118367760, 69015056, 100670728, 69144072, 70127106, 118367503, 118366989, 118369302, 118367246, 102699018, 118369559, 118369045, 82708757, 118368788, 102698247, 118366732, 82708500, 118368274, 118368017, 118368531, 33554441, 33554438, 33554443)),
    ((14, 17, 28, 30, 31, 225, 239, 241, 255, 271), 11, (69212933, 68163588, 69143552, 70128385, 67180803, 68028418, 104732440, 105714970, 101517081, 68028675, 101517851, 69144323, 118432525, 100733724, 105713181, 118433553, 69080849, 101517342, 118433296, 69080592, 118432268, 118433039, 118432782)),
    ((0, 1, 15, 30, 224, 272), 6, (100670488, 68028952, 105323033, 82909977, 104729882, 71176217, 104729627, 118500631, 118499346, 118499860, 118500117, 118499603, 118500374)),
    ((1, 2, 18, 19, 31, 49, 241, 273), 8, (81795328, 67178757, 67311616, 67177986, 67115523, 67177729, 101653511, 67178500, 103747608, 67178243, 118565139, 100734731, 103682585, 118564882, 118565396, 118565910, 118566167, 118565653, 33554442, 33554440, 33554441, 33554438)),
    ((1, 2, 3, 34, 48, 80, 210, 240, 242, 274), 9, (71374851, 82909189, 68224769, 69278208, 67180036, 67179522, 100731672, 100795929, 100796186, 100668955, 118631446, 67309590, 118630932, 118631703, 118630418, 118630675, 118631189, 33554441, 33554440, 33554442, 33554438, 33554443, 33554439)),
    ((1, 2, 3, 4, 5, 21, 51, 53, 81, 85, 115, 243, 275), 9, (72357892, 80877570, 67246083, 80877824, 82974981, 82975233, 100862488, 101782041, 100668698, 118695954, 118696211, 67374355, 118696982, 118696725, 118697239, 118696468, 33554442, 33554440, 33554439, 33554438, 33554441, 33554443)),
    ((4, 5, 21, 23, 26, 28, 52, 114, 212, 244, 276), 11, (74651653, 67311876, 83040258, 67442944, 68491521, 100862232, 83040515, 100861466, 105191705, 70851609, 102106652, 73142553, 118762518, 108662043, 118761490, 67439634, 67440662, 118762261, 118762775, 118762004, 118761747, 33554439, 33554441, 33554442, 33554438, 33554443, 33554440)),
    ((6, 20, 23, 53, 117, 149, 211, 229, 245, 247, 277), 8, (81008644, 67377155, 68421377, 83105797, 83106304, 83106562, 100993048, 101910297, 118827283, 67505427, 118827540, 118828054, 118828311, 118827026, 118827797, 33554439, 33554442, 33554443, 33554441, 33554440, 33554438)),
    ((4, 6, 7, 20, 38, 54, 86, 116, 228, 246, 278), 8, (80943107, 67508225, 82123013, 68622340, 83171330, 83302912, 101059352, 118892819, 67570963, 118893076, 67571220, 118893590, 118892562, 118893847, 118893333, 33554443, 33554441, 33554439, 33554438, 33554440, 33554442)),
    ((7, 8, 9, 22, 24, 25, 55, 57, 151, 166, 213, 247, 249, 279), 13, (82057218, 67377411, 69605380, 67508741, 83236865, 68426752, 102042136, 111548697, 67635225, 75042329, 101124890, 80222746, 101124123, 118959383, 118958098, 118958869, 118958612, 118958355, 118959126, 33554439, 33554441, 33554442, 33554443, 33554440, 33554438)),
    ((8, 9, 13, 28, 40, 56, 120, 152, 214, 233, 246, 280), 13, (67574019, 83302405, 70850564, 83433986, 68617985, 83434240, 114825753, 67569433, 101190170, 105649691, 67897883, 107681304, 101189148, 73142296, 119023891, 67702035, 119023634, 119024919, 119024662, 119024405, 119024148, 33554443, 33554439, 33554441, 33554440, 33554438, 33554442)),
    ((8, 9, 10, 26, 187, 200, 215, 245, 249, 281), 11, (80156672, 72882180, 67639557, 80287747, 69736707, 67639809, 80288002, 69802497, 116791832, 67635480, 75042584, 83237122, 103357191, 102175769, 101255706, 119090198, 119089684, 119090455, 119089427, 119089941, 119089170, 33554442, 33554438, 33554443, 33554440, 33554441)),
    ((9, 10, 11, 42, 58, 60, 182, 185, 202, 216, 218, 282), 12, (83106050, 71702532, 68749057, 80878080, 70785285, 68426497, 83368195, 67705348, 105520408, 67766040, 67705600, 101320985, 67705861, 119155734, 67833878, 119154963, 119155477, 119155220, 119155991, 119154706, 33554439, 33554441, 33554440, 33554438, 33554443, 33554442)),
    ((10, 12, 13, 28, 29, 57, 59, 61, 203, 211, 219, 221, 283), 9, (70719488, 67573761, 67770369, 70916357, 67704835, 71113476, 69540866, 101255448, 70916866, 101386777, 101387034, 119221270, 119220499, 119221013, 119220242, 119221527, 119220756, 33554442, 33554439, 33554441, 33554440, 33554438, 33554443)),
    ((12, 13, 29, 30, 220, 252, 284), 13, (68425989, 70653955, 67966977, 68687876, 69081089, 70916096, 68880900, 69868290, 101653768, 71178760, 101385752, 106697222, 119286806, 67964950, 119286035, 119286292, 119286549, 119287063, 119285778, 33554439, 33554441, 33554442, 33554443)),
    ((12, 13, 14, 30, 59, 235, 236, 241, 253, 255, 285), 10, (68945922, 81861120, 70064131, 67901441, 67967237, 72158465, 67901699, 67967492, 68945408, 103553304, 103553817, 67897113, 71110424, 71109913, 102438682, 119352085, 119351314, 119351571, 119352342, 119352599, 119351828, 33554438, 33554441, 33554440, 33554442, 33554443, 33554439)),
    ((0, 13, 14, 15, 28, 47, 62, 239, 240, 254, 286), 11, (69540101, 82122753, 68032770, 68098563, 69010944, 71175682, 68163844, 81992192, 69011715, 68164097, 71175939, 68164352, 106695960, 101586713, 104732170, 104731142, 102501146, 119417107, 119417621, 119417364, 119418135, 119417878, 119416850, 33554439, 33554441, 33554443, 33554440)),
    ((13, 14, 15, 46, 287), 9, (77666306, 67115264, 70129667, 68098053, 68032516, 68229124, 70192385, 70192128, 104666136, 119480844, 68229388, 68099608, 68027916, 104664601, 119481615, 119481358, 119481872, 119482129, 119481101)),
    ((15, 34, 35, 76), 4, (100797976, 100798233, 100798746, 70327066, 103683867, 100799260, 107876381)),
    ((18, 51, 52, 63), 4, (100865816, 100863769, 100733466, 105913371, 72289307)),
    ((35, 51), 4, (69212162, 70391812, 67243008, 69212419, 67243265, 69212677, 101848600, 100800281)),
    ((51, 52, 62), 7, (100864280, 75634947, 69213185, 69343493, 70392320, 70457858, 100865561, 70392580, 100864538, 100864795, 107812124)),
    ((8, 45, 52, 59, 62), 5, (100865304, 110760730, 109580057, 107746331, 104663324)),
    ((6, 27, 30, 85, 86), 5, (100995352, 103815961, 70983449, 72161049, 100996379, 107679260, 100992794)),
    ((7, 23, 42, 55), 5, (102107672, 106503194, 101058585, 76156698, 107615259)),
    ((59, 60, 119, 120), 2, (101126424, 109775898, 109778459, 101126937)),
    ((9, 10, 25, 42, 134, 136), 5, (107613976, 102238489, 109711386, 101189403, 101191708, 77141530, 101190429, 101193502)),
    ((25, 153, 154), 9, (70326533, 83433475, 70588929, 81336320, 77139458, 70589700, 104340248, 67702552, 110629658, 76090650, 101259033, 109646619)),
    ((12, 28, 43, 55, 60, 136, 171), 14, (82581509, 69605891, 76156418, 82319360, 69736964, 78256385, 109712921, 103488282, 72093466, 103488539, 101191452, 73141787, 70983707, 101323544, 108793885, 102368798)),
    ((42, 46, 61, 154), 12, (82450944, 69867780, 75174149, 70850817, 83564803, 72161538, 107810328, 101258777, 101516826, 106632475, 67832091, 107680796)),
    ((13, 29, 60, 61), 8, (81795073, 70588672, 71047171, 70981637, 71112706, 71964676, 105649944, 101452057, 72095001, 101451802, 105648923, 101451292, 72094236)),
    ((29, 46, 62, 125), 12, (81926656, 69475074, 73144581, 70982146, 71113728, 73207812, 70982915, 70392835, 73207041, 105713432, 104406554, 112004121, 74256922, 101517595, 71111963, 101518108)),
    ((0, 1, 14, 15, 17, 31, 32, 60, 62, 63, 64, 74, 78, 108, 302), 12, (70326787, 71113217, 72224772, 72223744, 120463884, 69933580, 104731928, 72225029, 71244556, 120464655, 70064911, 111939097, 104728346, 72224258, 120465169, 70065169, 71179025, 120465683, 68028179, 120464141, 71111437, 111808795, 105780746, 71241738, 120464398, 105779718, 120466711, 69144855, 71240710, 105779975, 68029207, 120466197, 120464912, 120466454, 120465426, 120465940, 33554440, 33554441, 33554443)),
    ((17, 31, 62, 63, 303), 8, (71309314, 71047425, 71241475, 71178244, 71241989, 71178496, 71240961, 105843992, 120529677, 69076749, 71176973, 120529420, 105714713, 120530448, 120530705, 120530191, 120529934)),
    ((37, 51, 60, 62, 63), 6, (100735512, 68293656, 111483161, 75238937, 106826778, 104730907, 106827804)),
    ((32, 41, 46, 51, 64, 65), 7, (116398360, 67308824, 104864538, 101783323, 73209114, 110694681, 101779740, 104795677)),
    ((34, 35, 45, 63), 3, (100798488, 100799002, 106829337, 100800027, 107746588)),
    ((4, 35, 52), 9, (70260738, 69343236, 70588416, 69408773, 70326273, 69277955, 100865048, 100799514, 101913625)),
    ((67, 85), 5, (69277701, 69474307, 70457346, 69409028, 69409280, 69409537, 101979672, 101979161)),
    ((11, 41, 44, 51, 84, 87), 6, (100863000, 108728857, 110693658, 101913884, 106631195, 102044958, 110694429)),
    ((28, 58, 69, 101), 7, (107420440, 70851352, 110565914, 73142040, 100930073, 77204506, 102110491)),
    ((7, 11, 12, 27, 136), 6, (103423512, 74124312, 103160601, 73076249, 101058331, 106632988, 102176026)),
    ((26, 41, 103, 153), 4, (101062424, 102240794, 107552025, 102241563, 75108633)),
    ((8, 11, 20, 24, 43, 45, 54), 7, (102173208, 108727577, 107615514, 73076506, 102435099, 108598813, 104662558, 102435612)),
    ((27, 28, 61), 10, (79305475, 72882433, 70654464, 83368452, 79305989, 104668440, 79306242, 108664601, 71048473, 108795674, 73141272, 102369307, 75109403, 102369820)),
    ((10, 11, 12, 37, 42, 44, 45, 62), 11, (82515972, 71965443, 69474817, 83433730, 69671424, 82516997, 108730136, 106630169, 106631707, 106762013, 106761754, 104662812, 102566687, 106631454, 102434848)),
    ((13, 44, 47, 58, 61, 74), 12, (70260994, 75238657, 81402115, 107745048, 75239685, 69671684, 103679769, 79436800, 69868804, 103553562, 72094746, 111807515, 108795420, 102370077)),
    ((1, 13, 27, 29, 31, 36, 44, 45, 46, 57, 58, 59, 62, 63, 91, 109, 317), 13, (70916613, 82582272, 72161793, 71048196, 69933058, 108729368, 74256131, 111873305, 106763034, 104471579, 74125339, 121446924, 69999628, 106761244, 121448980, 121448209, 107680285, 68879901, 121447695, 121447438, 121448723, 121447181, 121447952, 121449494, 121448466, 121449237, 121449751, 33554442, 33554440, 33554441, 33554439, 33554438, 33554443)),
    ((15, 16, 28, 30, 46, 47, 48, 79, 94, 161, 318), 15, (71243780, 82647301, 70064640, 73272577, 71244034, 69475331, 70982657, 73272834, 103680536, 80550148, 69409795, 121512974, 70195470, 73273605, 103679513, 70261248, 121513231, 73273091, 121514773, 69077269, 121515287, 70193431, 106697754, 69077783, 70192917, 121514259, 121512717, 104666907, 121514516, 69077012, 70192660, 121513488, 121512460, 121515030, 121514002, 121513745, 33554439, 33554441, 33554440, 33554443, 33554438, 33554442)),
    ((14, 46, 47, 49, 62, 319), 10, (69278464, 72227074, 70195201, 70392068, 70130177, 72290565, 73274627, 121578767, 72226063, 72290051, 121579281, 72226577, 103816216, 71109144, 121578253, 104663065, 104666650, 104665627, 121579024, 121577996, 121578510)),
    ((47, 49, 79), 7, (103882008, 72225816, 70125592, 108075801, 72222233, 74322457, 109843994, 72092186, 105778971)),
    ((18, 92), 4, (103881752, 67179800, 111024409, 78320409)),
    ((68, 69, 74, 76, 79), 7, (100929816, 100931097, 111808282, 110566171, 106109724, 72222748, 76288283, 74322972)),
    ((85, 86, 94), 4, (104077592, 67440152, 108337945, 76354329, 100996122)),
    ((69,), 6, (72423425, 67374594, 72620036, 73406464, 72685568, 71440389, 72620291, 100930584, 100930841)),
    ((20, 85), 7, (71440644, 77862913, 70654208, 72751365, 71571458, 100994840, 71571715, 107681561)),
    ((26, 74, 137), 3, (108662808, 111808538, 101193241, 111808027)),
    ((16, 75, 86, 93), 4, (100995609, 109906968, 111875099, 105715226)),
    ((77,), 1, (109843480,)),
    ((86, 92, 120), 4, (100996632, 106437145, 78320153, 101127962)),
    ((8, 26, 44, 59, 91, 93, 123), 12, (71440899, 71047936, 78253313, 71703044, 70130437, 71703298, 106633752, 74190872, 106694169, 110761243, 108661530, 107613724, 105645598, 106630429, 74060573)),
    ((76, 91, 92), 8, (83564544, 72817154, 77271301, 72620804, 77270787, 72817412, 105323288, 73074712, 77270273, 111873817, 106628634, 106629403, 106629660, 101386269, 73077789)),
    ((6, 12, 24, 42, 44, 60, 64, 74, 78, 91, 92, 93, 100, 108, 125, 332), 12, (71441157, 73078784, 76287490, 82712579, 72948227, 76287233, 102767896, 75306520, 76288004, 106695193, 122430478, 72031502, 77338137, 106694682, 122430992, 73078288, 122431249, 122432020, 107744027, 122430735, 107746844, 122432534, 122430221, 122432791, 122432277, 122431763, 122431506, 122429964, 33554440, 33554443, 33554442, 33554438, 33554439, 33554441)),
    ((13, 15, 29, 37, 43, 45, 47, 61, 71, 78, 79, 94, 125, 225, 227, 229, 333), 10, (75304707, 72292356, 71833602, 73209861, 73144322, 75304193, 73079040, 105847576, 73206552, 122495757, 73143053, 108727833, 106568218, 74255642, 122496271, 73143567, 122496785, 73144081, 122497813, 122498327, 122496528, 73143824, 107811611, 122495500, 122497299, 122497042, 122497556, 122496014, 122498070, 33554442, 33554439, 33554441, 33554440, 33554438, 33554443)),
    ((46, 63, 64, 66, 93, 94, 95, 110, 334), 13, (72095748, 72554757, 74320896, 72292609, 72157700, 72423939, 74321410, 73275395, 74322181, 73275650, 106760472, 75370264, 74321153, 106828825, 108925210, 122562064, 73341200, 105913627, 73271579, 122561036, 73341452, 122562321, 73209617, 122561550, 73208846, 122563349, 70125845, 122563092, 122563863, 70126359, 107878155, 122563606, 122562578, 122561807, 122561293, 122562835, 33554438, 33554440, 33554441, 33554439, 33554442)),
    ((33, 47, 63, 77, 78, 94, 95, 335), 12, (71309568, 75372547, 73338113, 71441410, 73338884, 104864280, 75304984, 73339141, 105711385, 75305753, 73338627, 122627857, 73275153, 107941146, 73271066, 122626829, 73274125, 109909787, 122627343, 122626572, 71173644, 107811868, 122627086, 122627600)),
    ((19, 33, 78, 92, 95), 5, (101845528, 108925465, 106826523, 110891290, 106828316, 107941661, 75371805)),
    ((68, 78, 94), 4, (101913368, 109386009, 73205785, 108860698)),
    ((86, 93), 2, (110892824, 100996890, 110892057)),
    ((66, 78, 85, 94), 4, (100994328, 108861209, 109909274, 106892827)),
    ((68, 75, 91), 4, (100929560, 104143897, 67374873, 112858138, 111810075)),
    ((68,), 7, (74586112, 71505922, 70522884, 71636995, 72554497, 69539845, 101913112)),
    ((69, 91, 119), 10, (72489477, 69540611, 71899140, 71768320, 102109976, 71506434, 67574273, 100931353, 111613978, 79304474)),
    ((75, 102, 120), 5, (104144408, 67505944, 101127193, 109451802, 77270554, 110825499)),
    ((25, 58, 73), 4, (110630424, 115939865, 77204761, 110890010)),
    ((9, 38, 76, 137, 154), 5, (108597273, 101192475, 110826778, 101258520, 110695708)),
    ((7, 77, 123), 2, (108661016, 108663577, 108794650)),
    ((6, 43, 53, 55, 57, 59, 74, 75, 76, 77, 93, 95, 347), 13, (72620546, 71112961, 72030467, 76225284, 72751621, 82516480, 110826008, 105520665, 74062105, 75303961, 108729882, 123413004, 74060300, 123414546, 72092690, 123413518, 123414803, 123415574, 123415831, 123415060, 123413261, 123414032, 123414289, 123415317, 123413775, 33554440, 33554439, 33554443, 33554438, 33554441, 33554442)),
    ((20, 24, 28, 30, 42, 45, 54, 58, 62, 74, 76, 77, 93, 124, 156, 348), 12, (72030210, 71375105, 82123267, 77336580, 73210113, 71899392, 73340933, 83630850, 72030720, 72358405, 105646104, 72030979, 77336323, 72031236, 106896153, 74192665, 110891526, 123480339, 123478797, 123479311, 123480082, 123479054, 123478540, 123480853, 123480596, 123479825, 123481367, 123479568, 123481110, 33554439, 33554442, 33554440, 33554441, 33554443)),
    ((45, 49, 59, 61, 77, 78, 81, 92, 95, 117, 124, 141, 349), 11, (72488965, 71964928, 74258435, 72096004, 73139969, 72489218, 71768064, 74258945, 72096258, 105646872, 106628889, 75305240, 123545104, 72096784, 123544333, 74191629, 123545875, 72224019, 123546389, 123544076, 123546903, 123544847, 123546132, 123544590, 123546646, 123545618, 123545361, 33554441, 33554443, 33554440, 33554438, 33554442, 33554439)),
    ((48, 50, 62, 63, 78, 79, 80, 95, 111, 126, 350), 11, (72423682, 73472000, 72161285, 72226819, 71506177, 75370500, 72227333, 75369472, 72555011, 75369729, 105711896, 74321688, 123609869, 72162061, 123610126, 72293390, 123610897, 123611925, 71174421, 105711641, 123610383, 123611668, 71174164, 72289812, 123612439, 71174935, 123612182, 71174678, 72290326, 108926474, 123611411, 123609612, 123611154, 123610640, 33554440, 33554441, 33554439, 33554443, 33554438)),
    ((78, 79, 83, 92, 113, 351), 10, (72227587, 74387460, 72358144, 72292865, 74387717, 72358661, 74386946, 123675405, 74322701, 73271298, 123676176, 74323472, 116072728, 73075480, 123676433, 72223505, 123675919, 106763801, 106762778, 106762523, 123675148, 123675662)),
    ((68, 125, 143), 3, (100928536, 112071961, 109843738)),
    ((94, 110), 2, (109908504, 107808281)),
    ((109,), 1, (111941400,)),
    ((126,), 1, (109909528,)),
    ((103, 108, 115, 125, 140), 5, (112924440, 101061145, 114036250, 105646363, 107611932)),
    ((108, 119, 120, 122, 124, 126), 6, (104209176, 67571480, 101127705, 110237978, 107677211, 80417562, 112005660, 113972765)),
    ((103,), 5, (74782721, 76879877, 72816643, 74782978, 75896834, 67506180, 67505152, 101061656)),
    ((54, 119, 120), 8, (74520580, 75634689, 70785029, 73799682, 74848259, 73668864, 101125144, 101126681, 101127450, 107681051)),
    ((109, 121, 123, 136), 4, (101190936, 109714457, 74188825, 109580826, 109713179)),
    ((56, 108, 122, 139, 214), 5, (112923672, 74123288, 108595993, 108595738, 101258267, 108596508, 109647645)),
    ((0, 8, 38, 40, 57, 74, 91, 100, 107, 122, 123, 124, 187, 230, 234, 362), 5, (124396815, 75044111, 111939352, 124397329, 75044625, 79369496, 124396301, 124398614, 75043597, 124396044, 109842969, 124397072, 124398871, 124396558, 124398357, 124397843, 124398100, 124397586, 33554441, 33554440, 33554438, 33554442, 33554443, 33554439)),
    ((7, 9, 24, 37, 43, 55, 61, 69, 101, 103, 105, 108, 122, 124, 125, 239, 363), 9, (74651905, 79367168, 75175938, 75110916, 79367939, 74783236, 75176709, 74057987, 108792344, 78450712, 124461580, 75108876, 124462351, 75109647, 108727065, 124461837, 124462608, 75109904, 124462094, 124464150, 124463379, 124463893, 124462865, 124463636, 124464407, 124463122, 33554439, 33554443, 33554442, 33554440, 33554441, 33554438)),
    ((36, 50, 60, 74, 76, 92, 93, 104, 123, 124, 125, 172, 224, 226, 236, 364), 12, (73668613, 75241475, 78385156, 70129922, 73996290, 73734912, 74123009, 74124037, 76159488, 74123780, 108726296, 108791833, 78384385, 108792090, 124528144, 124527887, 75175183, 105645851, 76288795, 124529943, 124527373, 124528915, 124528401, 124529172, 124527630, 124529429, 124528658, 124529686, 124527116, 33554438, 33554440, 33554439, 33554443, 33554441, 33554442)),
    ((35, 43, 45, 61, 77, 79, 93, 97, 111, 124, 126, 127, 157, 205, 237, 365), 15, (74717444, 73931010, 79501827, 82582017, 75307013, 75241728, 73537541, 75045122, 108796440, 76353304, 75307520, 116071961, 75172121, 109907226, 75307780, 124593423, 75240719, 109777691, 109778716, 124592909, 124595479, 71109399, 124593166, 75240462, 110957576, 124594194, 124595222, 124594965, 124594451, 124593937, 124594708, 124592652, 124593680, 33554441, 33554438, 33554439, 33554443, 33554442)),
    ((32, 64, 66, 78, 94, 95, 111, 126, 127, 142, 366), 9, (74389762, 76419333, 75438081, 83695619, 75372803, 76419076, 124658188, 75305484, 73472256, 76418048, 124658702, 75438350, 108927495, 76418305, 124659473, 108857112, 76418562, 124658445, 108990474, 108857625, 76420618, 124660501, 72222997, 124659987, 124658959, 72222483, 124660758, 124659730, 72223254, 109974022, 108990731, 124660244, 124659216, 124661015, 33554440, 33554441)),
    ((79, 80, 95, 110, 126, 127, 367), 10, (74520835, 74319617, 76420869, 75435522, 75435008, 74320388, 111023896, 75435265, 124724752, 73271824, 112006682, 107808793, 124725009, 75372305, 112005915, 124724238, 75371534, 77466907, 124723981, 75371277, 124724495, 124723724)),
    ((125,), 1, (112989976, 112988953)),
    ((64, 103, 111, 126), 6, (101062168, 109974809, 110107162, 75303450, 75435801, 106892315)),
    ((85,), 1, (101978648,)),
    ((20, 107), 3, (101911320, 107224089, 79367449)),
    ((109, 119), 2, (102110232, 111941145)),
    ((67, 102, 107), 3, (102044440, 102044697, 112922650, 106759963)),
    ((103,), 1, (101061912,)),
    ((), 6, (74717186, 72751105, 73865216, 73734147, 69670917, 67571716)),
    ((123, 137, 153, 155), 11, (73734404, 72816898, 73865472, 69671169, 73865731, 71899653, 108660761, 101192730, 102241819, 76023834, 110757400, 77072923)),
    ((8, 9, 23, 25, 57, 89, 105, 106, 109, 122, 123, 125, 179, 247, 377), 5, (125379084, 73931276, 112004632, 110956057, 125379855, 125381140, 125379598, 125380112, 76027408, 125380369, 125381397, 125381911, 125379341, 125380883, 125381654, 125380626, 33554440, 33554441, 33554438, 33554443, 33554442, 33554439)),
    ((20, 56, 58, 70, 74, 90, 107, 120, 123, 124, 210, 244, 248, 378), 11, (73996549, 75176192, 73996804, 75176449, 75040770, 112924952, 73735448, 75041027, 112987161, 75171353, 113973019, 107612698, 74127643, 79433752, 79434011, 125447447, 125445648, 76092944, 74125591, 125445391, 125445134, 125446676, 125444620, 125446162, 125446419, 125444877, 125446933, 125445905, 125447190, 33554442, 33554438, 33554439, 33554440, 33554443, 33554441)),
    ((43, 53, 57, 59, 61, 77, 91, 107, 108, 109, 122, 125, 138, 183, 187, 251, 379), 11, (71965189, 74979586, 75106820, 73013251, 75105792, 75106049, 107612184, 79367704, 108594713, 125511441, 73931537, 112922907, 108594970, 74058523, 125512983, 74191127, 125512212, 74190356, 125511698, 74189842, 125510670, 76157966, 125510413, 76157709, 125512726, 125510927, 125512469, 125511184, 125511955, 125510156, 33554441, 33554440, 33554438, 33554439, 33554443, 33554442)),
    ((42, 48, 58, 60, 90, 107, 108, 109, 125, 126, 188, 218, 236, 380), 11, (73734657, 75110404, 74258691, 79433218, 74192898, 75110656, 75307265, 75111173, 79433475, 107616280, 74123544, 107742745, 125575949, 74259213, 125576977, 74259473, 106694938, 112989192, 106760731, 112989706, 125578519, 74256663, 125578262, 125576206, 125577234, 74256406, 125578005, 125575692, 125576463, 125576720, 125577491, 125577748, 33554438, 33554441, 33554443, 33554439)),
    ((76, 77, 79, 81, 83, 91, 93, 109, 110, 113, 124, 126, 127, 140, 159, 253, 381), 15, (74455045, 70064384, 74127364, 74193154, 76355843, 74455297, 75044866, 74193411, 75236864, 125641999, 73669391, 73406991, 105650968, 77402392, 108726041, 125641485, 74193677, 109846042, 77401114, 125643798, 125642256, 110956571, 125642770, 72156690, 125642513, 125644055, 125643027, 76289809, 72157975, 110957340, 125641228, 125643541, 74189339, 125643284, 125641742, 33554438, 33554439, 33554441, 33554442, 33554440, 33554443)),
    ((78, 79, 80, 94, 110, 111, 133, 143, 158, 382), 13, (77467138, 82647813, 74323969, 74390020, 75302400, 74521092, 77467395, 74324227, 73735168, 77467909, 125707792, 73603088, 75242256, 74390273, 107877656, 77466624, 125706764, 107809049, 76418841, 125707021, 125707535, 109974298, 125708049, 125709591, 125708306, 73270802, 74386450, 125708820, 125708563, 125709077, 125707278, 125709334, 33554442, 33554438, 33554443, 33554439, 33554441, 33554440)),
    ((110, 111, 113, 383), 9, (83826946, 74389509, 76421121, 76421635, 77469188, 77468160, 125772814, 76420110, 76483584, 108862488, 125772300, 74319372, 74254104, 125772557, 108860441, 125773071, 125773328, 125773585)),
    ((140, 143, 159), 4, (113120793, 109971224, 114036506, 111020827)),
    ((159,), 2, (113119768, 78580760)),
    ((35, 103), 2, (101061400, 100799769)),
    ((132, 158, 159), 4, (110237720, 78581528, 112006425, 109775386)),
    ((140,), 2, (109255192, 80482328, 114035737)),
    ((81, 158), 3, (114103576, 108924441, 76354585)),
    ((87, 102, 137), 4, (101060120, 103292441, 76024601, 111809562)),
    ((153, 154, 157), 4, (101257241, 110565656, 67703320, 110499866, 80547354)),
    ((36, 104, 120, 121, 134, 137, 153, 166, 168, 184, 200, 214, 216, 246, 392), 10, (67636738, 73930753, 77010949, 81074180, 70720003, 77993984, 69868547, 69737476, 101192969, 110627608, 110627097, 110626330, 126362638, 126363923, 126363152, 126362895, 126364951, 126363666, 126364180, 126362381, 126363409, 126364694, 126362124, 126364437, 33554442, 33554439, 33554443, 33554438, 33554440)),
    ((41, 105, 122, 138, 139, 152, 153, 154, 199, 201, 210, 244, 248, 393), 11, (75897093, 71702788, 83367936, 76024067, 74979842, 79173632, 76024324, 72948481, 76023553, 110692120, 67703576, 110692633, 126427660, 77074956, 126428431, 126429973, 126428174, 126427917, 126429716, 126429202, 126429459, 126428945, 126430230, 126430487, 126428688, 33554438, 33554443, 33554441, 33554442, 33554439, 33554440)),
    ((38, 40, 42, 104, 108, 123, 139, 154, 155, 156, 157, 170, 232, 234, 236, 394), 9, (77142021, 76224771, 77142276, 76225537, 77142530, 110758680, 76088832, 110757657, 126493710, 77141006, 111938586, 79368730, 109841179, 126495766, 75173910, 126494481, 77141777, 126494738, 75172882, 111940636, 126493453, 126494224, 126493196, 126493967, 126495252, 126495509, 126496023, 126494995, 33554442, 33554439, 33554443, 33554438, 33554440, 33554441)),
    ((39, 91, 109, 131, 138, 140, 141, 154, 155, 156, 165, 171, 203, 235, 249, 395), 9, (77338880, 76155396, 76154625, 77207554, 76155653, 107551512, 77137944, 113053210, 77207811, 109644057, 109643548, 111874075, 126559760, 126559246, 77206542, 126558732, 77206028, 126560017, 126561302, 126560531, 126559503, 126561559, 126561045, 126560788, 126560274, 126558989, 33554443, 33554440, 33554438, 33554441, 33554439, 33554442)),
    ((64, 66, 72, 76, 96, 106, 108, 125, 138, 142, 155, 156, 157, 172, 187, 238, 396), 15, (75765764, 73669122, 77339137, 77273347, 80482565, 75766016, 77339394, 76221189, 75504131, 76356352, 110823704, 110889754, 81532698, 126624782, 77405454, 110823195, 110888732, 113055001, 126624525, 78515993, 110889245, 77405965, 114038025, 126625296, 77272592, 126626324, 75304468, 111940126, 126625039, 126625553, 126627095, 126626838, 126626067, 126624268, 126626581, 126625810, 33554442, 33554440, 33554443, 33554439, 33554438)),
    ((67, 71, 79, 83, 97, 99, 109, 125, 133, 140, 143, 145, 156, 157, 158, 189, 397), 11, (76814341, 76225026, 79498240, 77338627, 77404165, 76552448, 77404420, 79498497, 77339650, 77404931, 110822936, 114102298, 77335066, 112004889, 109774363, 126690575, 126691346, 73205266, 77337871, 109774620, 126690061, 77337357, 113054471, 113054728, 126691603, 126689804, 126692631, 126692117, 126692374, 126691089, 126691860, 126690318, 126690832, 33554438, 33554443, 33554442, 33554441)),
    ((110, 111, 113, 126, 127, 128, 158, 159, 160, 174, 398), 11, (76617989, 76290307, 77469697, 77535236, 79499776, 76487426, 78515457, 78515200, 111090201, 78515714, 79565081, 111022872, 126756625, 77403921, 111023386, 126756368, 77403664, 126758167, 74320663, 126755340, 77536268, 126755597, 112072202, 126755854, 126757396, 74319892, 126756111, 112071431, 77532423, 126757653, 74320149, 126757910, 126757139, 126756882, 33554438, 33554440, 33554443, 33554441)),
    ((127, 142, 157, 158, 159, 255, 399), 13, (76617733, 73406723, 77600768, 77533188, 75503617, 79567362, 77532160, 112136472, 77532931, 110955033, 77532674, 114101274, 109905947, 126820876, 126821390, 75368462, 77468686, 126821904, 126822161, 126821133, 126821647)),
    ((113, 141, 157), 3, (114037273, 110888472, 111022106)),
    ((142, 143, 158), 7, (111155992, 77533464, 112070937, 77405721, 114104090, 76352281, 112006171)),
    ((101, 131), 3, (113120536, 77465880, 112987417)),
    ((158,), 1, (114103320,)),
    ((141,), 1, (114038552,)),
    ((102,), 2, (115743256, 68491032)),
    ((135,), 1, (115086360,)),
    ((54, 66, 135, 136), 5, (115874072, 68622104, 111743514, 110827291, 110691865)),
    ((41, 88, 120, 136, 137, 153, 157, 184, 201, 212, 408), 4, (102241031, 110888984, 127413270, 68684310, 76091414, 127412499, 127412242, 127413527, 127412756, 127413013, 33554440, 33554443, 33554441, 33554442, 33554438)),
    ((40, 41, 49, 53, 89, 137, 138, 139, 151, 155, 185, 217, 249, 409), 10, (69801987, 77072129, 82384898, 75962628, 70785536, 77072386, 82385157, 74980100, 67701760, 109644568, 76027909, 109644313, 76028163, 109643802, 76028416, 127476750, 127478292, 127476493, 127477007, 127476236, 127477521, 127478806, 127478549, 127477264, 127479063, 127477778, 127478035, 33554440, 33554443, 33554439, 33554442, 33554441, 33554438)),
    ((36, 54, 74, 88, 120, 138, 139, 155, 156, 186, 248, 252, 410), 9, (76224514, 75962368, 72947715, 77273093, 76093441, 69802245, 77273604, 76093699, 69933316, 109709336, 109709593, 127544085, 76222229, 127542543, 127542029, 127543571, 76221715, 127542286, 127542800, 127543057, 127544342, 127541772, 127543828, 127543314, 127544599, 33554441, 33554442, 33554443, 33554439, 33554440, 33554438)),
    ((75, 87, 89, 91, 140, 141, 151, 154, 156, 157, 251, 411), 9, (74979328, 79304962, 76158981, 77203715, 76159233, 77203972, 110693144, 110692890, 127608593, 109775129, 78255889, 127608079, 78255375, 127607565, 78254861, 127608850, 76286994, 127607822, 127609364, 127609878, 127607308, 127609621, 127608336, 127609107, 127610135, 33554442, 33554441, 33554439, 33554438, 33554443, 33554440)),
    ((76, 80, 82, 88, 92, 139, 140, 141, 144, 152, 158, 235, 252, 412), 11, (76290051, 76355584, 77269508, 76290817, 77404677, 109840664, 77405186, 109911066, 80481562, 127673872, 109708825, 78453520, 109774875, 109840412, 127673615, 127675671, 73141015, 76353815, 127675414, 127674900, 76353044, 110761757, 76353558, 127673358, 127674129, 127675157, 127674643, 127673101, 127674386, 127672844, 33554443, 33554442, 33554439, 33554440, 33554441, 33554438)),
    ((109, 121, 125, 140, 141, 142, 143, 145, 156, 159, 189, 191, 205, 219, 236, 253, 413), 12, (75962882, 76552192, 76290565, 76356100, 80547587, 77076482, 76487168, 76291073, 80547073, 76291331, 109714200, 79499544, 113053721, 76286489, 113053467, 110824218, 110823452, 110826525, 127739665, 127741207, 74255127, 127739151, 127740950, 74254870, 113055518, 110826271, 127738380, 127738894, 127740693, 127739408, 127738637, 127740179, 127740436, 127739922, 33554442, 33554441, 33554443, 33554438, 33554439, 33554440)),
    ((65, 111, 126, 127, 128, 142, 143, 144, 146, 190, 414), 13, (76748802, 79436033, 76421381, 76486916, 75831299, 79563776, 77535491, 76618245, 79564804, 109905688, 79564547, 127804430, 76618510, 77536014, 79564290, 127804687, 75700495, 127805201, 127806486, 75368982, 76484630, 127803916, 127805458, 75367954, 127806743, 75369239, 127805715, 76484887, 75368211, 127806229, 76483859, 110890265, 75368725, 76484373, 127804173, 127805972, 127804944, 33554439, 33554440, 33554443, 33554441, 33554442, 33554438)),
    ((142, 143, 145, 158, 415), 12, (75700227, 78518274, 76486661, 75503876, 79565569, 75569152, 78580993, 127870480, 76417552, 113055256, 75504389, 78516248, 110954777, 127869452, 127870223, 127869966, 127870737, 110955290, 108857371, 110957084, 127869709)),
    ((143, 145, 175, 191), 3, (112071192, 114169369, 114169626, 109972251, 78518043)),
    ((31, 190), 4, (104731672, 114301465, 78715161, 82646553)),
    ((), 0, ()),
    ((172, 188), 3, (112794905, 67835673, 111871512)),
    ((69,), 1, (100930328,)),
    ((48, 190), 3, (112400664, 82646808, 109777945)),
    ((23, 136, 231), 3, (102175256, 67636248, 109581337, 109579290)),
    ((86,), 1, (111874328,)),
    ((8, 171, 187), 4, (101324568, 78252824, 111806233, 109579802, 109580316, 112855323)),
    ((151, 170, 171, 185, 186, 187, 188, 217, 233, 248, 425), 4, (116988937, 112794392, 67835160, 128526868, 128527382, 128527125, 128527639, 128526611, 128526354, 33554440, 33554442, 33554439, 33554438, 33554443)),
    ((42, 46, 60, 66, 70, 74, 84, 134, 155, 168, 186, 187, 202, 251, 426), 10, (79304704, 79960067, 78186755, 79370244, 80222213, 79239169, 81205505, 78186498, 67767810, 112854552, 128590605, 67767553, 112795161, 76156185, 109712666, 128590348, 128591376, 128591633, 128593175, 128590862, 128592661, 128591119, 128592147, 128592918, 128591890, 128592404, 33554441, 33554443, 33554439, 33554440, 33554438, 33554442)),
    ((61, 65, 71, 73, 75, 139, 163, 167, 172, 173, 181, 186, 188, 189, 229, 235, 427), 12, (82188546, 69867521, 78125061, 79305219, 80353536, 78125313, 80353796, 79305730, 112986904, 101389337, 79366169, 128656655, 79303951, 128656912, 79304208, 128656141, 111744283, 128657426, 79303437, 109777436, 112003610, 128655884, 128658197, 128657683, 128657940, 128656398, 128658454, 128657169, 128658711, 33554439, 33554440, 33554441, 33554442, 33554443, 33554438)),
    ((46, 98, 106, 108, 116, 138, 140, 174, 187, 188, 189, 221, 236, 428), 12, (77797376, 78452739, 79501572, 78317313, 78452997, 78317570, 128722448, 81468176, 112985624, 112986393, 112986650, 128721677, 115150087, 79368973, 128721934, 128723733, 74189077, 114037531, 76285723, 128721420, 128722191, 128724247, 128723990, 128723219, 128723476, 128722962, 128722705, 33554438, 33554442, 33554443, 33554440, 33554441)),
    ((45, 101, 107, 111, 121, 131, 141, 145, 156, 171, 172, 175, 181, 188, 221, 237, 429), 8, (78977024, 81596163, 79435777, 79501314, 81596677, 79436288, 81596420, 79436548, 111872280, 111872793, 101389850, 79366682, 128787727, 79435023, 111875611, 128789526, 128786956, 128787470, 79434252, 128787984, 128788755, 128789783, 128788498, 128788241, 128787213, 128789012, 128789269, 33554440, 33554438, 33554441, 33554439, 33554442, 33554443)),
    ((96, 140, 142, 145, 159, 160, 175, 189, 190, 191, 206, 430), 10, (78714881, 79632389, 80613123, 78584066, 78977284, 80612866, 78584320, 80612352, 80613380, 113051417, 113120280, 128852749, 128852492, 114168326, 79629318, 128853006, 113184778, 128854034, 76416530, 128853520, 128854548, 111937562, 76417044, 128853263, 128853777, 128854805, 76417301, 128855062, 128855319, 128854291, 33554443, 33554439, 33554441, 33554440)),
    ((129, 131, 143, 159, 174, 190, 191, 431), 9, (78649345, 79630597, 79566852, 79630083, 79629826, 77601028, 78513664, 114233624, 79563544, 112003097, 79629569, 112002586, 114232603, 128918285, 128919313, 79566609, 128918799, 114102812, 128918542, 128918028, 128919056)),
    ((175, 191), 2, (114168600, 115217177)),
    ((161, 174), 2, (115151640, 113052185)),
    ((191,), 1, (115217944,)),
    ((165, 230), 2, (108597784, 113052441)),
    ((5,), 1, (100927000,)),
    ((173, 174, 190, 191), 5, (111876633, 81597977, 115149848, 116200730, 79497498, 112003867)),
    ((185, 187), 3, (101387544, 79300376, 68817688, 112855833)),
    ((224,), 1, (108729112,)),
    ((137, 201), 2, (109577752, 110629913)),
    ((163, 169, 170, 186, 187, 232), 6, (112597273, 68818713, 111740696, 67834137, 111740442, 112920859, 110694940, 110695198, 112921373)),
    ((58, 84, 86, 155, 168, 170, 171, 182, 188, 216, 218, 250, 442), 8, (101321752, 79239704, 111806746, 67769626, 110757913, 111806492, 111876891, 77205275, 111744030, 113972255, 77205022, 111744797, 77205789, 129640980, 78319124, 129641751, 129641237, 129641494, 129640723, 129640466, 33554438, 33554439, 33554442, 33554441, 33554440, 33554443)),
    ((100, 105, 106, 107, 115, 117, 122, 123, 138, 170, 171, 172, 173, 185, 188, 189, 219, 251, 443), 16, (80353284, 79042561, 78256128, 81401858, 79239429, 81271040, 78125827, 67833603, 101322776, 78187032, 129704460, 74057228, 68752920, 129705231, 129704974, 129706516, 109839898, 129707287, 78385431, 129705745, 108726809, 129704717, 129706002, 129705488, 129706259, 129707030, 129706773, 33554439, 33554440, 33554442, 33554441, 33554438, 33554443)),
    ((60, 112, 122, 124, 146, 158, 171, 172, 173, 189, 190, 444), 14, (77797637, 82516224, 78190595, 82516737, 78321922, 78453252, 79365889, 111937304, 129770510, 79306510, 113118489, 111937050, 81468697, 111938075, 129770767, 80548633, 111877148, 75238428, 129769996, 80417292, 129772823, 78450967, 75238167, 129771795, 78449939, 75237139, 129771024, 129771281, 129772052, 129772309, 129772566, 129770253, 129771538, 33554440, 33554438, 33554441, 33554443, 33554442, 33554439)),
    ((109, 139, 140, 141, 142, 157, 159, 172, 173, 174, 177, 179, 181, 220, 223, 445), 11, (78321669, 79567105, 78387200, 79431682, 78387459, 78387716, 112073240, 81595928, 111872537, 129835532, 79370764, 129837074, 76350994, 111940890, 77401882, 129835789, 78387981, 129836817, 129836046, 80483342, 129838102, 76352022, 129836560, 80483856, 129837845, 76351765, 129836303, 129837331, 129837588, 129838359, 33554439, 33554442, 33554441, 33554438, 33554443, 33554440)),
    ((128, 129, 142, 143, 146, 158, 159, 174, 175, 188, 189, 207, 222, 254, 446), 11, (77666564, 81661185, 78518529, 77928453, 81661442, 81660928, 112069144, 78977539, 81661699, 129901068, 81662213, 79632652, 78584844, 129902096, 112071706, 80549392, 129901839, 129902867, 77465363, 112985881, 129901582, 129903124, 77465620, 78581268, 129901325, 129902353, 129903638, 77466134, 78581782, 129902610, 77465106, 129903895, 129903381, 33554443, 33554441, 33554440, 33554438, 33554442, 33554439)),
    ((174, 175, 190, 447), 12, (80677888, 78583813, 78780420, 81663235, 78649601, 80678402, 129967889, 77601297, 78514961, 115152664, 78584577, 129967375, 78977816, 80614671, 129967118, 80614414, 129966861, 110954009, 129966604, 129967632)),
    ((206, 207, 222, 223), 3, (114165784, 82711576, 101521177, 116264730, 116265499, 80610843)),
    ((206, 208, 222, 223), 4, (114628888, 67965720, 114101017, 116330778, 116330011)),
    ((3, 223), 3, (100796952, 116266521, 80611865)),
    ((4, 206, 222), 3, (100861976, 114099993, 116200474)),
    ((170,), 1, (101322520,)),
    ((6, 222), 2, (100992536, 116200217)),
    ((215,), 1, (114034712,)),
    ((25,), 2, (114694424, 76090392)),
    ((9, 23, 170), 4, (114891032, 67768600, 68753176, 109582105, 109580570)),
    ((8, 25), 4, (114563352, 76091160, 112728345, 76090905, 110630682, 76091674)),
    ((171, 187, 221), 5, (114957080, 68818456, 101323289, 101324314, 78251545, 115084059, 78252570)),
    ((101, 122, 186, 188, 204, 218, 219, 220, 221, 235, 251, 459), 5, (101519128, 81529112, 102437382, 109778201, 130755863, 130755092, 130754835, 130755349, 130754578, 130755606, 33554443, 33554439, 33554442, 33554440, 33554441)),
    ((12, 100, 128, 132, 140, 144, 148, 156, 172, 189, 198, 205, 218, 221, 238, 460), 10, (81664002, 67899653, 81467393, 81532928, 81598468, 80943363, 82451203, 81467650, 82713088, 80415493, 67899396, 115083288, 115082777, 130819857, 101455370, 101455627, 130818829, 130819600, 130821399, 130819343, 130819086, 130820885, 130820628, 130820114, 130818572, 130821142, 130820371, 33554438, 33554441, 33554439, 33554440)),
    ((62, 133, 135, 141, 143, 145, 147, 157, 175, 188, 190, 193, 195, 207, 220, 221, 222, 225, 233, 461), 11, (81205250, 83630593, 80480772, 81402368, 67900675, 80481029, 117250840, 130884879, 67966232, 81532175, 130884365, 81531661, 107812377, 130885136, 81532432, 130884108, 81531404, 130885907, 130884622, 130886164, 77400084, 130886678, 130886421, 130886935, 130885393, 130885650, 33554441, 33554438, 33554439, 33554443, 33554440, 33554442)),
    ((160, 174, 176, 191, 192, 194, 221, 222, 223, 238, 462), 10, (82710018, 79894785, 81598723, 82710532, 79763717, 80681472, 82709504, 82710789, 79698435, 115213848, 130950415, 81597711, 82709761, 130950158, 81730318, 115148313, 130949644, 81596940, 130950672, 115281416, 130951443, 78513939, 130951957, 78514453, 130951700, 78514196, 130951186, 130952214, 130950929, 130952471, 130949901, 33554443, 33554442, 33554441, 33554439, 33554438)),
    ((175, 191, 206, 222, 223, 463), 11, (81727492, 79697922, 81664261, 81726464, 80812033, 81727235, 80878341, 81727749, 117315096, 115284505, 131015180, 83761420, 114099738, 67966489, 131015694, 79562766, 82776088, 81662990, 116329499, 131016465, 81663761, 131015951, 131015437, 131016208)),
    ((161, 223), 4, (113318680, 81659928, 116329753, 83759897, 115216410)),
    ((207,), 2, (116265752, 81726744)),
    ((19, 26, 207), 4, (101845016, 101844505, 108661786, 76091930, 116266779)),
    ((22, 204), 2, (102041880, 102438169)),
    ((21, 201), 2, (101976600, 110630169)),
    ((136, 193), 2, (102176280, 115148569)),
    ((9, 199), 3, (107551768, 76026648, 102237721)),
    ((170, 205), 3, (113645592, 67900440, 102306585)),
    ((24, 187, 218, 221), 5, (101387289, 68817433, 115083800, 109579546, 112855067)),
    ((41, 200), 2, (110693400, 111741721)),
    ((60, 187, 202, 205), 8, (114826008, 67833368, 113973529, 75239193, 114034202, 67899930, 68817944, 112855579)),
    ((172, 188, 204, 221, 237), 7, (116006168, 80414488, 113969177, 101518874, 68883224, 115148828, 112924187, 110954269)),
    ((140, 150, 202, 203, 204, 205, 216, 221, 222, 476), 6, (113968664, 102503432, 131869461, 131869975, 80548119, 113051161, 82645529, 131868947, 131869718, 131868690, 131869204, 33554439, 33554441, 33554438, 33554443, 33554442)),
    ((172, 173, 177, 181, 189, 191, 204, 206, 213, 219, 223, 253, 477), 17, (80418819, 83630084, 81729536, 80484354, 81528577, 81270788, 82647557, 80484608, 81467906, 67964161, 80354053, 131933455, 82583055, 113969688, 68883992, 114100505, 131933969, 78383889, 131933712, 131933198, 131935511, 80613655, 131934997, 78448917, 131934483, 80612627, 78448403, 131934226, 131935254, 131932684, 131932941, 131934740, 33554438, 33554443, 33554441, 33554442, 33554440, 33554439)),
    ((176, 178, 190, 191, 204, 206, 207, 208, 239, 254, 478), 15, (79763457, 82647042, 80549891, 80681220, 80615680, 79698181, 67965440, 81729797, 101453336, 114166553, 131998477, 80025869, 131998734, 79895054, 81730574, 131998220, 81533196, 132000533, 79563029, 80678677, 131998991, 131999505, 117314054, 117314568, 132000790, 80678934, 79563286, 132000276, 132000019, 79562515, 132001047, 131999248, 131999762, 33554442, 33554439, 33554441, 33554443)),
    ((206, 207, 209, 221, 222, 479), 12, (80746498, 82581763, 80680964, 80615424, 80746753, 79763973, 132064784, 79829264, 101518360, 132063756, 79698700, 80681728, 132064527, 82711823, 115149593, 132065041, 115149338, 132064013, 115151899, 113051676, 80611085, 132064270)),
    ((1, 17, 44, 239), 7, (112662552, 101716505, 74190104, 100668442, 101585947, 82910235, 116464924, 82707996, 68031004)),
    ((2, 29, 238, 255), 4, (100730904, 100731417, 105712666, 101649947, 114100252)),
    ((3, 5, 45), 3, (100797208, 100927257, 107745818)),
    ((2, 30), 2, (100731160, 100730393, 105714202)),
    ((5, 7, 23), 3, (102107160, 100928026, 101058073)),
    ((6, 22, 30, 92), 5, (102042393, 116072472, 72160024, 111875354, 100993307, 100993564)),
    ((10, 149, 171), 5, (112400408, 82517272, 74058776, 101323801, 101060890)),
    ((0, 8), 3, (111548952, 67569176, 101124633, 101254938)),
    ((42, 151), 3, (112794648, 76155928, 101191961)),
    ((88, 153, 238), 4, (101256728, 102242073, 67703065, 111743770, 114100763)),
    ((10, 11, 43, 204, 219), 5, (107614489, 116137240, 74061336, 117119771, 109711898, 107616028, 67899163, 101453085)),
    ((59, 91, 95, 109, 188, 229, 230, 252), 11, (117185560, 76222488, 117119513, 67834393, 110894364, 101389083, 76222748, 117053466, 78318618, 101254685, 113972510, 116196895, 102565664, 111875873)),
    ((42, 61, 109, 221, 223, 234, 238), 10, (117314841, 109711640, 117251100, 69014812, 116202523, 75239963, 107743002, 77401370, 101321245, 78385946, 111937822)),
    ((62, 126, 161, 165, 181, 195, 197, 220, 221, 222, 235, 236, 239, 253, 254, 255, 493), 7, (115022872, 67965976, 117185818, 107812633, 117251355, 67965210, 78452507, 107809820, 132983830, 132984087, 132983573, 132983059, 132982802, 132983316, 33554443, 33554442, 33554440, 33554438, 33554441, 33554439)),
    ((14, 76, 192, 194, 204, 206, 209, 210, 223, 224, 239, 252, 255, 494), 14, (83761157, 83630336, 83826690, 68030468, 82778372, 82582531, 83827201, 68030211, 83695872, 83827461, 68029697, 133047310, 81861646, 68029954, 133047824, 82385680, 109842200, 133046796, 117311001, 117379339, 101452826, 133048081, 133047053, 133048852, 101585671, 114034459, 133049109, 80611605, 133048595, 133049623, 133047567, 133049366, 133048338, 33554438, 33554442, 33554441, 33554440)),
    ((13, 193, 207, 208, 238, 254, 255, 495), 11, (81795842, 83824387, 69081349, 81796096, 83823873, 68032004, 82709253, 83824644, 101650712, 116197913, 83757848, 107680538, 101649435, 101650204, 116197149, 133112589, 81659661, 133113617, 83760913, 133113360, 81660689, 133112332, 133112846, 133113103)),
    ((1, 49, 254, 255), 5, (100668184, 101847833, 102634522, 101585179, 83757082)),
    ((1, 16, 18, 224, 255), 5, (101780248, 101650457, 100667930, 102566427, 117378588, 117378077)),
    ((4, 19, 255), 3, (101845785, 100861720, 101844762, 117312027)),
    ((20,), 1, (101910552, 101910809)),
    ((21, 26), 4, (116726297, 75107865, 101975578, 76092441, 101976856, 101976091)),
    ((6, 22, 244), 3, (102041624, 100993817, 102303770)),
    ((23, 25), 3, (102106904, 102238233, 109581594)),
    ((9, 22, 24), 3, (102173464, 108597529, 102041114)),
    ((26, 58, 137), 6, (101192216, 116989209, 75108121, 76092697, 110759962, 78190106)),
    ((24, 41, 59, 169, 248), 4, (109776409, 102172698, 110694168, 102172187, 102307100, 102304029)),
    ((235,), 1, (112857624,)),
    ((43, 75, 234, 235), 5, (111811097, 75173657, 111809048, 77270040, 113969435, 112920090)),
    ((92, 205, 221, 235, 237, 238), 7, (102503960, 116072217, 116267802, 68029465, 67900186, 110890523, 110761500, 102504221)),
    ((110, 205, 236, 237, 238, 255), 5, (102568473, 110957848, 102568986, 115149083, 116197660, 108858141)),
    ((207, 208, 222, 236, 238, 239, 240, 242, 255, 510), 7, (116398872, 82643736, 102634247, 102634761, 134097942, 81660438, 134097685, 82775829, 113116697, 102633990, 81662489, 134097171, 81660181, 134096914, 134097428, 134098199, 33554443, 33554440, 33554442)),
    ((127, 238, 239, 241, 511), 14, (82909444, 82778117, 82712832, 68095233, 82844162, 83756801, 81861378, 83757315, 134161679, 117250584, 82975492, 82778880, 134161165, 82708237, 68031759, 82642968, 110038553, 116333850, 82779139, 69014298, 134161936, 102569755, 82709008, 134162193, 134161422, 134160908)),
)

LEFT, RIGHT0, RIGHT1 = CHUNKS, 2 * CHUNKS, 3 * CHUNKS
SIZE = 384 // CHUNKS
MAX_SENDS = max(len(p[2]) for p in PLAN)
MAX_FROM = max(1, max(len(p[0]) for p in PLAN))
MESH = pl.DeviceIdType.MESH


def nt_dot(left, right):
    return lax.dot_general(left, right, (((1,), (1,)), ((), ())), preferred_element_type=jnp.float32)


def choose(index, low, high, leaf):
    if all(PLAN[i] == PLAN[low] for i in range(low, high)):
        leaf(PLAN[low])
        return
    middle = (low + high) // 2

    @pl.when(index < middle)
    def _():
        choose(index, low, middle, leaf)

    @pl.when(index >= middle)
    def _():
        choose(index, middle, high, leaf)


def kernel(upper_ref, mask_hbm, out_ref, buf, acc, mask_ref, table, origin, count, in_sem, send_sem, recv_sem):
    brow, column = lax.axis_index("brow"), lax.axis_index("bcol")
    row, half = brow // 2, brow % 2
    own = buf.at[pl.ds(0, 384)]
    load = pltpu.make_async_copy(upper_ref, own, in_sem.at[0])
    load.start()
    load_mask = pltpu.make_async_copy(mask_hbm, mask_ref, in_sem.at[1])
    load_mask.start()

    def leaf(plan):
        origins, targets, sends = plan
        count[0] = len(origins)
        count[1] = targets
        count[2] = len(sends)
        for i, v in enumerate(origins):
            origin[i] = v
        for i, v in enumerate(sends):
            table[i] = v

    choose(row * 16 + column, 0, 256, leaf)
    sends = count[2]
    barrier = pltpu.get_barrier_semaphore()

    @pl.loop(0, count[0])
    def _(i):
        v = origin[i]
        there = ((v >> 4) & 15) * 2 + (half ^ (v >> 8))
        pl.semaphore_signal(barrier, inc=1, device_id=(there, v & 15), device_id_type=MESH)

    load_mask.wait()
    load.wait()
    for i in range(3):
        for j in range(6):
            keep = mask_ref[i, j].astype(jnp.float32)
            at = (pl.ds(i * 128, 128), pl.ds(j * 128, 128))
            buf[at] = (buf[at].astype(jnp.float32) * keep).astype(jnp.bfloat16)

    @pl.when(count[1] > 0)
    def _():
        pl.semaphore_wait(barrier, count[1])

    def slot(index):
        return buf.at[pl.ds(pl.multiple_of(index * SIZE, SIZE), SIZE)]

    def copy(v, i):
        there = ((v >> 20) & 15) * 2 + (half ^ ((v >> 24) & 1))
        return pltpu.make_async_remote_copy(
            src_ref=slot(v & 255),
            dst_ref=slot((v >> 8) & 255),
            send_sem=send_sem.at[i],
            recv_sem=recv_sem.at[(v >> 8) & 255],
            device_id=(there, (v >> 16) & 15),
            device_id_type=MESH,
        )

    def arrived(index):
        pltpu.make_async_copy(slot(index), slot(index), recv_sem.at[index]).wait()

    @pl.loop(0, sends)
    def _(i):
        v = table[i]

        @pl.when((v & (1 << 25)) != 0)
        def _():
            arrived(v & 255)

        @pl.when((v & (1 << 26)) != 0)
        def _():
            copy(v, i).start()

    has0 = (row == 0) | ((column >= row) & (row + column >= 16))
    has1 = (column < 15) & ((row <= 1) | ((column + 1 >= row) & (row + column >= 16)))
    here = pl.ds(pl.multiple_of(half * 384, 128), 384)
    other = pl.ds(pl.multiple_of(384 - half * 384, 128), 384)

    def rows(index):
        return buf[pl.ds(pl.multiple_of(index * SIZE, SIZE), 384), :]

    @pl.when(has0)
    def _():
        @pl.loop(0, CHUNKS)
        def _(j):
            arrived(SIB + j)

        right = jnp.where(row + column == 0, 0, RIGHT0)
        acc[:, here] = nt_dot(rows(0), rows(right))
        acc[:, other] = nt_dot(rows(0), rows(SIB))

    @pl.when(has1)
    def _():
        @pl.loop(0, CHUNKS)
        def _(j):
            arrived(SIB + CHUNKS + j)

        left = jnp.where(column == 0, RIGHT1, LEFT)
        for columns, right in ((here, RIGHT1), (other, SIB + CHUNKS)):
            term = nt_dot(rows(left), rows(right))

            @pl.when(has0)
            def _():
                out_ref[:, columns] = (acc[:, columns] + term).astype(jnp.bfloat16)

            @pl.when(jnp.logical_not(has0))
            def _():
                out_ref[:, columns] = term.astype(jnp.bfloat16)

    @pl.when(has0 & jnp.logical_not(has1))
    def _():
        out_ref[...] = acc[...].astype(jnp.bfloat16)

    @pl.when(jnp.logical_not(has0 | has1))
    def _():
        out_ref[...] = jnp.zeros_like(out_ref)

    @pl.loop(0, sends)
    def _(i):
        v = table[i]

        @pl.when((v & (1 << 26)) != 0)
        def _():
            copy(v, i).wait_send()


def per_device(upper_store, block_mask):
    return pl.pallas_call(
        kernel,
        out_shape=jax.ShapeDtypeStruct((384, 768), jnp.bfloat16),
        in_specs=[pl.BlockSpec(memory_space=pl.ANY)] * 2,
        out_specs=pl.BlockSpec(memory_space=pltpu.VMEM),
        scratch_shapes=[
            pltpu.VMEM((SLOTS * SIZE, 768), jnp.bfloat16),
            pltpu.VMEM((384, 768), jnp.float32),
            pltpu.SMEM((3, 6), jnp.int32),
            pltpu.SMEM((MAX_SENDS,), jnp.int32),
            pltpu.SMEM((MAX_FROM,), jnp.int32),
            pltpu.SMEM((3,), jnp.int32),
            pltpu.SemaphoreType.DMA((2,)),
            pltpu.SemaphoreType.DMA((MAX_SENDS,)),
            pltpu.SemaphoreType.DMA((SLOTS,)),
        ],
        compiler_params=pltpu.CompilerParams(
            collective_id=0, has_side_effects=True, vmem_limit_bytes=60 * 2**20
        ),
        name="cannon_steps",
    )(upper_store, block_mask)


def solution(mesh):
    spec = P("brow", "bcol")
    return jax.shard_map(per_device, mesh=mesh, in_specs=(spec, spec), out_specs=spec, check_vma=False)
```

time: 205 us -> 39.4 us (0.19)
  the two profiles are of different devices: /device:TPU:223 before, /device:TPU:417 now
where the time goes in v3:
time: 39.4 us; the launch traced here: 39.2 us
  Pallas kernels  37.3 us (95%)
  local copies, waits for them, and re-layouts  1.92 us (5%)
    pallas_call x1, Pallas kernels, per_device(): pl.pallas_call(kernel, out_shape=jax.ShapeDtypeStruct((384, 768), jnp.bfl...  37.3 us
    unnamed x1, local copies, waits for them, and re-layouts  1.92 us

profile of v3, /device:TPU:417, one launch (start us, length us, event | category | flops | bytes accessed | tf_op | source)
XLA Modules:
  0.0 39.2 jit_solution(8470772537544780843)
XLA Ops:
  0.0 37.3 %cannon_steps.1 = bf16[384,768]{1,0:T(8,128)(2,1)} custom-call(bf16[384,768]{1,0:T(8,128)(2,1)} %upper_ref.1, s32[3,6]{1,0:T(4,128)} %mask_hbm.1), custom_call_target="tpu_custom_call" | custom-call | tf_op jit(solution)/shard_map/cannon_steps/pallas_call | solution.py:420
  37.3 1.9 %copy.4 = bf16[384,768]{1,0:T(8,128)(2,1)} copy(bf16[384,768]{1,0:T(8,128)(2,1)} %cannon_steps.1) | data formatting | bytes 1179648

commit v4 on v0

v4 whole, which is shorter than its diff:
```python
import jax
import jax.numpy as jnp
from jax import lax
from jax.experimental import pallas as pl
from jax.experimental.pallas import tpu as pltpu
from jax.sharding import PartitionSpec as P

CHUNKS = 6
SLOTS = 45
SIB = 33
PLAN = (
    ((1, 14, 16, 31, 32, 192, 240, 256), 5, (83894528, 83894785, 83895042, 83895299, 83895556, 83895813, 102630936, 104799001, 117451799, 70127641, 117450514, 117451542, 117451285, 103682842, 117450771, 103683099, 117451028, 68028443)),
    ((2, 3, 13, 14, 15, 17, 18, 33, 225, 227, 257), 10, (79697921, 69212419, 117516307, 68163588, 67114757, 80812051, 82843906, 117515793, 68163345, 117516050, 68224530, 67113472, 117515279, 68162831, 117515536, 68163088, 117517078, 104665112, 117517335, 68225815, 101517849, 117515022, 68162574, 117516821, 117514508, 117516564, 117514765, 33554439, 33554443, 33554440, 33554441, 33554442, 33554438)),
    ((3, 12, 17, 18, 19, 32, 34, 35, 48, 53, 64, 194, 226, 258), 9, (117580301, 68227853, 69278723, 81860610, 117580558, 68294917, 67176193, 68228110, 81861124, 101845272, 81991936, 106371353, 72093721, 117580815, 68228367, 117582100, 117581072, 117582614, 117581586, 117581843, 117581329, 117580044, 117582871, 117582357, 33554438, 33554441, 33554440, 33554442, 33554443, 33554439)),
    ((5, 6, 18, 20, 21, 33, 35, 37, 39, 50, 53, 179, 227, 243, 259), 8, (79828996, 68294658, 67241472, 81926149, 67242243, 81926401, 101914648, 67180056, 117645837, 68293389, 117646608, 117645580, 100992537, 117646351, 68293132, 117648407, 117647122, 68293903, 117647379, 117646865, 117647636, 117648150, 117647893, 117646094, 33554442, 33554439, 33554441, 33554440, 33554438, 33554443)),
    ((5, 19, 20, 21, 34, 36, 64, 66, 68, 82, 84, 85, 164, 210, 228, 260), 8, (78845954, 68425985, 68491268, 81991683, 67442949, 83040256, 101976856, 101910553, 117711630, 101975578, 68359182, 117711116, 101910299, 117711887, 117713686, 117712401, 117713172, 117712658, 117712915, 117713943, 117712144, 117713429, 117711373, 33554441, 33554440, 33554438, 33554443, 33554439, 33554442)),
    ((3, 4, 20, 21, 22, 23, 37, 39, 65, 67, 69, 71, 83, 85, 229, 231, 244, 261), 8, (80877572, 69474560, 68425729, 67373315, 82057221, 67373058, 102041368, 117776909, 68424461, 117777423, 68424975, 102041882, 100862745, 117777937, 68425489, 117777166, 117777680, 117778965, 117778708, 117779479, 117776652, 117778451, 117778194, 117779222, 33554438, 33554441, 33554439, 33554442, 33554443, 33554440)),
    ((7, 12, 21, 22, 23, 38, 87, 102, 116, 130, 164, 230, 262), 11, (67311872, 83106308, 68491779, 117843216, 68490768, 68622849, 82123010, 117842959, 68490511, 82254085, 102106649, 103488792, 102107418, 72092952, 102107931, 73077528, 117843987, 117842188, 68489740, 117844758, 117843473, 117843730, 117844244, 117844501, 117845015, 117842445, 117842702, 33554441, 33554438, 33554440, 33554442, 33554439, 33554443)),
    ((9, 22, 23, 24, 25, 39, 41, 71, 99, 101, 103, 115, 118, 119, 135, 263), 8, (69605892, 82188544, 68556801, 67504387, 82188802, 68557061, 111548696, 75042328, 102172953, 117908752, 68556304, 117908238, 68555790, 117910551, 117907981, 68555533, 117908495, 117909523, 117910037, 117910294, 117909266, 117909009, 117909780, 117907724, 33554439, 33554440, 33554441, 33554443, 33554442, 33554438)),
    ((10, 24, 25, 40, 56, 57, 72, 104, 120, 132, 136, 137, 152, 228, 264), 13, (68622593, 68687874, 83106051, 69475072, 68753667, 68688645, 83367941, 69671684, 105520152, 67700760, 78125828, 69802240, 75043864, 117973774, 68621326, 102237977, 117974288, 68621840, 102239002, 117974031, 68621583, 117974802, 117973517, 117975316, 117975573, 117975059, 117976087, 117974545, 117975830, 117973260, 33554441, 33554440, 33554438, 33554443, 33554442, 33554439)),
    ((8, 11, 24, 26, 27, 41, 43, 57, 73, 105, 135, 137, 153, 199, 233, 265), 13, (82057473, 67573762, 68753411, 71833600, 68688130, 81205253, 69737477, 83368452, 70785284, 83433728, 70851844, 102173208, 118040081, 68687633, 118039310, 68686862, 102304537, 118041366, 118039567, 118039053, 118040595, 118041623, 118039824, 118041109, 118040852, 118038796, 118040338, 33554439, 33554442, 33554440, 33554443, 33554441, 33554438)),
    ((12, 26, 27, 29, 42, 90, 166, 168, 170, 186, 200, 202, 217, 234, 236, 251, 266), 15, (82188288, 69736451, 67639298, 68818945, 68884484, 82450693, 69475332, 67836421, 68885251, 74059009, 67836672, 102369560, 103488281, 102303514, 102368795, 70983193, 72093465, 118104589, 118106902, 118104332, 68751884, 118105617, 101452572, 118104846, 118106131, 118106388, 118105360, 118105103, 118105874, 118106645, 118107159, 33554438, 33554441, 33554443, 33554439, 33554442, 33554440)),
    ((10, 13, 27, 28, 29, 43, 167, 169, 171, 186, 187, 201, 203, 216, 235, 267), 12, (69605634, 68622339, 82450436, 68884736, 69015813, 68819203, 70982145, 82450949, 107679001, 68814617, 82451201, 105716248, 68880920, 101255962, 104664092, 101254683, 118170382, 68817934, 118170896, 68818448, 118171410, 118170125, 68817677, 118170639, 118172438, 118171153, 118171924, 118172695, 118169868, 118172181, 118171667, 33554440, 33554438, 33554442, 33554443, 33554441, 33554439)),
    ((10, 13, 27, 28, 29, 44, 192, 202, 204, 206, 208, 220, 221, 268), 10, (67246340, 67508225, 70981888, 68950274, 69015552, 67770627, 72093186, 69016068, 68885509, 72093957, 102500376, 102500121, 118236689, 69016593, 118236432, 68883984, 105648903, 71109895, 118235404, 118236175, 68882956, 118235661, 118238231, 118236946, 118237717, 118237460, 118235918, 118237203, 118237974, 33554442, 33554441, 33554438, 33554443, 33554440)),
    ((1, 15, 28, 29, 30, 45, 195, 197, 205, 208, 219, 221, 225, 237, 239, 252, 269), 14, (68884995, 67180548, 71047938, 68950788, 69016325, 104208664, 67836928, 68879896, 69998592, 67897089, 78322200, 105713689, 68819737, 116333595, 102566170, 68880155, 118301197, 68948749, 118300940, 68948492, 118302482, 118303253, 118301454, 118303767, 118302225, 118301711, 118302996, 118302739, 118301968, 118303510, 33554440, 33554443, 33554442, 33554439, 33554441, 33554438)),
    ((0, 15, 30, 31, 46, 74, 192, 236, 238, 240, 241, 254, 255, 270), 11, (67115268, 71111939, 68099074, 82778113, 69146880, 67180804, 70126592, 68099333, 102631192, 70127877, 100669959, 69143815, 70126849, 118366990, 111808793, 118366733, 103683594, 69144586, 118367247, 103683337, 69144329, 118369303, 82709271, 118366476, 118367504, 118369046, 118368275, 118368789, 82708757, 118367761, 118368532, 118368018, 33554443, 33554440, 33554438)),
    ((14, 17, 29, 30, 225, 239, 255, 271), 14, (69212928, 68229125, 68028161, 83695621, 69144066, 103095322, 69011482, 68028932, 105713177, 68028675, 101517340, 100731931, 71179036, 69143552, 101518109, 100732184, 71111708, 118433040, 69080592, 118432012, 118432783, 69080335, 118432526, 118432269, 118433297)),
    ((1, 30, 48, 62, 224, 272), 5, (100668952, 104930585, 71176217, 106827034, 118500375, 104729627, 118499090, 118499861, 118500118, 118499347, 118499604)),
    ((1, 2, 15, 18, 19, 48, 49, 81, 209, 241, 273), 7, (70260993, 81795328, 67178757, 68098049, 67178243, 68098816, 67178500, 100734217, 67177986, 103683864, 118564883, 100733960, 118565140, 118564626, 67243026, 118565654, 118565911, 118565397, 33554438, 33554442, 33554443, 33554439)),
    ((2, 3, 19, 48, 50, 80, 210, 212, 242, 274), 7, (67179265, 69277957, 82909186, 67311620, 68225283, 67179008, 100796440, 100731673, 118630676, 67309076, 118630419, 118631190, 118630162, 118631447, 118630933, 33554438, 33554441, 33554440, 33554442, 33554439, 33554443)),
    ((3, 4, 20, 35, 49, 51, 113, 243, 275), 8, (81008642, 68290048, 67246083, 80877828, 82974721, 82974981, 101779992, 118696726, 67375126, 118695955, 118695698, 118696212, 118696469, 118696983, 33554443, 33554442, 33554440, 33554441, 33554438, 33554439)),
    ((4, 5, 21, 26, 28, 36, 52, 82, 212, 244, 276), 11, (83040515, 67377410, 68356869, 100927256, 100861721, 83040768, 67377921, 68356612, 105192218, 68623130, 73142554, 118762262, 111745307, 67440662, 118761234, 75107611, 118761491, 67439634, 118762005, 118762519, 118761748, 33554440, 33554443, 33554439, 33554438, 33554441, 33554442)),
    ((4, 5, 6, 27, 51, 117, 119, 213, 245, 277), 11, (81008899, 70522881, 67377157, 68421634, 100862488, 83106564, 67377664, 112465945, 74124313, 100993306, 118827798, 118827284, 67505684, 118827027, 118827541, 118828055, 118826770, 33554439, 33554442, 33554443, 33554441, 33554438, 33554440)),
    ((6, 7, 54, 118, 214, 230, 246, 278), 7, (70457604, 81074181, 67442689, 83171328, 67443203, 83171586, 101058328, 101059353, 118893591, 67571991, 118892306, 118893334, 67570706, 118892820, 118893077, 118892563, 33554438, 33554441, 33554440, 33554443, 33554442, 33554439)),
    ((6, 7, 8, 9, 11, 20, 55, 57, 151, 183, 247, 279), 10, (81139970, 67508480, 82189057, 67508739, 83237124, 112794905, 67569433, 67508997, 100992794, 106630936, 102435611, 118958099, 118958356, 118958870, 118957842, 118958613, 118959127, 33554441, 33554442, 33554443, 33554439, 33554440, 33554438)),
    ((8, 9, 26, 56, 57, 58, 88, 152, 214, 248, 280), 10, (70719493, 67574019, 83302401, 67704836, 70719744, 70851586, 115874072, 67569688, 101189657, 101124891, 113842714, 75108634, 67705114, 119024406, 67702806, 119024663, 119024149, 119023378, 119023635, 119023892, 33554439, 33554440, 33554443, 33554441, 33554438, 33554442)),
    ((8, 9, 10, 57, 59, 166, 181, 200, 217, 233, 249, 251, 281), 10, (81139715, 72882178, 67639553, 82253829, 73996801, 67639813, 82385412, 70785536, 108597016, 67635480, 101124377, 119090199, 119089428, 119089942, 119089685, 119089171, 119088914, 33554439, 33554442, 33554441, 33554440, 33554438, 33554443)),
    ((10, 11, 13, 28, 58, 186, 216, 246, 250, 282), 13, (68426497, 82384898, 70850820, 67770881, 68688389, 83499264, 75108099, 101254936, 70982659, 101320985, 106696730, 71965444, 102500891, 119154964, 119155735, 119154450, 119155478, 119155221, 119154707, 33554439, 33554441, 33554438, 33554440, 33554442, 33554443)),
    ((10, 11, 12, 13, 23, 28, 29, 219, 221, 249, 251, 283), 14, (68491520, 70588932, 83236866, 67836161, 68950020, 67770371, 69933315, 67771136, 70916613, 101255704, 106630169, 67765785, 101255451, 103553562, 67897626, 71110426, 101387036, 119220500, 67898900, 119220757, 119221014, 119220243, 119221271, 119219986, 33554440, 33554438, 33554442, 33554439, 33554443, 33554441)),
    ((12, 13, 26, 27, 29, 60, 62, 205, 214, 220, 250, 252, 284), 11, (68426245, 83105795, 67966976, 67835908, 73141762, 67967745, 68819460, 71178241, 68880386, 101386265, 103553307, 67897883, 106697222, 102369816, 101455130, 119286550, 67964950, 119285779, 119285522, 119286036, 119286807, 119286293, 33554440, 33554439, 33554443, 33554442, 33554441)),
    ((11, 12, 13, 15, 30, 31, 63, 236, 241, 247, 253, 255, 285), 14, (69933059, 67967236, 68098306, 67901442, 71047429, 68945408, 67901697, 72158465, 101385752, 106631449, 101386778, 103422747, 67771419, 71110939, 119351315, 102438684, 119352086, 119351829, 119352343, 119351572, 119351058, 33554442, 33554443, 33554440, 33554441, 33554439, 33554438)),
    ((0, 14, 15, 31, 46, 47, 62, 239, 254, 286), 11, (69146629, 82122752, 68098562, 71175425, 67967491, 68163844, 71175939, 69011972, 68164352, 71175682, 104731656, 71176453, 101586712, 103746823, 71176967, 119417879, 68096279, 119417622, 83757590, 119417108, 119417365, 119416851, 119416594, 33554438, 33554443, 33554441, 33554442)),
    ((14, 15, 30, 253, 287), 10, (70192128, 68032513, 69076994, 67115008, 70129923, 71177989, 70193156, 111351832, 69012248, 104665625, 119481102, 67115790, 119480588, 119480845, 119481616, 119481873, 119481359)),
    ((1, 15, 34, 35, 44, 46, 61), 6, (100798232, 100668697, 108863002, 103682587, 74190362, 100799772, 107746333, 105779998)),
    ((2, 18, 51, 52), 4, (103815960, 67309592, 103947291, 100734745, 67309851, 100865562, 100731164)),
    ((35, 68), 6, (72423429, 69212163, 67243265, 70326272, 67243522, 70260740, 100929048, 100799001, 100800282)),
    ((51, 62, 63, 64), 9, (100863256, 100863769, 71309569, 69213187, 70589188, 69343488, 69343749, 67245058, 105844762, 101913883, 107812124)),
    ((5, 8, 10, 44, 62, 85, 113), 7, (101979672, 100927001, 108730138, 109579291, 107614236, 104663326, 75044380, 100928797)),
    ((15, 43, 52, 85), 4, (100995353, 100865050, 100865304, 108728603, 105714716)),
    ((7, 11, 103, 119), 4, (101061400, 106371865, 101059098, 69868569, 101059867, 74060825)),
    ((8, 52, 59, 60, 86), 4, (100864536, 109776921, 109775900, 101124635, 100996637, 109778458)),
    ((9, 10, 41, 42, 136), 5, (107613976, 101191449, 104274715, 101190938, 109711646, 76155931, 101190428, 110694175, 101190685)),
    ((8, 57, 59, 120, 138), 11, (70326789, 79239426, 72554753, 75044864, 101127960, 70720004, 69738243, 101123609, 108666138, 76221978, 109647388, 101258523)),
    ((29, 38, 43, 60, 186), 8, (82581508, 76156418, 69737216, 78256129, 69737989, 82319363, 109712920, 108793881, 101323290, 105649947, 101320732)),
    ((6, 10, 27, 29, 139, 154), 10, (69867524, 75173378, 79305217, 69540613, 73079043, 104733208, 75172864, 101258778, 72159000, 107679513, 101386523, 101258268, 101386013)),
    ((13, 27, 28, 60, 61), 9, (81795073, 69474821, 71047171, 70981632, 71964676, 69212674, 101451288, 72094232, 103681819, 105649689, 101451804, 105649434)),
    ((46, 61, 62, 124), 12, (71112962, 81926656, 70392323, 74062337, 70982403, 71113216, 73144325, 73207812, 104537880, 74258200, 104799514, 74256922, 113973017, 105714459, 101517596, 101516829)),
    ((0, 14, 17, 31, 32, 44, 47, 60, 62, 63, 78, 302), 11, (71243781, 72224772, 71112705, 70326531, 72223744, 72224258, 104728088, 72224001, 104729114, 120463628, 70065420, 102768135, 120464913, 71244817, 102631705, 70192921, 120463885, 71111437, 71177497, 104728347, 105780746, 120466455, 68029207, 120465170, 105779718, 71240710, 68027922, 120466198, 120464656, 120465941, 120465427, 120464399, 120465684, 120464142, 33554443, 33554440, 33554441)),
    ((30, 31, 46, 62, 63, 143, 303), 11, (70125313, 71047680, 73275906, 71178500, 71241475, 120529164, 71048204, 71241989, 105843992, 70327298, 71241732, 71240961, 120530192, 69077520, 71177744, 105714969, 114103834, 120530449, 120529935, 120529421, 120529678)),
    ((17, 33, 34, 61, 62), 6, (101783064, 67244056, 101848603, 101716761, 108794394, 106828060)),
    ((34, 41, 46, 47, 82), 6, (101782040, 104864537, 73209113, 110694682, 101914395, 104795676)),
    ((33, 45, 52, 60, 63), 6, (100864792, 106829593, 107289115, 101848860, 75238939, 107746586)),
    ((22, 68, 85), 6, (72357890, 69277700, 70588416, 69408769, 69278469, 69409027, 101914136, 102042137, 101913114)),
    ((21, 67), 6, (69278212, 70588677, 69670912, 69539843, 70391809, 69540354, 101975832, 101979161)),
    ((27, 35, 51, 52, 62), 4, (100863000, 100865817, 107679770, 100800027, 104663068)),
    ((13, 101), 2, (102110488, 106695705)),
    ((24, 40, 41), 2, (102173464, 110694426, 102172185, 110694939)),
    ((9, 25, 58), 6, (110759448, 105454107, 101190169, 77204507, 102237722, 76090394, 77074970)),
    ((9, 24, 26, 107, 137, 153), 8, (101192984, 103357465, 68749849, 102172700, 102240794, 108597277, 112921883, 67701786)),
    ((27, 61, 74, 153), 11, (72751361, 81271043, 70785026, 83368708, 70785792, 79305477, 108795417, 111808539, 102241560, 107680026, 68815642, 75110170)),
    ((10, 11, 12, 26, 44, 45, 62), 10, (83433473, 71965187, 69671172, 69671936, 108728856, 82516485, 69802498, 106631705, 106762011, 102304028, 106630426, 104662813, 106632478, 104663839)),
    ((13, 29, 44, 47), 15, (70392578, 69671428, 75238657, 107745048, 69867780, 79436547, 73014277, 79436800, 103679514, 105649179, 69999643, 102501145, 71110171, 104731164, 72159513, 73144089)),
    ((1, 11, 12, 14, 15, 27, 29, 31, 36, 45, 46, 53, 59, 60, 63, 108, 317), 11, (70261248, 82647041, 70916356, 72161538, 102767897, 74256131, 121448981, 69999381, 70065173, 74256645, 106761242, 106763032, 73207321, 121448210, 121447953, 121446668, 121447439, 113972507, 121447696, 121447182, 121448724, 121449238, 121448467, 121449495, 121446925, 33554442, 33554439, 33554441, 33554440, 33554443, 33554438)),
    ((15, 16, 28, 30, 31, 43, 46, 47, 60, 94, 318), 17, (68164097, 70064133, 73273348, 71244036, 69475843, 70064640, 121512461, 71244301, 73272834, 70064909, 70589442, 80550401, 70982913, 121512975, 70195471, 103680537, 73273091, 69409795, 106695960, 121512718, 121515031, 69077783, 73272320, 70193431, 70261765, 121513489, 105843718, 121514260, 73273862, 102500634, 70192660, 73143578, 121513232, 103681563, 121514774, 121512204, 121514517, 121513746, 121514003, 33554442, 33554440, 33554439, 33554443, 33554441)),
    ((0, 45, 46, 47, 49, 62, 319), 10, (70392069, 70129664, 72226818, 69409284, 70130180, 70195201, 72290051, 106764056, 70130433, 121578511, 72226063, 104663577, 121579025, 72226577, 70126353, 121578768, 102565658, 121577997, 104666651, 104666908, 104662557, 121578254, 121577740)),
    ((35, 49, 68, 79, 95), 4, (102963992, 67374872, 100799257, 105776666, 105778971, 105777180)),
    ((16, 77, 78, 86, 93, 94), 6, (108859416, 106306329, 76353049, 100996890, 106759707, 109909276, 105715229)),
    ((69, 74, 93), 3, (100930072, 111808281, 109843738)),
    ((77, 85, 93), 5, (104077592, 67440152, 109451545, 75304217, 109907994)),
    ((69,), 7, (74520577, 71309315, 69343234, 72685568, 72489221, 70457348, 100931096, 100930585, 100931354)),
    ((20, 78, 85, 86), 7, (100994840, 71440384, 77863171, 71571460, 72620033, 71571714, 71571973, 105711129, 100995866, 107681563)),
    ((74,), 1, (111807512, 111807769, 111808026)),
    ((81, 86, 119), 3, (101125656, 100996377, 105711386)),
    ((9, 77), 3, (101189144, 76026392, 105646617)),
    ((56, 92, 153), 5, (106043928, 72948760, 78320152, 101256985, 111743514)),
    ((8, 26, 44, 59, 123), 9, (71440643, 68032773, 71702528, 70916868, 106633752, 74190872, 71702785, 108661529, 71703042, 110761242, 108662811, 107613724)),
    ((76, 91, 140), 7, (73013507, 72947972, 73078789, 77270273, 83565056, 77270530, 111873817, 109775128, 106632218, 106632987)),
    ((2, 6, 10, 12, 42, 44, 60, 72, 77, 90, 91, 93, 125, 140, 332), 11, (83564803, 74324225, 83696133, 75176192, 76287490, 122430222, 72030734, 106694937, 77337881, 76288004, 122430993, 72030993, 108792600, 108859659, 106695194, 77338138, 76289803, 122431764, 122430736, 122431250, 122431507, 122429965, 122432278, 122430479, 122429708, 122432021, 122432535, 33554438, 33554441, 33554442, 33554439, 33554440)),
    ((11, 13, 15, 29, 37, 43, 45, 47, 60, 61, 65, 69, 71, 92, 93, 94, 95, 125, 163, 229, 333), 12, (71506177, 72751106, 73209859, 71374852, 71833860, 73210624, 73014017, 72092421, 106629144, 107810329, 122495501, 73143053, 122496272, 73143824, 107681306, 122495758, 73143310, 122496015, 107812379, 107811868, 122496529, 122497043, 122496786, 122497557, 122497814, 122497300, 122495244, 122498071, 33554443, 33554442, 33554440, 33554438, 33554441, 33554439)),
    ((32, 46, 63, 64, 79, 93, 94, 95, 110, 334), 10, (72423681, 73340931, 74322181, 73275397, 73210116, 71637248, 73341186, 74320896, 73276163, 74321924, 122561808, 73341456, 104930329, 73206041, 75370265, 106828824, 74321410, 122560780, 73341708, 106760218, 106825499, 122561294, 73208846, 122561037, 107878155, 122562836, 70125588, 122563093, 107876870, 70125845, 122563607, 122562065, 122561551, 122563350, 122562322, 122562579, 33554442, 33554441, 33554440, 33554439)),
    ((35, 47, 62, 63, 94, 95, 335), 8, (73338370, 75372803, 73275652, 73338113, 71309824, 116333336, 75370008, 72223493, 106826009, 74387225, 73338627, 122627087, 73274639, 73339141, 107941146, 73338884, 73337856, 122626573, 73274125, 122627344, 73274896, 122626316, 122626830, 122627601)),
    ((51, 92, 94, 95), 6, (101848088, 107026713, 72948249, 75369753, 108926746, 73272090, 110890267)),
    ((34, 78), 5, (115481368, 110959385, 71768601, 68228888, 74321177)),
    ((68, 73, 85), 4, (101978648, 103881497, 67375385, 110890010)),
    ((41, 86, 108), 3, (112924440, 110693657, 100995610)),
    ((69, 92), 3, (100930328, 113973529, 77336089)),
    ((68,), 8, (72488960, 69474308, 71636995, 71505922, 69540101, 67439873, 104012312, 67374104)),
    ((58, 65, 77, 91), 11, (71375365, 82123266, 71768323, 72555008, 69672196, 109843480, 71637505, 112857626, 111614489, 77204761, 106694683)),
    ((2, 38, 93, 103), 3, (101061144, 106632729, 106630683, 111874842)),
    ((25, 91), 3, (110629912, 68683800, 112858137)),
    ((73, 75, 80, 90, 122), 5, (110825497, 108594712, 106628636, 110825243, 108725789, 106759962)),
    ((60, 75, 77, 123, 171), 7, (106502937, 78255385, 101323544, 108794140, 76224284, 105645851, 108660762)),
    ((6, 23, 27, 29, 43, 59, 74, 75, 77, 87, 89, 92, 93, 106, 347), 12, (72751616, 83695877, 72030467, 76225028, 72882434, 82516225, 110825752, 108728089, 108729882, 123412748, 74060300, 123414290, 72092690, 123414033, 123413519, 74061071, 106761499, 123413005, 123414547, 123414804, 123415061, 123415318, 123415575, 123413776, 123413262, 33554442, 33554441, 33554440, 33554443, 33554439, 33554438)),
    ((20, 26, 28, 45, 54, 60, 62, 76, 77, 86, 93, 109, 156, 244, 348), 13, (71899136, 72620290, 73210369, 83630083, 75372549, 72161282, 73075204, 72358657, 73210885, 123478798, 77336580, 74126350, 73074947, 110892811, 106896408, 74192664, 123479312, 123479569, 123480083, 123479826, 72158226, 123478541, 123479055, 123480854, 123481111, 123478284, 123480597, 123480340, 33554441, 33554439, 33554442, 33554440, 33554438)),
    ((45, 49, 59, 61, 63, 65, 77, 78, 89, 91, 92, 94, 95, 109, 349), 15, (71375106, 82582016, 72096003, 73140997, 74258689, 71506436, 104995352, 105712153, 116267803, 72091163, 106371610, 72096260, 75303963, 72091928, 75306521, 123544848, 106629916, 74192400, 123546647, 72225047, 73074458, 75304728, 108860445, 123543820, 123545876, 123546133, 123544591, 123545619, 123546390, 123544334, 123545362, 123544077, 123545105, 33554443, 33554441, 33554440, 33554438, 33554442, 33554439)),
    ((16, 47, 48, 50, 62, 78, 79, 80, 126, 350), 10, (72358145, 72227075, 72292354, 75370500, 73206533, 72227330, 75370757, 75369472, 105712408, 71375616, 107877913, 72223257, 123610384, 72162064, 107876123, 105780250, 123609870, 72162318, 123610127, 123611412, 71174164, 123609356, 108926217, 72289812, 123612183, 71174935, 123611669, 108925703, 72290583, 71174421, 123609613, 123610898, 123611155, 123610641, 123611926, 33554443, 33554438, 33554442, 33554440)),
    ((78, 79, 92, 351), 12, (72358405, 74323972, 72292611, 72227585, 74386946, 108860696, 75371008, 72292865, 123675406, 83827470, 106765593, 71310350, 123675149, 72157209, 74322701, 74386432, 123675663, 106763802, 123676177, 106762779, 123675920, 123674892, 106762524)),
    ((110, 111, 127), 2, (108075544, 76420888, 109972761, 109974810, 109973019)),
    ((80, 126), 2, (112006936, 109908761)),
    ((111,), 1, (109974296,)),
    ((115, 117, 120, 126), 3, (101127448, 112006425, 107808282, 112005659)),
    ((108,), 2, (111938840, 79368984)),
    ((50, 119, 124), 4, (104208408, 67571480, 113972761, 109777946)),
    ((103,), 5, (74717184, 77862917, 74913793, 67506180, 74782722, 67505923, 101062168, 101061657)),
    ((120,), 6, (75634693, 74717443, 69605377, 73799684, 72816640, 73799938, 101127192)),
    ((123, 136), 3, (108660504, 101191962, 108660249, 109712411)),
    ((25, 108, 122, 138, 154, 230), 5, (108595481, 109645082, 101259036, 77138716, 108595995, 109644312, 107677470, 108597789)),
    ((10, 36, 38, 40, 45, 74, 91, 108, 120, 122, 123, 155, 187, 230, 234, 362), 9, (108661272, 111938587, 124396045, 75043597, 106634010, 74191642, 108730908, 78385436, 124396559, 75044111, 110757401, 124397073, 75044625, 112922377, 124398358, 73076758, 124395788, 124398615, 124396816, 124397330, 124397587, 124396302, 124397844, 124398101, 33554440, 33554439, 33554438, 33554443, 33554442)),
    ((11, 21, 43, 53, 58, 69, 77, 92, 105, 109, 122, 123, 124, 125, 135, 157, 171, 229, 239, 363), 12, (74782981, 79367168, 75175938, 70851329, 74783492, 75110659, 74979845, 75111169, 108595225, 75111428, 112989464, 75237656, 78450456, 124461581, 124463380, 75109133, 124462352, 108726810, 75109904, 124461324, 124462095, 75109647, 107809051, 124462609, 124463894, 124464151, 124461838, 124462866, 124463637, 124463123, 33554440, 33554438, 33554441, 33554439, 33554443, 33554442)),
    ((32, 50, 60, 74, 92, 93, 106, 123, 124, 125, 140, 156, 157, 224, 226, 364), 13, (72554501, 76159492, 73668609, 74062592, 75241730, 82713091, 78384642, 74783747, 74062853, 75242243, 108791832, 74258944, 73997825, 104667929, 75172121, 124527888, 124527631, 75175183, 124528659, 124529687, 124527117, 124529430, 124527374, 124526860, 124528402, 124529173, 124528145, 124528916, 33554439, 33554443, 33554440, 33554441, 33554438, 33554442)),
    ((35, 45, 61, 77, 93, 99, 107, 108, 111, 124, 125, 126, 127, 157, 205, 237, 365), 13, (83630337, 75307008, 77401602, 75241985, 82582788, 75307781, 77339139, 75308036, 112004120, 77401859, 75236888, 109907225, 73139993, 107677210, 124593167, 75240719, 106760731, 76355099, 124593681, 75241233, 109777693, 124592910, 75240462, 124592653, 109909788, 124595223, 75240205, 124593938, 124594195, 124594709, 124593424, 124594966, 124594452, 124592396, 33554440, 33554442, 33554439, 33554443, 33554441, 33554438)),
    ((76, 78, 81, 94, 95, 111, 126, 127, 142, 255, 366), 11, (74651904, 77403395, 75438085, 75307522, 74390020, 76419076, 75438337, 124659217, 75438865, 76419333, 124657932, 108857626, 75439116, 108926488, 73406721, 76418819, 124658960, 73407234, 109841689, 124658446, 108989446, 76419590, 124660245, 72222997, 124660502, 124659731, 72222483, 124660759, 124658703, 109975050, 124658189, 124659988, 124659474, 33554441, 33554443, 33554440, 33554439)),
    ((79, 95, 110, 126, 127, 367), 11, (73406469, 75435779, 73537537, 75435522, 75436036, 111023896, 108075289, 74319360, 110038555, 75368475, 75435265, 124723982, 78451481, 75371534, 107809306, 77466905, 76484888, 124724239, 124723468, 124723725, 124724496, 124724753)),
    ((125,), 2, (112989976, 112989721, 112988442, 75237913)),
    ((68, 96, 111), 4, (103030040, 68358936, 108990746, 108857113)),
    ((125,), 3, (109517336, 75237144, 79434520)),
    ((110, 120), 4, (101126936, 107158041, 75045145, 76418073)),
    ((102, 103, 117, 124), 3, (101059608, 101061913, 112987930, 111021083)),
    ((102, 107, 108, 126), 5, (102044696, 112922905, 107158298, 74717978, 112922651, 112923932, 75302426)),
    ((119, 120), 2, (102111000, 102109721, 101127706)),
    ((102, 120), 7, (73734147, 74848261, 75962369, 71768066, 74848512, 67571716, 103160600, 68490008, 101126681)),
    ((107, 137), 8, (74651649, 69801989, 73603075, 74914048, 74848772, 73865218, 101192472, 101193241, 107612954)),
    ((7, 8, 25, 36, 41, 57, 89, 105, 106, 107, 115, 122, 151, 215, 249, 377), 4, (110693400, 125379599, 76027151, 125379342, 125380884, 110957081, 125380627, 125378828, 125380113, 125381141, 125381398, 125379856, 125379085, 125380370, 125381655, 33554442, 33554441, 33554439, 33554440, 33554438, 33554443)),
    ((20, 24, 26, 41, 58, 74, 90, 104, 106, 107, 123, 124, 180, 246, 250, 378), 10, (72947712, 73996547, 74127618, 73997061, 113711384, 75041284, 72949016, 107612441, 125445135, 76225551, 75040513, 107682330, 107611931, 79433754, 79432728, 107612700, 125446420, 125444364, 74124820, 110760989, 125445649, 125445392, 125446163, 125444621, 125447191, 125446934, 125445906, 125444878, 125446677, 33554441, 33554442, 33554443, 33554439, 33554438, 33554440)),
    ((36, 37, 43, 59, 76, 89, 91, 106, 107, 108, 125, 138, 157, 185, 186, 379), 11, (71964933, 73930753, 74061828, 75106563, 73013762, 73931008, 107612184, 79367704, 125510414, 73931534, 110826009, 125511442, 74189842, 125509900, 76157452, 125512727, 74191127, 125510671, 76158223, 107678490, 125511185, 76158737, 125512470, 125512213, 125510157, 125511956, 125511699, 125510928, 33554443, 33554441, 33554439, 33554440, 33554442, 33554438)),
    ((42, 48, 50, 58, 60, 76, 90, 107, 108, 109, 112, 114, 141, 188, 380), 15, (75307269, 77207809, 75110400, 70064389, 73734404, 74193155, 79433218, 75110916, 74717699, 75308289, 116138008, 76286488, 77405186, 125575693, 74259725, 107743002, 107677721, 107677979, 112004616, 79434760, 125578006, 74256406, 125576721, 125576978, 74255378, 125577749, 125576207, 125576464, 125575950, 125578263, 125575436, 125577492, 125577235, 33554438, 33554441, 33554443, 33554439, 33554442)),
    ((32, 65, 67, 76, 93, 95, 109, 110, 113, 117, 124, 127, 140, 147, 157, 173, 381), 11, (74586113, 74192898, 74258432, 74127363, 72095749, 74455045, 74455300, 109845272, 108010009, 75172633, 110956827, 74189595, 107808794, 77403162, 77401112, 125643285, 72157461, 108726045, 110956572, 125640972, 125642000, 76289552, 125643542, 108729374, 125641229, 110957343, 74189340, 125642257, 125641743, 125643799, 125643028, 125642771, 125642514, 125641486, 33554441, 33554442, 33554438, 33554439, 33554440, 33554443)),
    ((78, 79, 80, 92, 94, 95, 110, 111, 142, 158, 382), 14, (74783232, 77467138, 74389761, 83761156, 74324483, 73472005, 77467395, 75438596, 125707536, 74259216, 77467909, 109779736, 107877657, 125707793, 74259473, 77336856, 125706508, 73603331, 76354060, 125708050, 73270802, 125707279, 125706765, 125707022, 125709078, 73271830, 74387478, 125709335, 74387735, 125708564, 73271316, 125708821, 125708307, 33554440, 33554438, 33554441, 33554442, 33554443, 33554439)),
    ((110, 111, 113, 126, 383), 10, (82712833, 74389509, 76421124, 74390274, 76421376, 76421891, 125772815, 73406991, 110958360, 74320143, 76484355, 125772558, 108863257, 76420110, 125773072, 74254105, 74320400, 108857882, 125772301, 108861211, 108859932, 125772044, 125773329)),
    ((129, 140, 141, 143), 3, (110172696, 78517528, 114036505, 114035994, 112069915)),
    ((142, 158, 159), 5, (112135193, 110434330, 80549658, 109905688, 75504408)),
    ((103, 143), 2, (101062424, 112072473)),
    ((157,), 2, (115085848, 80546840)),
    ((137, 140), 3, (101193496, 76024600, 114036761)),
    ((156, 158), 2, (114103065, 110823960)),
    ((67, 137, 154, 215), 3, (109578008, 113971994, 109843225, 109582107)),
    ((114, 119, 137, 138), 4, (101125400, 101257753, 112004378, 107678235)),
    ((36, 72, 121, 132, 134, 139, 151, 152, 153, 166, 168, 184, 185, 228, 232, 244, 248, 392), 8, (69736707, 67636738, 77010945, 69736961, 67637252, 69737728, 79108096, 73931269, 79108357, 110626584, 109709337, 110626842, 126363410, 126362896, 126363153, 126361868, 126363667, 126364181, 126364438, 126363924, 126362639, 126362382, 126362125, 126364695, 33554440, 33554441, 33554443, 33554438, 33554439, 33554442)),
    ((41, 56, 105, 138, 139, 151, 152, 154, 155, 169, 201, 231, 233, 393), 13, (75765765, 70850563, 77076482, 78125059, 75896833, 74979329, 79173888, 77011460, 74979588, 67637760, 109517080, 77137432, 101258009, 77137689, 126429460, 126427661, 77075213, 126428432, 77075984, 126428689, 126427918, 126428946, 126429974, 126427404, 126429717, 126430231, 126428175, 126429203, 33554441, 33554438, 33554439, 33554440, 33554443, 33554442)),
    ((40, 42, 104, 108, 123, 136, 139, 154, 155, 170, 186, 232, 236, 394), 13, (77011202, 73996292, 77273088, 76089603, 77273857, 77274117, 103357208, 77138200, 110758169, 126493454, 77141006, 110758683, 111939610, 75963162, 110757916, 79369754, 126495510, 75173910, 126493968, 111809309, 126494225, 77141777, 126493197, 126492940, 126494482, 126494739, 126493711, 126495253, 126495767, 126494996, 33554441, 33554442, 33554439, 33554440, 33554443, 33554438)),
    ((39, 41, 75, 90, 91, 101, 109, 122, 126, 140, 141, 154, 155, 157, 171, 173, 188, 235, 249, 395), 10, (76028162, 77207556, 76155139, 77208069, 77208320, 103488536, 77137944, 114102041, 77334809, 76154625, 111874074, 126558733, 77206285, 126559504, 109647132, 111875867, 77207056, 126558476, 77206028, 126560018, 126561046, 126559761, 126560275, 126561303, 126558990, 126559247, 126560532, 126560789, 33554443, 33554439, 33554442, 33554440, 33554441, 33554438)),
    ((66, 76, 86, 110, 124, 125, 134, 141, 142, 155, 156, 157, 170, 172, 236, 238, 253, 396), 18, (76355585, 76683266, 72030211, 77273602, 80482565, 77338880, 75766020, 76356100, 75503875, 76221189, 113055000, 110889753, 110823194, 81532697, 78515992, 126624526, 77405454, 126625040, 77405712, 107742747, 78385691, 113053706, 126626068, 72091668, 126624269, 77271821, 75304468, 126625297, 126626839, 126626582, 126626325, 126624783, 126624012, 126625554, 126625811, 33554441, 33554440, 33554438, 33554443, 33554439)),
    ((65, 67, 97, 109, 126, 129, 140, 145, 156, 173, 189, 239, 397), 12, (75241476, 77273346, 79370240, 77404163, 77338624, 82582533, 78388225, 77404677, 109058584, 76220184, 79498497, 76286211, 110822937, 109775386, 126689805, 77337357, 113054471, 126691090, 113055499, 126690062, 77337614, 126692118, 126690576, 126691604, 126690319, 126692375, 126691861, 126690833, 126691347, 126689548, 33554441, 33554442, 33554438, 33554440)),
    ((96, 98, 110, 115, 127, 143, 144, 158, 159, 174, 398), 11, (75569153, 76290051, 78515200, 77535236, 76617733, 79632642, 78515714, 111023640, 126756112, 77536272, 110954778, 111022617, 75367961, 126756369, 108923163, 126755855, 77468955, 112072202, 126757911, 74320663, 112071174, 111086855, 126757140, 74319892, 78516999, 126756883, 126755084, 74319635, 126756626, 126755341, 126757397, 126757654, 126755598, 33554443, 33554440, 33554441)),
    ((111, 127, 158, 159, 399), 11, (75503619, 77532674, 77469701, 76552193, 77532160, 75634949, 76417540, 103750168, 77400600, 77533188, 113120025, 77533445, 113120538, 126821391, 78581017, 126821134, 77468686, 78581530, 126821905, 126821648, 126820620, 126820877)),
    ((143, 159), 2, (109971224, 111019545)),
    ((128, 142, 158), 5, (111155736, 76352280, 113056537, 80548889, 111087386)),
    ((140,), 1, (114036248,)),
    ((158,), 2, (112006168, 75302936)),
    ((157,), 2, (115086360, 80547352)),
    ((129,), 1, (110955288,)),
    ((153,), 1, (110627608,)),
    ((136, 137, 138, 228), 4, (102175512, 109643801, 109578778, 108596507)),
    ((56, 88, 136, 137, 150, 153, 168, 184, 214, 408), 5, (101192728, 76023832, 102241802, 102241031, 127412500, 76090900, 127412757, 76091157, 127412243, 127413271, 127413014, 127411986, 33554438, 33554443, 33554440, 33554441)),
    ((40, 49, 55, 83, 105, 121, 137, 138, 139, 154, 185, 187, 232, 249, 409), 11, (77072900, 82385154, 76027905, 70916099, 76945413, 77071872, 80156673, 70851072, 67703045, 76028418, 71899395, 78126083, 127478036, 127475980, 127477008, 127476494, 127476237, 127476751, 127477265, 127478293, 127477522, 127477779, 127478550, 127478807, 33554442, 33554441, 33554438, 33554440, 33554439, 33554443)),
    ((56, 74, 86, 106, 122, 124, 138, 139, 155, 156, 186, 216, 248, 410), 10, (76158979, 76093440, 76224514, 69933572, 76093697, 73997317, 77138436, 109709848, 109451801, 109710106, 79432985, 109708827, 127542030, 78189582, 127543829, 76222229, 127542287, 127542801, 127542544, 127543315, 127541516, 127544086, 127541773, 127543058, 127544343, 127543572, 33554439, 33554441, 33554442, 33554443, 33554440, 33554438)),
    ((75, 89, 91, 123, 133, 138, 140, 141, 156, 157, 159, 187, 251, 411), 10, (74062080, 76159235, 77203201, 76159749, 76160002, 109643288, 77203972, 109643547, 113908761, 76285977, 109644572, 127607309, 76160269, 109774874, 127607566, 78255118, 79498777, 127608337, 78255889, 127608080, 78255632, 127608594, 76286994, 127609365, 127607823, 127607052, 127609108, 127608851, 127609879, 127609622, 33554440, 33554439, 33554438, 33554443, 33554441, 33554442)),
    ((76, 80, 82, 84, 92, 109, 126, 139, 140, 141, 157, 158, 188, 220, 235, 236, 252, 412), 13, (75831300, 76290561, 76355840, 77535747, 77404421, 77268994, 112007961, 80481305, 107743514, 127673616, 109839896, 78454032, 78386458, 127673359, 127674901, 76353301, 127675415, 127673873, 76353815, 127674130, 73139730, 76352530, 110761755, 127675158, 127673102, 127674387, 127672845, 127672588, 127674644, 33554439, 33554443, 33554441, 33554438, 33554442, 33554440)),
    ((81, 109, 110, 121, 124, 125, 127, 140, 141, 142, 143, 149, 156, 159, 172, 189, 413), 18, (76814338, 80547073, 76224771, 76290309, 77334273, 75700224, 78453252, 77469952, 113053464, 127738638, 78518798, 74188814, 127740437, 113053978, 74128149, 110824217, 108726300, 127738895, 108860187, 127739409, 78386961, 127740951, 74255127, 127740180, 110826525, 127738124, 110827038, 127739152, 127739923, 127740694, 127738381, 127739666, 33554442, 33554441, 33554439, 33554438, 33554440, 33554443)),
    ((111, 116, 126, 142, 143, 144, 157, 159, 190, 238, 254, 414), 11, (75569669, 76486660, 77535489, 79563776, 76617986, 76421635, 79564547, 75831553, 79564290, 127804174, 76748814, 109972248, 77536000, 79564804, 127804431, 113121035, 79565061, 127804945, 110888473, 127806230, 75368982, 76484630, 127806487, 127805202, 75369239, 76483602, 127805459, 75368211, 76483859, 127804688, 127803917, 127805973, 127805716, 127803660, 33554438, 33554440, 33554439, 33554441, 33554442)),
    ((142, 143, 145, 156, 158, 415), 11, (75569408, 78518274, 77466373, 78581764, 76486913, 76487171, 127869710, 78517262, 76552448, 127869196, 112008216, 76416524, 112073497, 127870224, 78516248, 110823706, 127870481, 77399833, 110954011, 110958108, 127869967, 127869453)),
    ((145, 175), 3, (112269592, 80614680, 114169625, 112070938)),
    ((174,), 1, (116200216,)),
    ((165, 175), 2, (114168600, 78513944, 114167833)),
    ((31,), 1, (105715480,)),
    ((69, 102), 3, (114628888, 67506456, 100930841)),
    ((172, 174, 190), 6, (111286552, 78977560, 78449176, 116201242, 79108634, 111871513)),
    ((7, 170), 3, (101322520, 68752664, 109581337)),
    ((86, 186, 187), 3, (101387544, 79042584, 111740441, 111743770)),
    ((8, 137, 153, 171), 4, (109578520, 101323801, 78252057, 109580315, 101324058, 110627100, 78252314)),
    ((20, 73, 154, 167, 170, 185, 186, 188, 201, 217, 248, 425), 4, (101389848, 79366680, 109646617, 128527383, 128527126, 128526869, 128526612, 128526355, 128526098, 33554439, 33554441, 33554440, 33554442, 33554443, 33554438)),
    ((14, 42, 58, 66, 70, 90, 138, 155, 168, 171, 184, 186, 202, 251, 426), 12, (79239169, 79304960, 80222213, 77993987, 81336322, 79239682, 83565316, 79239940, 67767553, 78186755, 112925464, 76156184, 101324555, 109842201, 128590092, 128590863, 128592405, 128592148, 128591377, 128591120, 128591634, 128590349, 128592919, 128590606, 128592662, 128591891, 33554439, 33554438, 33554440, 33554442, 33554441)),
    ((13, 73, 75, 87, 139, 165, 172, 173, 186, 187, 188, 203, 235, 237, 253, 427), 11, (79304704, 79173637, 73013249, 80353284, 78251777, 78125314, 78125571, 101388312, 101389337, 79366169, 128657170, 128656656, 79304208, 107680282, 128656399, 79303951, 109778203, 128657941, 128655885, 128658455, 128656913, 128655628, 128657684, 128658198, 128656142, 128657427, 33554439, 33554443, 33554440, 33554442, 33554441, 33554438)),
    ((100, 106, 108, 138, 140, 141, 156, 157, 174, 188, 189, 204, 236, 238, 252, 428), 11, (77928704, 79436036, 79370498, 78452995, 78317313, 78318341, 112986392, 112920857, 112986650, 128721678, 112985627, 81468686, 114037532, 115149830, 76285724, 128721164, 79368716, 115150087, 128722192, 128722963, 77401363, 128721421, 128723477, 128721935, 128723734, 128722706, 128722449, 128723991, 128723220, 33554442, 33554443, 33554441, 33554440)),
    ((97, 99, 107, 109, 111, 124, 135, 147, 156, 157, 159, 165, 172, 175, 188, 221, 237, 429), 11, (81467394, 79435776, 79501316, 81596163, 79436289, 79501573, 112920344, 114102298, 79437338, 111872281, 128786700, 79434252, 115151880, 109774363, 113055260, 76352028, 128789527, 111875613, 75303703, 128788499, 128787214, 128787471, 128789013, 128787985, 128786957, 128788756, 128788242, 128789270, 128787728, 33554439, 33554442, 33554438, 33554441, 33554443)),
    ((128, 130, 140, 142, 157, 159, 160, 162, 190, 191, 206, 222, 430), 14, (77928452, 80613123, 78583810, 79632384, 78714881, 81730053, 78584321, 80612352, 128852236, 79499788, 111220761, 81661209, 113120280, 78649858, 80613637, 79496985, 128852750, 114169354, 79630346, 114168326, 128854292, 76417044, 128854549, 111940634, 76417301, 128853007, 113118491, 128854806, 128853264, 128855063, 128853778, 128853521, 128854035, 128852493, 33554440, 33554439, 33554441, 33554443)),
    ((129, 143, 159, 174, 190, 191, 431), 9, (77600771, 79566852, 79629312, 81664514, 77601029, 79630597, 77731841, 79629826, 112003096, 79629569, 114301977, 112002842, 128918800, 80677913, 79566352, 128917772, 114232604, 112002587, 79565324, 128918029, 128918286, 128918543, 128919057)),
    ((174, 191, 223), 3, (117314328, 115217945, 114167322)),
    ((160, 174), 2, (115151640, 113184537)),
    ((189, 190, 195), 2, (112986136, 115217177, 115215130)),
    ((4,), 1, (100861976,)),
    ((21,), 1, (108663320,)),
    ((165, 185, 190), 4, (113318424, 79497496, 102306585, 115152410)),
    ((167,), 1, (112854808,)),
    ((136, 165), 2, (102175256, 102176537, 113052442)),
    ((137, 171, 231), 3, (111807256, 109577753, 110630682)),
    ((23, 41, 170, 189, 224), 6, (112531736, 78186264, 111740954, 111741467, 110693913, 108729116, 116200478, 109579549)),
    ((43, 58, 86, 88, 170, 171, 182, 187, 188, 202, 216, 218, 442), 13, (103422488, 78251544, 101321753, 78059801, 101388555, 108727578, 68818699, 76157722, 111744795, 77205787, 113972252, 129640210, 78318610, 129640724, 78319124, 129641238, 129640981, 129641495, 129640467, 33554442, 33554440, 33554441, 33554439, 33554438)),
    ((57, 83, 100, 106, 107, 117, 123, 138, 141, 169, 170, 171, 172, 173, 189, 219, 251, 253, 443), 12, (78059521, 78321668, 80418819, 79301381, 81271296, 79301124, 67833346, 79300610, 80354051, 111872025, 113052696, 129704204, 74057228, 129704718, 110695195, 129705489, 129706774, 110827290, 129705232, 129706003, 129707031, 129706517, 129705746, 129704461, 129704975, 129706260, 33554441, 33554439, 33554442, 33554443, 33554440, 33554438)),
    ((60, 107, 112, 114, 116, 122, 124, 154, 172, 173, 178, 189, 190, 220, 444), 13, (82515968, 78190596, 78387459, 78452737, 80288005, 78321922, 82516739, 111937048, 79501829, 111872537, 82517249, 111937306, 129770254, 79305742, 108793627, 78322459, 108792860, 76223004, 114102813, 110889502, 129769997, 129772567, 78450967, 129772310, 78450710, 129770768, 129771282, 129771539, 129769740, 129772053, 129771796, 129770511, 129771025, 33554443, 33554441, 33554442, 33554438, 33554439, 33554440)),
    ((140, 141, 145, 155, 157, 173, 174, 181, 183, 187, 188, 190, 191, 445), 11, (78780418, 81533441, 78387203, 79432453, 78387716, 78387968, 115150872, 78383640, 115151129, 78383897, 112795144, 112921370, 129835533, 129836047, 80483599, 129837589, 129835276, 76351765, 80482828, 129836818, 76350994, 129836561, 129837332, 76351508, 110954523, 129835790, 129837846, 129836304, 129837075, 129838103, 33554441, 33554439, 33554438, 33554442, 33554443)),
    ((143, 158, 174, 175, 191, 207, 208, 222, 446), 12, (78977027, 78518529, 79497218, 81660928, 77928965, 79632900, 81662213, 79633152, 112069144, 81661442, 129900812, 79437068, 112335111, 81661699, 78584839, 129901583, 80549135, 81661956, 129901326, 129901840, 129902868, 77465620, 78581268, 129902097, 129902611, 77465363, 129903639, 78582039, 129903125, 77465877, 129903382, 77466134, 129902354, 129901069, 33554441, 33554440, 33554442, 33554438, 33554443)),
    ((142, 174, 175, 177, 190, 447), 11, (80615941, 79562497, 81663235, 78584064, 78649604, 80678402, 129966348, 78513676, 112139032, 81596952, 129967633, 129966862, 113054745, 116200986, 129966605, 113051163, 79497754, 129967376, 129967119)),
    ((1, 222, 239), 4, (100668184, 101585945, 101455386, 82708505)),
    ((181, 206, 208), 3, (114099992, 116330265, 116200730)),
    ((3, 207, 223), 3, (100796952, 114497561, 82711833, 116265498)),
    ((206, 223), 3, (112335384, 83760920, 101520921)),
    ((), 0, ()),
    ((206, 222), 4, (114497816, 80546072, 114629401, 67965721)),
    ((), 0, ()),
    ((122, 153), 2, (101256472, 113971737)),
    ((170,), 3, (114891032, 67768600, 68753176)),
    ((24, 188, 204, 216), 4, (101390105, 113969176, 109647642, 111744283)),
    ((155, 171, 187, 205), 5, (101324312, 101454361, 80479769, 112855323, 114034714, 78252568, 114037788)),
    ((45, 61, 84, 101, 134, 186, 187, 199, 201, 204, 219, 220, 221, 459), 4, (117053976, 67833624, 111875097, 130755607, 130755350, 130754836, 130754322, 130755093, 130754579, 33554443, 33554441, 33554439, 33554442, 33554438, 33554440)),
    ((128, 132, 140, 146, 156, 172, 189, 202, 205, 219, 220, 221, 222, 236, 460), 10, (83564546, 80615424, 81533185, 81598467, 80287746, 67899653, 81467908, 67899396, 81468160, 115083288, 80415493, 130819601, 101455627, 115082777, 101454599, 111937818, 111937563, 130818316, 130820115, 130820629, 130819087, 130821143, 130818830, 130819858, 130820372, 130818573, 130820886, 130819344, 33554441, 33554438, 33554442, 33554440)),
    ((47, 62, 129, 131, 133, 139, 145, 148, 157, 173, 188, 190, 193, 197, 207, 220, 221, 222, 223, 237, 461), 11, (81664004, 81532929, 80353536, 68950531, 80481029, 80747010, 81533699, 80353794, 101518360, 117185305, 130884109, 81402125, 67965209, 101519131, 107811610, 130884880, 130884623, 81532175, 81532432, 130886165, 130886679, 130885394, 130885651, 130885908, 130883852, 130884366, 130886422, 130885137, 33554442, 33554443, 33554440, 33554439, 33554441, 33554438)),
    ((160, 162, 174, 176, 191, 204, 207, 221, 222, 223, 238, 462), 12, (80025603, 81729536, 81664258, 82710789, 79763457, 81729797, 80681220, 82709761, 82710532, 101452824, 113449241, 81594905, 130950159, 115218202, 80747290, 81597711, 115149595, 130949388, 116265735, 130950673, 130951701, 78514453, 116265992, 130952215, 130951444, 78514967, 130951187, 130951958, 130949902, 130950930, 130950416, 130949645, 33554438, 33554443, 33554441, 33554442)),
    ((175, 191, 206, 222, 223, 463), 12, (79829251, 83826693, 81726464, 81795844, 81726978, 80611073, 81727492, 117314584, 114100761, 81726721, 82775576, 131015438, 79562766, 81662990, 116199962, 131014924, 81662476, 131015695, 131016209, 131015181, 131015952)),
    ((175, 205, 206, 222, 223), 7, (114629145, 67965465, 113318168, 81660184, 80878360, 101454874, 113117979, 113116700)),
    ((1,), 1, (101779224,)),
    ((5, 19, 208, 255), 4, (100928024, 101845529, 117314843, 116266778)),
    ((194, 197), 2, (115281688, 116264729)),
    ((19, 21), 2, (101845016, 101976345)),
    ((22, 164, 197, 208), 2, (102042392, 102045465, 115148314, 115148571)),
    ((23, 25, 216), 4, (102238488, 77075736, 102107161, 102503706)),
    ((9,), 2, (109452056, 75043096)),
    ((58, 187, 221, 253), 8, (114694680, 81529112, 114956314, 67832858, 110759705, 80288537, 68817434, 112858907)),
    ((170, 200), 3, (101322264, 68752408, 111741721)),
    ((205, 216, 235), 2, (112854552, 115086105, 112857882)),
    ((172, 173, 204, 220, 221), 6, (101518873, 113969690, 114039576, 113968667, 81595928, 102437660, 112923677)),
    ((131, 140, 148, 189, 204, 205, 216, 218, 221, 250, 252, 476), 9, (114034456, 115022873, 67898649, 114034971, 80414489, 102503432, 112985882, 131869719, 80548119, 131868948, 77334548, 131868434, 131869205, 131868691, 131869462, 33554441, 33554439, 33554442, 33554438, 33554443)),
    ((172, 173, 177, 181, 189, 191, 204, 206, 213, 219, 223, 241, 253, 477), 13, (81270787, 83499012, 80549888, 80484354, 81467650, 67964161, 80550149, 80484608, 101453592, 80415000, 80550659, 68883736, 131933199, 80484879, 81528577, 131933456, 131933970, 131933713, 131934741, 78448917, 131934227, 80612627, 131932942, 131935255, 78449431, 131934484, 131932428, 131932685, 131934998, 33554442, 33554443, 33554441, 33554438, 33554440, 33554439)),
    ((174, 175, 176, 178, 190, 191, 205, 206, 207, 208, 223, 254, 478), 15, (81860866, 80746752, 80615684, 82647299, 80025857, 80616197, 83630597, 113252888, 116264473, 131997964, 80681484, 80480792, 117315082, 131999249, 80545817, 112068634, 80614426, 131998478, 132000277, 80678677, 131998735, 79563029, 132000791, 80679191, 131998992, 131998221, 132000534, 79563286, 80678934, 132000020, 131999763, 131999506, 33554441, 33554440, 33554439, 33554443, 33554438)),
    ((174, 206, 207, 211, 255, 479), 13, (80746499, 78649345, 81660420, 82775040, 79894533, 80680962, 116202008, 132063500, 79829516, 80610828, 82709528, 132064014, 80611342, 114101017, 132064528, 115152666, 132063757, 132064785, 80612113, 132064271)),
    ((17, 44, 207, 239), 4, (101716505, 112794648, 74190104, 116262426, 116266523)),
    ((2, 222, 255), 4, (100730904, 100731418, 116464153, 101649947, 67965977)),
    ((3, 45, 81), 2, (100797208, 100796185, 100798747, 107745818)),
    ((2, 4), 2, (100862232, 100730393)),
    ((5, 9), 4, (100928280, 110566169, 67634969, 76026649)),
    ((6, 30, 86, 244, 255), 5, (116857112, 72159768, 100996122, 107681051, 100993049, 116197148)),
    ((7, 10, 23), 4, (107552024, 101058073, 74058776, 101058586, 102106907)),
    ((6, 25), 3, (112728600, 76091672, 100993817)),
    ((24, 42, 241), 4, (109711128, 77141272, 109579801, 116197914)),
    ((25, 26, 153, 250), 6, (116791832, 83434264, 76092440, 101256729, 116923418, 76091418, 109646363, 68748827)),
    ((10, 11), 3, (107614489, 116137752, 74061336, 107616026, 67767066, 107615003, 67766043)),
    ((59, 91, 188, 238, 255), 7, (117120024, 67834392, 110893850, 114956825, 101389595, 76222746, 101389085, 78318873, 116197404, 116198174)),
    ((42, 93, 109, 124, 141, 234, 238, 255), 12, (117311257, 101583899, 116988952, 76156952, 83696667, 116197662, 110891546, 69014814, 109841180, 101321247, 111941149, 80484124, 114038304)),
    ((61, 161, 165, 185, 191, 193, 207, 222, 223, 229, 232, 235, 236, 252, 253, 254, 493), 7, (107810072, 117251353, 67966233, 111875355, 114099738, 112006684, 132983574, 132983831, 132982546, 132982803, 132983317, 132983060, 33554441, 33554438, 33554440, 33554443, 33554442, 33554439)),
    ((14, 93, 108, 127, 192, 194, 206, 210, 211, 222, 223, 224, 239, 254, 255, 494), 13, (82909444, 83826945, 82582272, 68029954, 82844165, 83827205, 82583043, 68029697, 117311512, 133047825, 82516994, 68030211, 133046797, 83696386, 111022873, 133047568, 101585671, 83823879, 111939354, 133047054, 101585414, 109842971, 83823622, 133048853, 133046540, 80611605, 133048339, 117379082, 133049110, 80611862, 133048596, 133048082, 133047311, 133049367, 33554443, 33554440, 33554441)),
    ((13, 14, 79, 193, 207, 223, 254, 255, 495), 12, (81795584, 79698178, 69081093, 83824387, 83761412, 82708225, 83824130, 101650201, 83171845, 133112076, 101517080, 83759628, 101649690, 109909019, 107680540, 133112590, 133112847, 133113104, 133112333, 133113361)),
    ((1, 238, 255), 3, (117311000, 100668441, 101585178)),
    ((18, 225, 238), 5, (101779480, 115874329, 68030489, 69015065, 115148826)),
    ((19,), 1, (101844760, 101845785)),
    ((4, 20), 2, (100861464, 101910809, 101910042)),
    ((6, 8, 21, 28), 6, (116988440, 82123544, 73142040, 100993562, 109580057, 101976603)),
    ((22, 239), 2, (102041112, 102041625, 117379354)),
    ((23, 27, 233), 3, (108663832, 68814872, 102107673, 108662298)),
    ((24, 229), 2, (102172440, 102565401)),
    ((8, 9, 58, 233, 255), 5, (109580568, 109581850, 117311769, 110759963, 78190107, 102238748)),
    ((9, 59, 233, 236, 244), 5, (109776152, 108596249, 102303771, 102435098, 110695964)),
    ((26, 203, 221), 5, (115940121, 75107353, 102503960, 81529368, 102372634)),
    ((75, 76, 170, 204, 235), 6, (102437912, 111810841, 77272345, 101322779, 68752923, 111809050, 77270042, 112920092)),
    ((92, 109, 205, 222), 6, (116202264, 77336344, 111940377, 101521178, 102504219, 81529627)),
    ((15, 76, 91, 236, 237, 238), 8, (114826009, 112925210, 102699288, 76288282, 102568987, 78319897, 102568476, 82642460, 115149085)),
    ((30, 126, 176, 195, 207, 210, 222, 236, 238, 239, 240, 248, 255, 510), 8, (102635275, 101586457, 82709017, 116202520, 77467672, 102634504, 134097686, 82776086, 102634247, 134097172, 81659924, 134096915, 82775315, 102633990, 134096658, 81659667, 134097943, 81659410, 82776343, 134097429, 33554441, 33554442)),
    ((95, 207, 238, 239, 245, 511), 16, (82843648, 82581761, 68096004, 83757829, 82712578, 81861378, 83368195, 68094976, 82778371, 82778625, 115678233, 69014297, 114432536, 134161423, 116071962, 68031759, 81727768, 69015322, 134161166, 107877403, 134160909, 134161937, 134160652, 134161680)),
)

LEFT, RIGHT0, RIGHT1 = CHUNKS, 2 * CHUNKS, 3 * CHUNKS
SIZE = 384 // CHUNKS
MAX_SENDS = max(len(p[2]) for p in PLAN)
MAX_FROM = max(1, max(len(p[0]) for p in PLAN))
MESH = pl.DeviceIdType.MESH


def nt_dot(left, right):
    return lax.dot_general(left, right, (((1,), (1,)), ((), ())), preferred_element_type=jnp.float32)


def choose(index, low, high, leaf):
    if all(PLAN[i] == PLAN[low] for i in range(low, high)):
        leaf(PLAN[low])
        return
    middle = (low + high) // 2

    @pl.when(index < middle)
    def _():
        choose(index, low, middle, leaf)

    @pl.when(index >= middle)
    def _():
        choose(index, middle, high, leaf)


def kernel(upper_ref, mask_hbm, out_ref, buf, acc, mask_ref, table, origin, count, in_sem, send_sem, recv_sem):
    brow, column = lax.axis_index("brow"), lax.axis_index("bcol")
    row, half = brow // 2, brow % 2
    own = buf.at[pl.ds(0, 384)]
    load = pltpu.make_async_copy(upper_ref, own, in_sem.at[0])
    load.start()
    load_mask = pltpu.make_async_copy(mask_hbm, mask_ref, in_sem.at[1])
    load_mask.start()

    def leaf(plan):
        origins, targets, sends = plan
        count[0] = len(origins)
        count[1] = targets
        count[2] = len(sends)
        for i, v in enumerate(origins):
            origin[i] = v
        for i, v in enumerate(sends):
            table[i] = v

    choose(row * 16 + column, 0, 256, leaf)
    sends = count[2]
    barrier = pltpu.get_barrier_semaphore()

    @pl.loop(0, count[0])
    def _(i):
        v = origin[i]
        there = ((v >> 4) & 15) * 2 + (half ^ (v >> 8))
        pl.semaphore_signal(barrier, inc=1, device_id=(there, v & 15), device_id_type=MESH)

    load_mask.wait()
    load.wait()
    for i in range(3):
        for j in range(6):
            keep = mask_ref[i, j].astype(jnp.float32)
            at = (pl.ds(i * 128, 128), pl.ds(j * 128, 128))
            buf[at] = (buf[at].astype(jnp.float32) * keep).astype(jnp.bfloat16)

    @pl.when(count[1] > 0)
    def _():
        pl.semaphore_wait(barrier, count[1])

    def slot(index):
        return buf.at[pl.ds(pl.multiple_of(index * SIZE, SIZE), SIZE)]

    def copy(v, i):
        there = ((v >> 20) & 15) * 2 + (half ^ ((v >> 24) & 1))
        return pltpu.make_async_remote_copy(
            src_ref=slot(v & 255),
            dst_ref=slot((v >> 8) & 255),
            send_sem=send_sem.at[i],
            recv_sem=recv_sem.at[(v >> 8) & 255],
            device_id=(there, (v >> 16) & 15),
            device_id_type=MESH,
        )

    def arrived(index):
        pltpu.make_async_copy(slot(index), slot(index), recv_sem.at[index]).wait()

    @pl.loop(0, sends)
    def _(i):
        v = table[i]

        @pl.when((v & (1 << 25)) != 0)
        def _():
            arrived(v & 255)

        @pl.when((v & (1 << 26)) != 0)
        def _():
            copy(v, i).start()

    has0 = (row == 0) | ((column >= row) & (row + column >= 16))
    has1 = (column < 15) & ((row <= 1) | ((column + 1 >= row) & (row + column >= 16)))
    here = pl.ds(pl.multiple_of(half * 384, 128), 384)
    other = pl.ds(pl.multiple_of(384 - half * 384, 128), 384)

    def rows(index):
        return buf[pl.ds(pl.multiple_of(index * SIZE, SIZE), 384), :]

    @pl.when(has0)
    def _():
        right = jnp.where(row + column == 0, 0, RIGHT0)
        acc[:, here] = nt_dot(rows(0), rows(right))

        @pl.loop(0, CHUNKS)
        def _(j):
            arrived(SIB + j)

        acc[:, other] = nt_dot(rows(0), rows(SIB))

    @pl.when(has1)
    def _():
        left = jnp.where(column == 0, RIGHT1, LEFT)
        for columns, right in ((here, RIGHT1), (other, SIB + CHUNKS)):
            if right != RIGHT1:

                @pl.loop(0, CHUNKS)
                def _(j):
                    arrived(SIB + CHUNKS + j)

            term = nt_dot(rows(left), rows(right))

            @pl.when(has0)
            def _():
                out_ref[:, columns] = (acc[:, columns] + term).astype(jnp.bfloat16)

            @pl.when(jnp.logical_not(has0))
            def _():
                out_ref[:, columns] = term.astype(jnp.bfloat16)

    @pl.when(has0 & jnp.logical_not(has1))
    def _():
        out_ref[...] = acc[...].astype(jnp.bfloat16)

    @pl.when(jnp.logical_not(has0 | has1))
    def _():
        out_ref[...] = jnp.zeros_like(out_ref)

    @pl.loop(0, sends)
    def _(i):
        v = table[i]

        @pl.when((v & (1 << 26)) != 0)
        def _():
            copy(v, i).wait_send()


def per_device(upper_store, block_mask):
    return pl.pallas_call(
        kernel,
        out_shape=jax.ShapeDtypeStruct((384, 768), jnp.bfloat16),
        in_specs=[pl.BlockSpec(memory_space=pl.ANY)] * 2,
        out_specs=pl.BlockSpec(memory_space=pltpu.VMEM),
        scratch_shapes=[
            pltpu.VMEM((SLOTS * SIZE, 768), jnp.bfloat16),
            pltpu.VMEM((384, 768), jnp.float32),
            pltpu.SMEM((3, 6), jnp.int32),
            pltpu.SMEM((MAX_SENDS,), jnp.int32),
            pltpu.SMEM((MAX_FROM,), jnp.int32),
            pltpu.SMEM((3,), jnp.int32),
            pltpu.SemaphoreType.DMA((2,)),
            pltpu.SemaphoreType.DMA((MAX_SENDS,)),
            pltpu.SemaphoreType.DMA((SLOTS,)),
        ],
        compiler_params=pltpu.CompilerParams(
            collective_id=0, has_side_effects=True, vmem_limit_bytes=60 * 2**20
        ),
        name="cannon_steps",
    )(upper_store, block_mask)


def solution(mesh):
    spec = P("brow", "bcol")
    return jax.shard_map(per_device, mesh=mesh, in_specs=(spec, spec), out_specs=spec, check_vma=False)
```

time: 205 us -> 39.1 us (0.19)
  the two profiles are of different devices: /device:TPU:223 before, /device:TPU:430 now
where the time goes in v4:
time: 39.1 us; the launch traced here: 38.9 us
  Pallas kernels  37 us (95%)
  local copies, waits for them, and re-layouts  1.92 us (5%)
    pallas_call x1, Pallas kernels, per_device(): pl.pallas_call(kernel, out_shape=jax.ShapeDtypeStruct((384, 768), jnp.bfl...  37 us
    unnamed x1, local copies, waits for them, and re-layouts  1.92 us

profile of v4, /device:TPU:430, one launch (start us, length us, event | category | flops | bytes accessed | tf_op | source)
XLA Modules:
  0.0 38.9 jit_solution(15268833703611186239)
XLA Ops:
  0.0 37.0 %cannon_steps.1 = bf16[384,768]{1,0:T(8,128)(2,1)} custom-call(bf16[384,768]{1,0:T(8,128)(2,1)} %upper_ref.1, s32[3,6]{1,0:T(4,128)} %mask_hbm.1), custom_call_target="tpu_custom_call" | custom-call | tf_op jit(solution)/shard_map/cannon_steps/pallas_call | solution.py:423
  37.0 1.9 %copy.4 = bf16[384,768]{1,0:T(8,128)(2,1)} copy(bf16[384,768]{1,0:T(8,128)(2,1)} %cannon_steps.1) | data formatting | bytes 1179648

commit v5 on v4

v5 whole, which is shorter than its diff:
```python
import jax
import jax.numpy as jnp
from jax import lax
from jax.experimental import pallas as pl
from jax.experimental.pallas import tpu as pltpu
from jax.sharding import PartitionSpec as P

CHUNKS = 6
SLOTS = 45
SIB = 33
PLAN = (
    ((1, 14, 16, 31, 32, 192, 240, 256), 5, (83894528, 83894785, 83895042, 83895299, 83895556, 83895813, 134217728, 102630936, 104799001, 117451799, 70127641, 117450514, 117451542, 117451285, 103682842, 117450771, 103683099, 117451028, 68028443)),
    ((2, 3, 13, 14, 15, 17, 18, 33, 225, 227, 257), 10, (79697921, 69212419, 117516307, 68163588, 67114757, 80812051, 82843906, 117515793, 68163345, 117516050, 68224530, 67113472, 117515279, 68162831, 117515536, 68163088, 117517078, 104665112, 117517335, 68225815, 101517849, 117515022, 68162574, 117516821, 117514508, 117516564, 117514765, 134217728, 33554439, 33554443, 33554440, 33554441, 33554442, 33554438)),
    ((3, 12, 17, 18, 19, 32, 34, 35, 48, 53, 64, 194, 226, 258), 9, (117580301, 68227853, 69278723, 81860610, 117580558, 68294917, 67176193, 68228110, 81861124, 101845272, 81991936, 106371353, 72093721, 117580815, 68228367, 117582100, 117581072, 117582614, 117581586, 117581843, 117581329, 117580044, 117582871, 117582357, 134217728, 33554438, 33554441, 33554440, 33554442, 33554443, 33554439)),
    ((5, 6, 18, 20, 21, 33, 35, 37, 39, 50, 53, 179, 227, 243, 259), 8, (79828996, 68294658, 67241472, 81926149, 67242243, 81926401, 101914648, 67180056, 117645837, 68293389, 117646608, 117645580, 100992537, 117646351, 68293132, 117648407, 117647122, 68293903, 117647379, 117646865, 117647636, 117648150, 117647893, 117646094, 134217728, 33554442, 33554439, 33554441, 33554440, 33554438, 33554443)),
    ((5, 19, 20, 21, 34, 36, 64, 66, 68, 82, 84, 85, 164, 210, 228, 260), 8, (78845954, 68425985, 68491268, 81991683, 67442949, 83040256, 101976856, 101910553, 117711630, 101975578, 68359182, 117711116, 101910299, 117711887, 117713686, 117712401, 117713172, 117712658, 117712915, 117713943, 117712144, 117713429, 117711373, 134217728, 33554441, 33554440, 33554438, 33554443, 33554439, 33554442)),
    ((3, 4, 20, 21, 22, 23, 37, 39, 65, 67, 69, 71, 83, 85, 229, 231, 244, 261), 8, (80877572, 69474560, 68425729, 67373315, 82057221, 67373058, 102041368, 117776909, 68424461, 117777423, 68424975, 102041882, 100862745, 117777937, 68425489, 117777166, 117777680, 117778965, 117778708, 117779479, 117776652, 117778451, 117778194, 117779222, 134217728, 33554438, 33554441, 33554439, 33554442, 33554443, 33554440)),
    ((7, 12, 21, 22, 23, 38, 87, 102, 116, 130, 164, 230, 262), 11, (67311872, 83106308, 68491779, 117843216, 68490768, 68622849, 82123010, 117842959, 68490511, 82254085, 102106649, 103488792, 102107418, 72092952, 102107931, 73077528, 117843987, 117842188, 68489740, 117844758, 117843473, 117843730, 117844244, 117844501, 117845015, 117842445, 117842702, 134217728, 33554441, 33554438, 33554440, 33554442, 33554439, 33554443)),
    ((9, 22, 23, 24, 25, 39, 41, 71, 99, 101, 103, 115, 118, 119, 135, 263), 8, (69605892, 82188544, 68556801, 67504387, 82188802, 68557061, 111548696, 75042328, 102172953, 117908752, 68556304, 117908238, 68555790, 117910551, 117907981, 68555533, 117908495, 117909523, 117910037, 117910294, 117909266, 117909009, 117909780, 117907724, 134217728, 33554439, 33554440, 33554441, 33554443, 33554442, 33554438)),
    ((10, 24, 25, 40, 56, 57, 72, 104, 120, 132, 136, 137, 152, 228, 264), 13, (68622593, 68687874, 83106051, 69475072, 68753667, 68688645, 83367941, 69671684, 105520152, 67700760, 78125828, 69802240, 75043864, 117973774, 68621326, 102237977, 117974288, 68621840, 102239002, 117974031, 68621583, 117974802, 117973517, 117975316, 117975573, 117975059, 117976087, 117974545, 117975830, 117973260, 134217728, 33554441, 33554440, 33554438, 33554443, 33554442, 33554439)),
    ((8, 11, 24, 26, 27, 41, 43, 57, 73, 105, 135, 137, 153, 199, 233, 265), 13, (82057473, 67573762, 68753411, 71833600, 68688130, 81205253, 69737477, 83368452, 70785284, 83433728, 70851844, 102173208, 118040081, 68687633, 118039310, 68686862, 102304537, 118041366, 118039567, 118039053, 118040595, 118041623, 118039824, 118041109, 118040852, 118038796, 118040338, 134217728, 33554439, 33554442, 33554440, 33554443, 33554441, 33554438)),
    ((12, 26, 27, 29, 42, 90, 166, 168, 170, 186, 200, 202, 217, 234, 236, 251, 266), 15, (82188288, 69736451, 67639298, 68818945, 68884484, 82450693, 69475332, 67836421, 68885251, 74059009, 67836672, 102369560, 103488281, 102303514, 102368795, 70983193, 72093465, 118104589, 118106902, 118104332, 68751884, 118105617, 101452572, 118104846, 118106131, 118106388, 118105360, 118105103, 118105874, 118106645, 118107159, 134217728, 33554438, 33554441, 33554443, 33554439, 33554442, 33554440)),
    ((10, 13, 27, 28, 29, 43, 167, 169, 171, 186, 187, 201, 203, 216, 235, 267), 12, (69605634, 68622339, 82450436, 68884736, 69015813, 68819203, 70982145, 82450949, 107679001, 68814617, 82451201, 105716248, 68880920, 101255962, 104664092, 101254683, 118170382, 68817934, 118170896, 68818448, 118171410, 118170125, 68817677, 118170639, 118172438, 118171153, 118171924, 118172695, 118169868, 118172181, 118171667, 134217728, 33554440, 33554438, 33554442, 33554443, 33554441, 33554439)),
    ((10, 13, 27, 28, 29, 44, 192, 202, 204, 206, 208, 220, 221, 268), 10, (67246340, 67508225, 70981888, 68950274, 69015552, 67770627, 72093186, 69016068, 68885509, 72093957, 102500376, 102500121, 118236689, 69016593, 118236432, 68883984, 105648903, 71109895, 118235404, 118236175, 68882956, 118235661, 118238231, 118236946, 118237717, 118237460, 118235918, 118237203, 118237974, 134217728, 33554442, 33554441, 33554438, 33554443, 33554440)),
    ((1, 15, 28, 29, 30, 45, 195, 197, 205, 208, 219, 221, 225, 237, 239, 252, 269), 14, (68884995, 67180548, 71047938, 68950788, 69016325, 104208664, 67836928, 68879896, 69998592, 67897089, 78322200, 105713689, 68819737, 116333595, 102566170, 68880155, 118301197, 68948749, 118300940, 68948492, 118302482, 118303253, 118301454, 118303767, 118302225, 118301711, 118302996, 118302739, 118301968, 118303510, 134217728, 33554440, 33554443, 33554442, 33554439, 33554441, 33554438)),
    ((0, 15, 30, 31, 46, 74, 192, 236, 238, 240, 241, 254, 255, 270), 11, (67115268, 71111939, 68099074, 82778113, 69146880, 67180804, 70126592, 68099333, 102631192, 70127877, 100669959, 69143815, 70126849, 118366990, 111808793, 118366733, 103683594, 69144586, 118367247, 103683337, 69144329, 118369303, 82709271, 118366476, 118367504, 118369046, 118368275, 118368789, 82708757, 118367761, 118368532, 134217728, 118368018, 33554443, 33554440, 33554438)),
    ((14, 17, 29, 30, 225, 239, 255, 271), 14, (69212928, 68229125, 68028161, 83695621, 69144066, 103095322, 69011482, 68028932, 105713177, 68028675, 101517340, 100731931, 71179036, 69143552, 101518109, 100732184, 71111708, 118433040, 69080592, 118432012, 118432783, 69080335, 118432526, 118432269, 118433297, 134217728)),
    ((1, 30, 48, 62, 224, 272), 5, (100668952, 104930585, 71176217, 106827034, 118500375, 104729627, 118499090, 118499861, 118500118, 118499347, 118499604)),
    ((1, 2, 15, 18, 19, 48, 49, 81, 209, 241, 273), 7, (70260993, 81795328, 67178757, 68098049, 67178243, 68098816, 67178500, 100734217, 67177986, 103683864, 118564883, 100733960, 118565140, 118564626, 67243026, 118565654, 118565911, 118565397, 33554438, 33554442, 33554443, 33554439)),
    ((2, 3, 19, 48, 50, 80, 210, 212, 242, 274), 7, (67179265, 69277957, 82909186, 67311620, 68225283, 67179008, 100796440, 100731673, 118630676, 67309076, 118630419, 118631190, 118630162, 118631447, 118630933, 33554438, 33554441, 33554440, 33554442, 33554439, 33554443)),
    ((3, 4, 20, 35, 49, 51, 113, 243, 275), 8, (81008642, 68290048, 67246083, 80877828, 82974721, 82974981, 101779992, 118696726, 67375126, 118695955, 118695698, 118696212, 118696469, 118696983, 33554443, 33554442, 33554440, 33554441, 33554438, 33554439)),
    ((4, 5, 21, 26, 28, 36, 52, 82, 212, 244, 276), 11, (83040515, 67377410, 68356869, 100927256, 100861721, 83040768, 67377921, 68356612, 105192218, 68623130, 73142554, 118762262, 111745307, 67440662, 118761234, 75107611, 118761491, 67439634, 118762005, 118762519, 118761748, 33554440, 33554443, 33554439, 33554438, 33554441, 33554442)),
    ((4, 5, 6, 27, 51, 117, 119, 213, 245, 277), 11, (81008899, 70522881, 67377157, 68421634, 100862488, 83106564, 67377664, 112465945, 74124313, 100993306, 118827798, 118827284, 67505684, 118827027, 118827541, 118828055, 118826770, 33554439, 33554442, 33554443, 33554441, 33554438, 33554440)),
    ((6, 7, 54, 118, 214, 230, 246, 278), 7, (70457604, 81074181, 67442689, 83171328, 67443203, 83171586, 101058328, 101059353, 118893591, 67571991, 118892306, 118893334, 67570706, 118892820, 118893077, 118892563, 33554438, 33554441, 33554440, 33554443, 33554442, 33554439)),
    ((6, 7, 8, 9, 11, 20, 55, 57, 151, 183, 247, 279), 10, (81139970, 67508480, 82189057, 67508739, 83237124, 112794905, 67569433, 67508997, 100992794, 106630936, 102435611, 118958099, 118958356, 118958870, 118957842, 118958613, 118959127, 33554441, 33554442, 33554443, 33554439, 33554440, 33554438)),
    ((8, 9, 26, 56, 57, 58, 88, 152, 214, 248, 280), 10, (70719493, 67574019, 83302401, 67704836, 70719744, 70851586, 115874072, 67569688, 101189657, 101124891, 113842714, 75108634, 67705114, 119024406, 67702806, 119024663, 119024149, 119023378, 119023635, 119023892, 33554439, 33554440, 33554443, 33554441, 33554438, 33554442)),
    ((8, 9, 10, 57, 59, 166, 181, 200, 217, 233, 249, 251, 281), 10, (81139715, 72882178, 67639553, 82253829, 73996801, 67639813, 82385412, 70785536, 108597016, 67635480, 101124377, 119090199, 119089428, 119089942, 119089685, 119089171, 119088914, 33554439, 33554442, 33554441, 33554440, 33554438, 33554443)),
    ((10, 11, 13, 28, 58, 186, 216, 246, 250, 282), 13, (68426497, 82384898, 70850820, 67770881, 68688389, 83499264, 75108099, 101254936, 70982659, 101320985, 106696730, 71965444, 102500891, 119154964, 119155735, 119154450, 119155478, 119155221, 119154707, 33554439, 33554441, 33554438, 33554440, 33554442, 33554443)),
    ((10, 11, 12, 13, 23, 28, 29, 219, 221, 249, 251, 283), 14, (68491520, 70588932, 83236866, 67836161, 68950020, 67770371, 69933315, 67771136, 70916613, 101255704, 106630169, 67765785, 101255451, 103553562, 67897626, 71110426, 101387036, 119220500, 67898900, 119220757, 119221014, 119220243, 119221271, 119219986, 33554440, 33554438, 33554442, 33554439, 33554443, 33554441)),
    ((12, 13, 26, 27, 29, 60, 62, 205, 214, 220, 250, 252, 284), 11, (68426245, 83105795, 67966976, 67835908, 73141762, 67967745, 68819460, 71178241, 68880386, 101386265, 103553307, 67897883, 106697222, 102369816, 101455130, 119286550, 67964950, 119285779, 119285522, 119286036, 119286807, 119286293, 33554440, 33554439, 33554443, 33554442, 33554441)),
    ((11, 12, 13, 15, 30, 31, 63, 236, 241, 247, 253, 255, 285), 14, (69933059, 67967236, 68098306, 67901442, 71047429, 68945408, 67901697, 72158465, 101385752, 106631449, 101386778, 103422747, 67771419, 71110939, 119351315, 102438684, 119352086, 119351829, 119352343, 119351572, 119351058, 33554442, 33554443, 33554440, 33554441, 33554439, 33554438)),
    ((0, 14, 15, 31, 46, 47, 62, 239, 254, 286), 11, (69146629, 82122752, 68098562, 71175425, 67967491, 68163844, 71175939, 69011972, 68164352, 71175682, 104731656, 71176453, 101586712, 103746823, 71176967, 119417879, 68096279, 119417622, 83757590, 119417108, 119417365, 119416851, 119416594, 33554438, 33554443, 33554441, 33554442)),
    ((14, 15, 30, 253, 287), 10, (70192128, 68032513, 69076994, 67115008, 70129923, 71177989, 70193156, 111351832, 69012248, 104665625, 119481102, 67115790, 119480588, 119480845, 119481616, 119481873, 119481359, 134217728)),
    ((1, 15, 34, 35, 44, 46, 61), 6, (100798232, 100668697, 108863002, 103682587, 74190362, 100799772, 107746333, 105779998)),
    ((2, 18, 51, 52), 4, (103815960, 67309592, 103947291, 100734745, 67309851, 100865562, 100731164)),
    ((35, 68), 6, (72423429, 69212163, 67243265, 70326272, 67243522, 70260740, 100929048, 100799001, 100800282)),
    ((51, 62, 63, 64), 9, (100863256, 100863769, 71309569, 69213187, 70589188, 69343488, 69343749, 67245058, 105844762, 101913883, 107812124)),
    ((5, 8, 10, 44, 62, 85, 113), 7, (101979672, 100927001, 108730138, 109579291, 107614236, 104663326, 75044380, 100928797)),
    ((15, 43, 52, 85), 4, (100995353, 100865050, 100865304, 108728603, 105714716)),
    ((7, 11, 103, 119), 4, (101061400, 106371865, 101059098, 69868569, 101059867, 74060825)),
    ((8, 52, 59, 60, 86), 4, (100864536, 109776921, 109775900, 101124635, 100996637, 109778458)),
    ((9, 10, 41, 42, 136), 5, (107613976, 101191449, 104274715, 101190938, 109711646, 76155931, 101190428, 110694175, 101190685)),
    ((8, 57, 59, 120, 138), 11, (70326789, 79239426, 72554753, 75044864, 101127960, 70720004, 69738243, 101123609, 108666138, 76221978, 109647388, 101258523)),
    ((29, 38, 43, 60, 186), 8, (82581508, 76156418, 69737216, 78256129, 69737989, 82319363, 109712920, 108793881, 101323290, 105649947, 101320732)),
    ((6, 10, 27, 29, 139, 154), 10, (69867524, 75173378, 79305217, 69540613, 73079043, 104733208, 75172864, 101258778, 72159000, 107679513, 101386523, 101258268, 101386013)),
    ((13, 27, 28, 60, 61), 9, (81795073, 69474821, 71047171, 70981632, 71964676, 69212674, 101451288, 72094232, 103681819, 105649689, 101451804, 105649434)),
    ((46, 61, 62, 124), 12, (71112962, 81926656, 70392323, 74062337, 70982403, 71113216, 73144325, 73207812, 104537880, 74258200, 104799514, 74256922, 113973017, 105714459, 101517596, 101516829)),
    ((0, 14, 17, 31, 32, 44, 47, 60, 62, 63, 78, 302), 11, (71243781, 72224772, 71112705, 70326531, 72223744, 72224258, 104728088, 72224001, 104729114, 120463628, 70065420, 102768135, 120464913, 71244817, 102631705, 70192921, 120463885, 71111437, 71177497, 104728347, 105780746, 120466455, 68029207, 120465170, 105779718, 71240710, 68027922, 120466198, 120464656, 120465941, 120465427, 120464399, 120465684, 120464142, 134217728, 33554443, 33554440, 33554441)),
    ((30, 31, 46, 62, 63, 143, 303), 11, (70125313, 71047680, 73275906, 71178500, 71241475, 120529164, 71048204, 71241989, 105843992, 70327298, 71241732, 71240961, 120530192, 69077520, 71177744, 105714969, 114103834, 120530449, 120529935, 120529421, 120529678, 134217728)),
    ((17, 33, 34, 61, 62), 6, (101783064, 67244056, 101848603, 101716761, 108794394, 106828060)),
    ((34, 41, 46, 47, 82), 6, (101782040, 104864537, 73209113, 110694682, 101914395, 104795676)),
    ((33, 45, 52, 60, 63), 6, (100864792, 106829593, 107289115, 101848860, 75238939, 107746586)),
    ((22, 68, 85), 6, (72357890, 69277700, 70588416, 69408769, 69278469, 69409027, 101914136, 102042137, 101913114)),
    ((21, 67), 6, (69278212, 70588677, 69670912, 69539843, 70391809, 69540354, 101975832, 101979161)),
    ((27, 35, 51, 52, 62), 4, (100863000, 100865817, 107679770, 100800027, 104663068)),
    ((13, 101), 2, (102110488, 106695705)),
    ((24, 40, 41), 2, (102173464, 110694426, 102172185, 110694939)),
    ((9, 25, 58), 6, (110759448, 105454107, 101190169, 77204507, 102237722, 76090394, 77074970)),
    ((9, 24, 26, 107, 137, 153), 8, (101192984, 103357465, 68749849, 102172700, 102240794, 108597277, 112921883, 67701786)),
    ((27, 61, 74, 153), 11, (72751361, 81271043, 70785026, 83368708, 70785792, 79305477, 108795417, 111808539, 102241560, 107680026, 68815642, 75110170)),
    ((10, 11, 12, 26, 44, 45, 62), 10, (83433473, 71965187, 69671172, 69671936, 108728856, 82516485, 69802498, 106631705, 106762011, 102304028, 106630426, 104662813, 106632478, 104663839)),
    ((13, 29, 44, 47), 15, (70392578, 69671428, 75238657, 107745048, 69867780, 79436547, 73014277, 79436800, 103679514, 105649179, 69999643, 102501145, 71110171, 104731164, 72159513, 73144089)),
    ((1, 11, 12, 14, 15, 27, 29, 31, 36, 45, 46, 53, 59, 60, 63, 108, 317), 11, (70261248, 82647041, 70916356, 72161538, 102767897, 74256131, 121448981, 69999381, 70065173, 74256645, 106761242, 106763032, 73207321, 121448210, 121447953, 121446668, 121447439, 113972507, 121447696, 121447182, 121448724, 121449238, 121448467, 121449495, 121446925, 134217728, 33554442, 33554439, 33554441, 33554440, 33554443, 33554438)),
    ((15, 16, 28, 30, 31, 43, 46, 47, 60, 94, 318), 17, (68164097, 70064133, 73273348, 71244036, 69475843, 70064640, 121512461, 71244301, 73272834, 70064909, 70589442, 80550401, 70982913, 121512975, 70195471, 103680537, 73273091, 69409795, 106695960, 121512718, 121515031, 69077783, 73272320, 70193431, 70261765, 121513489, 105843718, 121514260, 73273862, 102500634, 70192660, 73143578, 121513232, 103681563, 121514774, 121512204, 121514517, 121513746, 121514003, 134217728, 33554442, 33554440, 33554439, 33554443, 33554441)),
    ((0, 45, 46, 47, 49, 62, 319), 10, (70392069, 70129664, 72226818, 69409284, 70130180, 70195201, 72290051, 106764056, 70130433, 121578511, 72226063, 104663577, 121579025, 72226577, 70126353, 121578768, 102565658, 121577997, 104666651, 104666908, 104662557, 121578254, 121577740, 134217728)),
    ((35, 49, 68, 79, 95), 4, (102963992, 67374872, 100799257, 105776666, 105778971, 105777180)),
    ((16, 77, 78, 86, 93, 94), 6, (108859416, 106306329, 76353049, 100996890, 106759707, 109909276, 105715229)),
    ((69, 74, 93), 3, (100930072, 111808281, 109843738)),
    ((77, 85, 93), 5, (104077592, 67440152, 109451545, 75304217, 109907994)),
    ((69,), 7, (74520577, 71309315, 69343234, 72685568, 72489221, 70457348, 100931096, 100930585, 100931354)),
    ((20, 78, 85, 86), 7, (100994840, 71440384, 77863171, 71571460, 72620033, 71571714, 71571973, 105711129, 100995866, 107681563)),
    ((74,), 1, (111807512, 111807769, 111808026)),
    ((81, 86, 119), 3, (101125656, 100996377, 105711386)),
    ((9, 77), 3, (101189144, 76026392, 105646617)),
    ((56, 92, 153), 5, (106043928, 72948760, 78320152, 101256985, 111743514)),
    ((8, 26, 44, 59, 123), 9, (71440643, 68032773, 71702528, 70916868, 106633752, 74190872, 71702785, 108661529, 71703042, 110761242, 108662811, 107613724)),
    ((76, 91, 140), 7, (73013507, 72947972, 73078789, 77270273, 83565056, 77270530, 111873817, 109775128, 106632218, 106632987)),
    ((2, 6, 10, 12, 42, 44, 60, 72, 77, 90, 91, 93, 125, 140, 332), 11, (83564803, 74324225, 83696133, 75176192, 76287490, 122430222, 72030734, 106694937, 77337881, 76288004, 122430993, 72030993, 108792600, 108859659, 106695194, 77338138, 76289803, 122431764, 122430736, 122431250, 122431507, 122429965, 122432278, 122430479, 122429708, 122432021, 122432535, 134217728, 33554438, 33554441, 33554442, 33554439, 33554440)),
    ((11, 13, 15, 29, 37, 43, 45, 47, 60, 61, 65, 69, 71, 92, 93, 94, 95, 125, 163, 229, 333), 12, (71506177, 72751106, 73209859, 71374852, 71833860, 73210624, 73014017, 72092421, 106629144, 107810329, 122495501, 73143053, 122496272, 73143824, 107681306, 122495758, 73143310, 122496015, 107812379, 107811868, 122496529, 122497043, 122496786, 122497557, 122497814, 122497300, 122495244, 122498071, 134217728, 33554443, 33554442, 33554440, 33554438, 33554441, 33554439)),
    ((32, 46, 63, 64, 79, 93, 94, 95, 110, 334), 10, (72423681, 73340931, 74322181, 73275397, 73210116, 71637248, 73341186, 74320896, 73276163, 74321924, 122561808, 73341456, 104930329, 73206041, 75370265, 106828824, 74321410, 122560780, 73341708, 106760218, 106825499, 122561294, 73208846, 122561037, 107878155, 122562836, 70125588, 122563093, 107876870, 70125845, 122563607, 122562065, 122561551, 122563350, 122562322, 134217728, 122562579, 33554442, 33554441, 33554440, 33554439)),
    ((35, 47, 62, 63, 94, 95, 335), 8, (73338370, 75372803, 73275652, 73338113, 71309824, 116333336, 75370008, 72223493, 106826009, 74387225, 73338627, 122627087, 73274639, 73339141, 107941146, 73338884, 73337856, 122626573, 73274125, 122627344, 73274896, 122626316, 122626830, 122627601, 134217728)),
    ((51, 92, 94, 95), 6, (101848088, 107026713, 72948249, 75369753, 108926746, 73272090, 110890267)),
    ((34, 78), 5, (115481368, 110959385, 71768601, 68228888, 74321177)),
    ((68, 73, 85), 4, (101978648, 103881497, 67375385, 110890010)),
    ((41, 86, 108), 3, (112924440, 110693657, 100995610)),
    ((69, 92), 3, (100930328, 113973529, 77336089)),
    ((68,), 8, (72488960, 69474308, 71636995, 71505922, 69540101, 67439873, 104012312, 67374104)),
    ((58, 65, 77, 91), 11, (71375365, 82123266, 71768323, 72555008, 69672196, 109843480, 71637505, 112857626, 111614489, 77204761, 106694683)),
    ((2, 38, 93, 103), 3, (101061144, 106632729, 106630683, 111874842)),
    ((25, 91), 3, (110629912, 68683800, 112858137)),
    ((73, 75, 80, 90, 122), 5, (110825497, 108594712, 106628636, 110825243, 108725789, 106759962)),
    ((60, 75, 77, 123, 171), 7, (106502937, 78255385, 101323544, 108794140, 76224284, 105645851, 108660762)),
    ((6, 23, 27, 29, 43, 59, 74, 75, 77, 87, 89, 92, 93, 106, 347), 12, (72751616, 83695877, 72030467, 76225028, 72882434, 82516225, 110825752, 108728089, 108729882, 123412748, 74060300, 123414290, 72092690, 123414033, 123413519, 74061071, 106761499, 123413005, 123414547, 123414804, 123415061, 123415318, 123415575, 123413776, 123413262, 134217728, 33554442, 33554441, 33554440, 33554443, 33554439, 33554438)),
    ((20, 26, 28, 45, 54, 60, 62, 76, 77, 86, 93, 109, 156, 244, 348), 13, (71899136, 72620290, 73210369, 83630083, 75372549, 72161282, 73075204, 72358657, 73210885, 123478798, 77336580, 74126350, 73074947, 110892811, 106896408, 74192664, 123479312, 123479569, 123480083, 123479826, 72158226, 123478541, 123479055, 123480854, 123481111, 123478284, 123480597, 123480340, 134217728, 33554441, 33554439, 33554442, 33554440, 33554438)),
    ((45, 49, 59, 61, 63, 65, 77, 78, 89, 91, 92, 94, 95, 109, 349), 15, (71375106, 82582016, 72096003, 73140997, 74258689, 71506436, 104995352, 105712153, 116267803, 72091163, 106371610, 72096260, 75303963, 72091928, 75306521, 123544848, 106629916, 74192400, 123546647, 72225047, 73074458, 75304728, 108860445, 123543820, 123545876, 123546133, 123544591, 123545619, 123546390, 123544334, 123545362, 123544077, 123545105, 134217728, 33554443, 33554441, 33554440, 33554438, 33554442, 33554439)),
    ((16, 47, 48, 50, 62, 78, 79, 80, 126, 350), 10, (72358145, 72227075, 72292354, 75370500, 73206533, 72227330, 75370757, 75369472, 105712408, 71375616, 107877913, 72223257, 123610384, 72162064, 107876123, 105780250, 123609870, 72162318, 123610127, 123611412, 71174164, 123609356, 108926217, 72289812, 123612183, 71174935, 123611669, 108925703, 72290583, 71174421, 123609613, 123610898, 123611155, 123610641, 123611926, 134217728, 33554443, 33554438, 33554442, 33554440)),
    ((78, 79, 92, 351), 12, (72358405, 74323972, 72292611, 72227585, 74386946, 108860696, 75371008, 72292865, 123675406, 83827470, 106765593, 71310350, 123675149, 72157209, 74322701, 74386432, 123675663, 106763802, 123676177, 106762779, 123675920, 123674892, 106762524, 134217728)),
    ((110, 111, 127), 2, (108075544, 76420888, 109972761, 109974810, 109973019)),
    ((80, 126), 2, (112006936, 109908761)),
    ((111,), 1, (109974296,)),
    ((115, 117, 120, 126), 3, (101127448, 112006425, 107808282, 112005659)),
    ((108,), 2, (111938840, 79368984)),
    ((50, 119, 124), 4, (104208408, 67571480, 113972761, 109777946)),
    ((103,), 5, (74717184, 77862917, 74913793, 67506180, 74782722, 67505923, 101062168, 101061657)),
    ((120,), 6, (75634693, 74717443, 69605377, 73799684, 72816640, 73799938, 101127192)),
    ((123, 136), 3, (108660504, 101191962, 108660249, 109712411)),
    ((25, 108, 122, 138, 154, 230), 5, (108595481, 109645082, 101259036, 77138716, 108595995, 109644312, 107677470, 108597789)),
    ((10, 36, 38, 40, 45, 74, 91, 108, 120, 122, 123, 155, 187, 230, 234, 362), 9, (108661272, 111938587, 124396045, 75043597, 106634010, 74191642, 108730908, 78385436, 124396559, 75044111, 110757401, 124397073, 75044625, 112922377, 124398358, 73076758, 124395788, 124398615, 124396816, 124397330, 124397587, 124396302, 124397844, 124398101, 134217728, 33554440, 33554439, 33554438, 33554443, 33554442)),
    ((11, 21, 43, 53, 58, 69, 77, 92, 105, 109, 122, 123, 124, 125, 135, 157, 171, 229, 239, 363), 12, (74782981, 79367168, 75175938, 70851329, 74783492, 75110659, 74979845, 75111169, 108595225, 75111428, 112989464, 75237656, 78450456, 124461581, 124463380, 75109133, 124462352, 108726810, 75109904, 124461324, 124462095, 75109647, 107809051, 124462609, 124463894, 124464151, 124461838, 124462866, 124463637, 124463123, 134217728, 33554440, 33554438, 33554441, 33554439, 33554443, 33554442)),
    ((32, 50, 60, 74, 92, 93, 106, 123, 124, 125, 140, 156, 157, 224, 226, 364), 13, (72554501, 76159492, 73668609, 74062592, 75241730, 82713091, 78384642, 74783747, 74062853, 75242243, 108791832, 74258944, 73997825, 104667929, 75172121, 124527888, 124527631, 75175183, 124528659, 124529687, 124527117, 124529430, 124527374, 124526860, 124528402, 124529173, 124528145, 124528916, 134217728, 33554439, 33554443, 33554440, 33554441, 33554438, 33554442)),
    ((35, 45, 61, 77, 93, 99, 107, 108, 111, 124, 125, 126, 127, 157, 205, 237, 365), 13, (83630337, 75307008, 77401602, 75241985, 82582788, 75307781, 77339139, 75308036, 112004120, 77401859, 75236888, 109907225, 73139993, 107677210, 124593167, 75240719, 106760731, 76355099, 124593681, 75241233, 109777693, 124592910, 75240462, 124592653, 109909788, 124595223, 75240205, 124593938, 124594195, 124594709, 124593424, 124594966, 124594452, 124592396, 134217728, 33554440, 33554442, 33554439, 33554443, 33554441, 33554438)),
    ((76, 78, 81, 94, 95, 111, 126, 127, 142, 255, 366), 11, (74651904, 77403395, 75438085, 75307522, 74390020, 76419076, 75438337, 124659217, 75438865, 76419333, 124657932, 108857626, 75439116, 108926488, 73406721, 76418819, 124658960, 73407234, 109841689, 124658446, 108989446, 76419590, 124660245, 72222997, 124660502, 124659731, 72222483, 124660759, 124658703, 109975050, 124658189, 134217728, 124659988, 124659474, 33554441, 33554443, 33554440, 33554439)),
    ((79, 95, 110, 126, 127, 367), 11, (73406469, 75435779, 73537537, 75435522, 75436036, 111023896, 108075289, 74319360, 110038555, 75368475, 75435265, 124723982, 78451481, 75371534, 107809306, 77466905, 76484888, 124724239, 124723468, 124723725, 124724496, 124724753, 134217728)),
    ((125,), 2, (112989976, 112989721, 112988442, 75237913)),
    ((68, 96, 111), 4, (103030040, 68358936, 108990746, 108857113)),
    ((125,), 3, (109517336, 75237144, 79434520)),
    ((110, 120), 4, (101126936, 107158041, 75045145, 76418073)),
    ((102, 103, 117, 124), 3, (101059608, 101061913, 112987930, 111021083)),
    ((102, 107, 108, 126), 5, (102044696, 112922905, 107158298, 74717978, 112922651, 112923932, 75302426)),
    ((119, 120), 2, (102111000, 102109721, 101127706)),
    ((102, 120), 7, (73734147, 74848261, 75962369, 71768066, 74848512, 67571716, 103160600, 68490008, 101126681)),
    ((107, 137), 8, (74651649, 69801989, 73603075, 74914048, 74848772, 73865218, 101192472, 101193241, 107612954)),
    ((7, 8, 25, 36, 41, 57, 89, 105, 106, 107, 115, 122, 151, 215, 249, 377), 4, (110693400, 125379599, 76027151, 125379342, 125380884, 110957081, 125380627, 125378828, 125380113, 125381141, 125381398, 125379856, 125379085, 125380370, 125381655, 134217728, 33554442, 33554441, 33554439, 33554440, 33554438, 33554443)),
    ((20, 24, 26, 41, 58, 74, 90, 104, 106, 107, 123, 124, 180, 246, 250, 378), 10, (72947712, 73996547, 74127618, 73997061, 113711384, 75041284, 72949016, 107612441, 125445135, 76225551, 75040513, 107682330, 107611931, 79433754, 79432728, 107612700, 125446420, 125444364, 74124820, 110760989, 125445649, 125445392, 125446163, 125444621, 125447191, 125446934, 125445906, 125444878, 125446677, 134217728, 33554441, 33554442, 33554443, 33554439, 33554438, 33554440)),
    ((36, 37, 43, 59, 76, 89, 91, 106, 107, 108, 125, 138, 157, 185, 186, 379), 11, (71964933, 73930753, 74061828, 75106563, 73013762, 73931008, 107612184, 79367704, 125510414, 73931534, 110826009, 125511442, 74189842, 125509900, 76157452, 125512727, 74191127, 125510671, 76158223, 107678490, 125511185, 76158737, 125512470, 125512213, 125510157, 125511956, 125511699, 125510928, 134217728, 33554443, 33554441, 33554439, 33554440, 33554442, 33554438)),
    ((42, 48, 50, 58, 60, 76, 90, 107, 108, 109, 112, 114, 141, 188, 380), 15, (75307269, 77207809, 75110400, 70064389, 73734404, 74193155, 79433218, 75110916, 74717699, 75308289, 116138008, 76286488, 77405186, 125575693, 74259725, 107743002, 107677721, 107677979, 112004616, 79434760, 125578006, 74256406, 125576721, 125576978, 74255378, 125577749, 125576207, 125576464, 125575950, 125578263, 125575436, 125577492, 134217728, 125577235, 33554438, 33554441, 33554443, 33554439, 33554442)),
    ((32, 65, 67, 76, 93, 95, 109, 110, 113, 117, 124, 127, 140, 147, 157, 173, 381), 11, (74586113, 74192898, 74258432, 74127363, 72095749, 74455045, 74455300, 109845272, 108010009, 75172633, 110956827, 74189595, 107808794, 77403162, 77401112, 125643285, 72157461, 108726045, 110956572, 125640972, 125642000, 76289552, 125643542, 108729374, 125641229, 110957343, 74189340, 125642257, 125641743, 125643799, 125643028, 125642771, 125642514, 125641486, 134217728, 33554441, 33554442, 33554438, 33554439, 33554440, 33554443)),
    ((78, 79, 80, 92, 94, 95, 110, 111, 142, 158, 382), 14, (74783232, 77467138, 74389761, 83761156, 74324483, 73472005, 77467395, 75438596, 125707536, 74259216, 77467909, 109779736, 107877657, 125707793, 74259473, 77336856, 125706508, 73603331, 76354060, 125708050, 73270802, 125707279, 125706765, 125707022, 125709078, 73271830, 74387478, 125709335, 74387735, 134217728, 125708564, 73271316, 125708821, 125708307, 33554440, 33554438, 33554441, 33554442, 33554443, 33554439)),
    ((110, 111, 113, 126, 383), 10, (82712833, 74389509, 76421124, 74390274, 76421376, 76421891, 125772815, 73406991, 110958360, 74320143, 76484355, 125772558, 108863257, 76420110, 125773072, 74254105, 74320400, 108857882, 125772301, 108861211, 108859932, 125772044, 125773329, 134217728)),
    ((129, 140, 141, 143), 3, (110172696, 78517528, 114036505, 114035994, 112069915)),
    ((142, 158, 159), 5, (112135193, 110434330, 80549658, 109905688, 75504408)),
    ((103, 143), 2, (101062424, 112072473)),
    ((157,), 2, (115085848, 80546840)),
    ((137, 140), 3, (101193496, 76024600, 114036761)),
    ((156, 158), 2, (114103065, 110823960)),
    ((67, 137, 154, 215), 3, (109578008, 113971994, 109843225, 109582107)),
    ((114, 119, 137, 138), 4, (101125400, 101257753, 112004378, 107678235)),
    ((36, 72, 121, 132, 134, 139, 151, 152, 153, 166, 168, 184, 185, 228, 232, 244, 248, 392), 8, (69736707, 67636738, 77010945, 69736961, 67637252, 69737728, 79108096, 73931269, 79108357, 110626584, 109709337, 110626842, 126363410, 126362896, 126363153, 126361868, 126363667, 126364181, 126364438, 126363924, 126362639, 126362382, 126362125, 126364695, 134217728, 33554440, 33554441, 33554443, 33554438, 33554439, 33554442)),
    ((41, 56, 105, 138, 139, 151, 152, 154, 155, 169, 201, 231, 233, 393), 13, (75765765, 70850563, 77076482, 78125059, 75896833, 74979329, 79173888, 77011460, 74979588, 67637760, 109517080, 77137432, 101258009, 77137689, 126429460, 126427661, 77075213, 126428432, 77075984, 126428689, 126427918, 126428946, 126429974, 126427404, 126429717, 126430231, 126428175, 126429203, 134217728, 33554441, 33554438, 33554439, 33554440, 33554443, 33554442)),
    ((40, 42, 104, 108, 123, 136, 139, 154, 155, 170, 186, 232, 236, 394), 13, (77011202, 73996292, 77273088, 76089603, 77273857, 77274117, 103357208, 77138200, 110758169, 126493454, 77141006, 110758683, 111939610, 75963162, 110757916, 79369754, 126495510, 75173910, 126493968, 111809309, 126494225, 77141777, 126493197, 126492940, 126494482, 126494739, 126493711, 126495253, 126495767, 134217728, 126494996, 33554441, 33554442, 33554439, 33554440, 33554443, 33554438)),
    ((39, 41, 75, 90, 91, 101, 109, 122, 126, 140, 141, 154, 155, 157, 171, 173, 188, 235, 249, 395), 10, (76028162, 77207556, 76155139, 77208069, 77208320, 103488536, 77137944, 114102041, 77334809, 76154625, 111874074, 126558733, 77206285, 126559504, 109647132, 111875867, 77207056, 126558476, 77206028, 126560018, 126561046, 126559761, 126560275, 126561303, 126558990, 126559247, 126560532, 126560789, 134217728, 33554443, 33554439, 33554442, 33554440, 33554441, 33554438)),
    ((66, 76, 86, 110, 124, 125, 134, 141, 142, 155, 156, 157, 170, 172, 236, 238, 253, 396), 18, (76355585, 76683266, 72030211, 77273602, 80482565, 77338880, 75766020, 76356100, 75503875, 76221189, 113055000, 110889753, 110823194, 81532697, 78515992, 126624526, 77405454, 126625040, 77405712, 107742747, 78385691, 113053706, 126626068, 72091668, 126624269, 77271821, 75304468, 126625297, 126626839, 126626582, 126626325, 126624783, 126624012, 126625554, 126625811, 134217728, 33554441, 33554440, 33554438, 33554443, 33554439)),
    ((65, 67, 97, 109, 126, 129, 140, 145, 156, 173, 189, 239, 397), 12, (75241476, 77273346, 79370240, 77404163, 77338624, 82582533, 78388225, 77404677, 109058584, 76220184, 79498497, 76286211, 110822937, 109775386, 126689805, 77337357, 113054471, 126691090, 113055499, 126690062, 77337614, 126692118, 126690576, 126691604, 126690319, 126692375, 126691861, 126690833, 126691347, 126689548, 134217728, 33554441, 33554442, 33554438, 33554440)),
    ((96, 98, 110, 115, 127, 143, 144, 158, 159, 174, 398), 11, (75569153, 76290051, 78515200, 77535236, 76617733, 79632642, 78515714, 111023640, 126756112, 77536272, 110954778, 111022617, 75367961, 126756369, 108923163, 126755855, 77468955, 112072202, 126757911, 74320663, 112071174, 111086855, 126757140, 74319892, 78516999, 126756883, 126755084, 74319635, 126756626, 126755341, 126757397, 126757654, 126755598, 134217728, 33554443, 33554440, 33554441)),
    ((111, 127, 158, 159, 399), 11, (75503619, 77532674, 77469701, 76552193, 77532160, 75634949, 76417540, 103750168, 77400600, 77533188, 113120025, 77533445, 113120538, 126821391, 78581017, 126821134, 77468686, 78581530, 126821905, 126821648, 126820620, 126820877, 134217728)),
    ((143, 159), 2, (109971224, 111019545)),
    ((128, 142, 158), 5, (111155736, 76352280, 113056537, 80548889, 111087386)),
    ((140,), 1, (114036248,)),
    ((158,), 2, (112006168, 75302936)),
    ((157,), 2, (115086360, 80547352)),
    ((129,), 1, (110955288,)),
    ((153,), 1, (110627608,)),
    ((136, 137, 138, 228), 4, (102175512, 109643801, 109578778, 108596507)),
    ((56, 88, 136, 137, 150, 153, 168, 184, 214, 408), 5, (101192728, 76023832, 102241802, 102241031, 127412500, 76090900, 127412757, 76091157, 127412243, 127413271, 127413014, 127411986, 33554438, 33554443, 33554440, 33554441)),
    ((40, 49, 55, 83, 105, 121, 137, 138, 139, 154, 185, 187, 232, 249, 409), 11, (77072900, 82385154, 76027905, 70916099, 76945413, 77071872, 80156673, 70851072, 67703045, 76028418, 71899395, 78126083, 127478036, 127475980, 127477008, 127476494, 127476237, 127476751, 127477265, 127478293, 127477522, 127477779, 127478550, 134217728, 127478807, 33554442, 33554441, 33554438, 33554440, 33554439, 33554443)),
    ((56, 74, 86, 106, 122, 124, 138, 139, 155, 156, 186, 216, 248, 410), 10, (76158979, 76093440, 76224514, 69933572, 76093697, 73997317, 77138436, 109709848, 109451801, 109710106, 79432985, 109708827, 127542030, 78189582, 127543829, 76222229, 127542287, 127542801, 127542544, 127543315, 127541516, 127544086, 127541773, 127543058, 127544343, 127543572, 134217728, 33554439, 33554441, 33554442, 33554443, 33554440, 33554438)),
    ((75, 89, 91, 123, 133, 138, 140, 141, 156, 157, 159, 187, 251, 411), 10, (74062080, 76159235, 77203201, 76159749, 76160002, 109643288, 77203972, 109643547, 113908761, 76285977, 109644572, 127607309, 76160269, 109774874, 127607566, 78255118, 79498777, 127608337, 78255889, 127608080, 78255632, 127608594, 76286994, 127609365, 127607823, 127607052, 127609108, 127608851, 134217728, 127609879, 127609622, 33554440, 33554439, 33554438, 33554443, 33554441, 33554442)),
    ((76, 80, 82, 84, 92, 109, 126, 139, 140, 141, 157, 158, 188, 220, 235, 236, 252, 412), 13, (75831300, 76290561, 76355840, 77535747, 77404421, 77268994, 112007961, 80481305, 107743514, 127673616, 109839896, 78454032, 78386458, 127673359, 127674901, 76353301, 127675415, 127673873, 76353815, 127674130, 73139730, 76352530, 110761755, 127675158, 127673102, 127674387, 127672845, 127672588, 127674644, 134217728, 33554439, 33554443, 33554441, 33554438, 33554442, 33554440)),
    ((81, 109, 110, 121, 124, 125, 127, 140, 141, 142, 143, 149, 156, 159, 172, 189, 413), 18, (76814338, 80547073, 76224771, 76290309, 77334273, 75700224, 78453252, 77469952, 113053464, 127738638, 78518798, 74188814, 127740437, 113053978, 74128149, 110824217, 108726300, 127738895, 108860187, 127739409, 78386961, 127740951, 74255127, 127740180, 110826525, 127738124, 110827038, 127739152, 127739923, 127740694, 127738381, 127739666, 134217728, 33554442, 33554441, 33554439, 33554438, 33554440, 33554443)),
    ((111, 116, 126, 142, 143, 144, 157, 159, 190, 238, 254, 414), 11, (75569669, 76486660, 77535489, 79563776, 76617986, 76421635, 79564547, 75831553, 79564290, 127804174, 76748814, 109972248, 77536000, 79564804, 127804431, 113121035, 79565061, 127804945, 110888473, 127806230, 75368982, 76484630, 127806487, 127805202, 75369239, 76483602, 127805459, 75368211, 76483859, 127804688, 127803917, 127805973, 127805716, 127803660, 134217728, 33554438, 33554440, 33554439, 33554441, 33554442)),
    ((142, 143, 145, 156, 158, 415), 11, (75569408, 78518274, 77466373, 78581764, 76486913, 76487171, 127869710, 78517262, 76552448, 127869196, 112008216, 76416524, 112073497, 127870224, 78516248, 110823706, 127870481, 77399833, 110954011, 110958108, 127869967, 127869453, 134217728)),
    ((145, 175), 3, (112269592, 80614680, 114169625, 112070938)),
    ((174,), 1, (116200216,)),
    ((165, 175), 2, (114168600, 78513944, 114167833)),
    ((31,), 1, (105715480,)),
    ((69, 102), 3, (114628888, 67506456, 100930841)),
    ((172, 174, 190), 6, (111286552, 78977560, 78449176, 116201242, 79108634, 111871513)),
    ((7, 170), 3, (101322520, 68752664, 109581337)),
    ((86, 186, 187), 3, (101387544, 79042584, 111740441, 111743770)),
    ((8, 137, 153, 171), 4, (109578520, 101323801, 78252057, 109580315, 101324058, 110627100, 78252314)),
    ((20, 73, 154, 167, 170, 185, 186, 188, 201, 217, 248, 425), 4, (101389848, 79366680, 109646617, 128527383, 128527126, 128526869, 128526612, 128526355, 128526098, 33554439, 33554441, 33554440, 33554442, 33554443, 33554438)),
    ((14, 42, 58, 66, 70, 90, 138, 155, 168, 171, 184, 186, 202, 251, 426), 12, (79239169, 79304960, 80222213, 77993987, 81336322, 79239682, 83565316, 79239940, 67767553, 78186755, 112925464, 76156184, 101324555, 109842201, 128590092, 128590863, 128592405, 128592148, 128591377, 128591120, 128591634, 128590349, 128592919, 128590606, 128592662, 128591891, 134217728, 33554439, 33554438, 33554440, 33554442, 33554441)),
    ((13, 73, 75, 87, 139, 165, 172, 173, 186, 187, 188, 203, 235, 237, 253, 427), 11, (79304704, 79173637, 73013249, 80353284, 78251777, 78125314, 78125571, 101388312, 101389337, 79366169, 128657170, 128656656, 79304208, 107680282, 128656399, 79303951, 109778203, 128657941, 128655885, 128658455, 128656913, 128655628, 128657684, 128658198, 128656142, 128657427, 134217728, 33554439, 33554443, 33554440, 33554442, 33554441, 33554438)),
    ((100, 106, 108, 138, 140, 141, 156, 157, 174, 188, 189, 204, 236, 238, 252, 428), 11, (77928704, 79436036, 79370498, 78452995, 78317313, 78318341, 112986392, 112920857, 112986650, 128721678, 112985627, 81468686, 114037532, 115149830, 76285724, 128721164, 79368716, 115150087, 128722192, 128722963, 77401363, 128721421, 128723477, 128721935, 128723734, 128722706, 128722449, 128723991, 128723220, 134217728, 33554442, 33554443, 33554441, 33554440)),
    ((97, 99, 107, 109, 111, 124, 135, 147, 156, 157, 159, 165, 172, 175, 188, 221, 237, 429), 11, (81467394, 79435776, 79501316, 81596163, 79436289, 79501573, 112920344, 114102298, 79437338, 111872281, 128786700, 79434252, 115151880, 109774363, 113055260, 76352028, 128789527, 111875613, 75303703, 128788499, 128787214, 128787471, 128789013, 128787985, 128786957, 128788756, 128788242, 128789270, 128787728, 134217728, 33554439, 33554442, 33554438, 33554441, 33554443)),
    ((128, 130, 140, 142, 157, 159, 160, 162, 190, 191, 206, 222, 430), 14, (77928452, 80613123, 78583810, 79632384, 78714881, 81730053, 78584321, 80612352, 128852236, 79499788, 111220761, 81661209, 113120280, 78649858, 80613637, 79496985, 128852750, 114169354, 79630346, 114168326, 128854292, 76417044, 128854549, 111940634, 76417301, 128853007, 113118491, 128854806, 128853264, 128855063, 128853778, 128853521, 128854035, 128852493, 134217728, 33554440, 33554439, 33554441, 33554443)),
    ((129, 143, 159, 174, 190, 191, 431), 9, (77600771, 79566852, 79629312, 81664514, 77601029, 79630597, 77731841, 79629826, 112003096, 79629569, 114301977, 112002842, 128918800, 80677913, 79566352, 128917772, 114232604, 112002587, 79565324, 128918029, 128918286, 128918543, 128919057, 134217728)),
    ((174, 191, 223), 3, (117314328, 115217945, 114167322)),
    ((160, 174), 2, (115151640, 113184537)),
    ((189, 190, 195), 2, (112986136, 115217177, 115215130)),
    ((4,), 1, (100861976,)),
    ((21,), 1, (108663320,)),
    ((165, 185, 190), 4, (113318424, 79497496, 102306585, 115152410)),
    ((167,), 1, (112854808,)),
    ((136, 165), 2, (102175256, 102176537, 113052442)),
    ((137, 171, 231), 3, (111807256, 109577753, 110630682)),
    ((23, 41, 170, 189, 224), 6, (112531736, 78186264, 111740954, 111741467, 110693913, 108729116, 116200478, 109579549)),
    ((43, 58, 86, 88, 170, 171, 182, 187, 188, 202, 216, 218, 442), 13, (103422488, 78251544, 101321753, 78059801, 101388555, 108727578, 68818699, 76157722, 111744795, 77205787, 113972252, 129640210, 78318610, 129640724, 78319124, 129641238, 129640981, 129641495, 129640467, 33554442, 33554440, 33554441, 33554439, 33554438)),
    ((57, 83, 100, 106, 107, 117, 123, 138, 141, 169, 170, 171, 172, 173, 189, 219, 251, 253, 443), 12, (78059521, 78321668, 80418819, 79301381, 81271296, 79301124, 67833346, 79300610, 80354051, 111872025, 113052696, 129704204, 74057228, 129704718, 110695195, 129705489, 129706774, 110827290, 129705232, 129706003, 129707031, 129706517, 129705746, 129704461, 129704975, 129706260, 134217728, 33554441, 33554439, 33554442, 33554443, 33554440, 33554438)),
    ((60, 107, 112, 114, 116, 122, 124, 154, 172, 173, 178, 189, 190, 220, 444), 13, (82515968, 78190596, 78387459, 78452737, 80288005, 78321922, 82516739, 111937048, 79501829, 111872537, 82517249, 111937306, 129770254, 79305742, 108793627, 78322459, 108792860, 76223004, 114102813, 110889502, 129769997, 129772567, 78450967, 129772310, 78450710, 129770768, 129771282, 129771539, 129769740, 129772053, 129771796, 129770511, 129771025, 134217728, 33554443, 33554441, 33554442, 33554438, 33554439, 33554440)),
    ((140, 141, 145, 155, 157, 173, 174, 181, 183, 187, 188, 190, 191, 445), 11, (78780418, 81533441, 78387203, 79432453, 78387716, 78387968, 115150872, 78383640, 115151129, 78383897, 112795144, 112921370, 129835533, 129836047, 80483599, 129837589, 129835276, 76351765, 80482828, 129836818, 76350994, 129836561, 129837332, 76351508, 110954523, 129835790, 129837846, 129836304, 129837075, 129838103, 134217728, 33554441, 33554439, 33554438, 33554442, 33554443)),
    ((143, 158, 174, 175, 191, 207, 208, 222, 446), 12, (78977027, 78518529, 79497218, 81660928, 77928965, 79632900, 81662213, 79633152, 112069144, 81661442, 129900812, 79437068, 112335111, 81661699, 78584839, 129901583, 80549135, 81661956, 129901326, 129901840, 129902868, 77465620, 78581268, 129902097, 129902611, 77465363, 129903639, 78582039, 129903125, 77465877, 129903382, 77466134, 129902354, 129901069, 134217728, 33554441, 33554440, 33554442, 33554438, 33554443)),
    ((142, 174, 175, 177, 190, 447), 11, (80615941, 79562497, 81663235, 78584064, 78649604, 80678402, 129966348, 78513676, 112139032, 81596952, 129967633, 129966862, 113054745, 116200986, 129966605, 113051163, 79497754, 129967376, 129967119, 134217728)),
    ((1, 222, 239), 4, (100668184, 101585945, 101455386, 82708505)),
    ((181, 206, 208), 3, (114099992, 116330265, 116200730)),
    ((3, 207, 223), 3, (100796952, 114497561, 82711833, 116265498)),
    ((206, 223), 3, (112335384, 83760920, 101520921)),
    ((), 0, ()),
    ((206, 222), 4, (114497816, 80546072, 114629401, 67965721)),
    ((), 0, ()),
    ((122, 153), 2, (101256472, 113971737)),
    ((170,), 3, (114891032, 67768600, 68753176)),
    ((24, 188, 204, 216), 4, (101390105, 113969176, 109647642, 111744283)),
    ((155, 171, 187, 205), 5, (101324312, 101454361, 80479769, 112855323, 114034714, 78252568, 114037788)),
    ((45, 61, 84, 101, 134, 186, 187, 199, 201, 204, 219, 220, 221, 459), 4, (117053976, 67833624, 111875097, 130755607, 130755350, 130754836, 130754322, 130755093, 130754579, 33554443, 33554441, 33554439, 33554442, 33554438, 33554440)),
    ((128, 132, 140, 146, 156, 172, 189, 202, 205, 219, 220, 221, 222, 236, 460), 10, (83564546, 80615424, 81533185, 81598467, 80287746, 67899653, 81467908, 67899396, 81468160, 115083288, 80415493, 130819601, 101455627, 115082777, 101454599, 111937818, 111937563, 130818316, 130820115, 130820629, 130819087, 130821143, 130818830, 130819858, 130820372, 130818573, 130820886, 130819344, 134217728, 33554441, 33554438, 33554442, 33554440)),
    ((47, 62, 129, 131, 133, 139, 145, 148, 157, 173, 188, 190, 193, 197, 207, 220, 221, 222, 223, 237, 461), 11, (81664004, 81532929, 80353536, 68950531, 80481029, 80747010, 81533699, 80353794, 101518360, 117185305, 130884109, 81402125, 67965209, 101519131, 107811610, 130884880, 130884623, 81532175, 81532432, 130886165, 130886679, 130885394, 130885651, 130885908, 130883852, 130884366, 130886422, 130885137, 134217728, 33554442, 33554443, 33554440, 33554439, 33554441, 33554438)),
    ((160, 162, 174, 176, 191, 204, 207, 221, 222, 223, 238, 462), 12, (80025603, 81729536, 81664258, 82710789, 79763457, 81729797, 80681220, 82709761, 82710532, 101452824, 113449241, 81594905, 130950159, 115218202, 80747290, 81597711, 115149595, 130949388, 116265735, 130950673, 130951701, 78514453, 116265992, 130952215, 130951444, 78514967, 130951187, 130951958, 130949902, 130950930, 130950416, 130949645, 134217728, 33554438, 33554443, 33554441, 33554442)),
    ((175, 191, 206, 222, 223, 463), 12, (79829251, 83826693, 81726464, 81795844, 81726978, 80611073, 81727492, 117314584, 114100761, 81726721, 82775576, 131015438, 79562766, 81662990, 116199962, 131014924, 81662476, 131015695, 131016209, 131015181, 131015952, 134217728)),
    ((175, 205, 206, 222, 223), 7, (114629145, 67965465, 113318168, 81660184, 80878360, 101454874, 113117979, 113116700)),
    ((1,), 1, (101779224,)),
    ((5, 19, 208, 255), 4, (100928024, 101845529, 117314843, 116266778)),
    ((194, 197), 2, (115281688, 116264729)),
    ((19, 21), 2, (101845016, 101976345)),
    ((22, 164, 197, 208), 2, (102042392, 102045465, 115148314, 115148571)),
    ((23, 25, 216), 4, (102238488, 77075736, 102107161, 102503706)),
    ((9,), 2, (109452056, 75043096)),
    ((58, 187, 221, 253), 8, (114694680, 81529112, 114956314, 67832858, 110759705, 80288537, 68817434, 112858907)),
    ((170, 200), 3, (101322264, 68752408, 111741721)),
    ((205, 216, 235), 2, (112854552, 115086105, 112857882)),
    ((172, 173, 204, 220, 221), 6, (101518873, 113969690, 114039576, 113968667, 81595928, 102437660, 112923677)),
    ((131, 140, 148, 189, 204, 205, 216, 218, 221, 250, 252, 476), 9, (114034456, 115022873, 67898649, 114034971, 80414489, 102503432, 112985882, 131869719, 80548119, 131868948, 77334548, 131868434, 131869205, 131868691, 131869462, 33554441, 33554439, 33554442, 33554438, 33554443)),
    ((172, 173, 177, 181, 189, 191, 204, 206, 213, 219, 223, 241, 253, 477), 13, (81270787, 83499012, 80549888, 80484354, 81467650, 67964161, 80550149, 80484608, 101453592, 80415000, 80550659, 68883736, 131933199, 80484879, 81528577, 131933456, 131933970, 131933713, 131934741, 78448917, 131934227, 80612627, 131932942, 131935255, 78449431, 131934484, 131932428, 131932685, 131934998, 134217728, 33554442, 33554443, 33554441, 33554438, 33554440, 33554439)),
    ((174, 175, 176, 178, 190, 191, 205, 206, 207, 208, 223, 254, 478), 15, (81860866, 80746752, 80615684, 82647299, 80025857, 80616197, 83630597, 113252888, 116264473, 131997964, 80681484, 80480792, 117315082, 131999249, 80545817, 112068634, 80614426, 131998478, 132000277, 80678677, 131998735, 79563029, 132000791, 80679191, 131998992, 131998221, 132000534, 79563286, 80678934, 132000020, 134217728, 131999763, 131999506, 33554441, 33554440, 33554439, 33554443, 33554438)),
    ((174, 206, 207, 211, 255, 479), 13, (80746499, 78649345, 81660420, 82775040, 79894533, 80680962, 116202008, 132063500, 79829516, 80610828, 82709528, 132064014, 80611342, 114101017, 132064528, 115152666, 132063757, 132064785, 80612113, 132064271, 134217728)),
    ((17, 44, 207, 239), 4, (101716505, 112794648, 74190104, 116262426, 116266523)),
    ((2, 222, 255), 4, (100730904, 100731418, 116464153, 101649947, 67965977)),
    ((3, 45, 81), 2, (100797208, 100796185, 100798747, 107745818)),
    ((2, 4), 2, (100862232, 100730393)),
    ((5, 9), 4, (100928280, 110566169, 67634969, 76026649)),
    ((6, 30, 86, 244, 255), 5, (116857112, 72159768, 100996122, 107681051, 100993049, 116197148)),
    ((7, 10, 23), 4, (107552024, 101058073, 74058776, 101058586, 102106907)),
    ((6, 25), 3, (112728600, 76091672, 100993817)),
    ((24, 42, 241), 4, (109711128, 77141272, 109579801, 116197914)),
    ((25, 26, 153, 250), 6, (116791832, 83434264, 76092440, 101256729, 116923418, 76091418, 109646363, 68748827)),
    ((10, 11), 3, (107614489, 116137752, 74061336, 107616026, 67767066, 107615003, 67766043)),
    ((59, 91, 188, 238, 255), 7, (117120024, 67834392, 110893850, 114956825, 101389595, 76222746, 101389085, 78318873, 116197404, 116198174)),
    ((42, 93, 109, 124, 141, 234, 238, 255), 12, (117311257, 101583899, 116988952, 76156952, 83696667, 116197662, 110891546, 69014814, 109841180, 101321247, 111941149, 80484124, 114038304)),
    ((61, 161, 165, 185, 191, 193, 207, 222, 223, 229, 232, 235, 236, 252, 253, 254, 493), 7, (107810072, 117251353, 67966233, 111875355, 114099738, 112006684, 132983574, 132983831, 132982546, 132982803, 132983317, 132983060, 33554441, 33554438, 33554440, 33554443, 33554442, 33554439)),
    ((14, 93, 108, 127, 192, 194, 206, 210, 211, 222, 223, 224, 239, 254, 255, 494), 13, (82909444, 83826945, 82582272, 68029954, 82844165, 83827205, 82583043, 68029697, 117311512, 133047825, 82516994, 68030211, 133046797, 83696386, 111022873, 133047568, 101585671, 83823879, 111939354, 133047054, 101585414, 109842971, 83823622, 133048853, 133046540, 80611605, 133048339, 117379082, 133049110, 80611862, 133048596, 133048082, 133047311, 133049367, 134217728, 33554443, 33554440, 33554441)),
    ((13, 14, 79, 193, 207, 223, 254, 255, 495), 12, (81795584, 79698178, 69081093, 83824387, 83761412, 82708225, 83824130, 101650201, 83171845, 133112076, 101517080, 83759628, 101649690, 109909019, 107680540, 133112590, 133112847, 133113104, 133112333, 133113361, 134217728)),
    ((1, 238, 255), 3, (117311000, 100668441, 101585178)),
    ((18, 225, 238), 5, (101779480, 115874329, 68030489, 69015065, 115148826)),
    ((19,), 1, (101844760, 101845785)),
    ((4, 20), 2, (100861464, 101910809, 101910042)),
    ((6, 8, 21, 28), 6, (116988440, 82123544, 73142040, 100993562, 109580057, 101976603)),
    ((22, 239), 2, (102041112, 102041625, 117379354)),
    ((23, 27, 233), 3, (108663832, 68814872, 102107673, 108662298)),
    ((24, 229), 2, (102172440, 102565401)),
    ((8, 9, 58, 233, 255), 5, (109580568, 109581850, 117311769, 110759963, 78190107, 102238748)),
    ((9, 59, 233, 236, 244), 5, (109776152, 108596249, 102303771, 102435098, 110695964)),
    ((26, 203, 221), 5, (115940121, 75107353, 102503960, 81529368, 102372634)),
    ((75, 76, 170, 204, 235), 6, (102437912, 111810841, 77272345, 101322779, 68752923, 111809050, 77270042, 112920092)),
    ((92, 109, 205, 222), 6, (116202264, 77336344, 111940377, 101521178, 102504219, 81529627)),
    ((15, 76, 91, 236, 237, 238), 8, (114826009, 112925210, 102699288, 76288282, 102568987, 78319897, 102568476, 82642460, 115149085)),
    ((30, 126, 176, 195, 207, 210, 222, 236, 238, 239, 240, 248, 255, 510), 8, (102635275, 101586457, 82709017, 116202520, 77467672, 102634504, 134097686, 82776086, 102634247, 134097172, 81659924, 134096915, 82775315, 102633990, 134096658, 81659667, 134097943, 81659410, 82776343, 134097429, 33554441, 33554442)),
    ((95, 207, 238, 239, 245, 511), 16, (82843648, 82581761, 68096004, 83757829, 82712578, 81861378, 83368195, 68094976, 82778371, 82778625, 115678233, 69014297, 114432536, 134161423, 116071962, 68031759, 81727768, 69015322, 134161166, 107877403, 134160909, 134161937, 134160652, 134161680, 134217728)),
)

LEFT, RIGHT0, RIGHT1 = CHUNKS, 2 * CHUNKS, 3 * CHUNKS
SIZE = 384 // CHUNKS
MAX_SENDS = max(len(p[2]) for p in PLAN)
MAX_FROM = max(1, max(len(p[0]) for p in PLAN))
MESH = pl.DeviceIdType.MESH


def nt_dot(left, right):
    return lax.dot_general(left, right, (((1,), (1,)), ((), ())), preferred_element_type=jnp.float32)


def choose(index, low, high, leaf):
    if all(PLAN[i] == PLAN[low] for i in range(low, high)):
        leaf(PLAN[low])
        return
    middle = (low + high) // 2

    @pl.when(index < middle)
    def _():
        choose(index, low, middle, leaf)

    @pl.when(index >= middle)
    def _():
        choose(index, middle, high, leaf)


def kernel(upper_ref, mask_hbm, out_ref, buf, acc, mask_ref, table, origin, count, in_sem, send_sem, recv_sem):
    brow, column = lax.axis_index("brow"), lax.axis_index("bcol")
    row, half = brow // 2, brow % 2
    own = buf.at[pl.ds(0, 384)]
    load = pltpu.make_async_copy(upper_ref, own, in_sem.at[0])
    load.start()
    load_mask = pltpu.make_async_copy(mask_hbm, mask_ref, in_sem.at[1])
    load_mask.start()

    def leaf(plan):
        origins, targets, sends = plan
        count[0] = len(origins)
        count[1] = targets
        count[2] = len(sends)
        for i, v in enumerate(origins):
            origin[i] = v
        for i, v in enumerate(sends):
            table[i] = v

    choose(row * 16 + column, 0, 256, leaf)
    sends = count[2]
    barrier = pltpu.get_barrier_semaphore()

    @pl.loop(0, count[0])
    def _(i):
        v = origin[i]
        there = ((v >> 4) & 15) * 2 + (half ^ (v >> 8))
        pl.semaphore_signal(barrier, inc=1, device_id=(there, v & 15), device_id_type=MESH)

    load_mask.wait()
    load.wait()
    for i in range(3):
        for j in range(6):
            keep = mask_ref[i, j].astype(jnp.float32)
            at = (pl.ds(i * 128, 128), pl.ds(j * 128, 128))
            buf[at] = (buf[at].astype(jnp.float32) * keep).astype(jnp.bfloat16)

    @pl.when(count[1] > 0)
    def _():
        pl.semaphore_wait(barrier, count[1])

    def slot(index):
        return buf.at[pl.ds(pl.multiple_of(index * SIZE, SIZE), SIZE)]

    def copy(v, i):
        there = ((v >> 20) & 15) * 2 + (half ^ ((v >> 24) & 1))
        return pltpu.make_async_remote_copy(
            src_ref=slot(v & 255),
            dst_ref=slot((v >> 8) & 255),
            send_sem=send_sem.at[i],
            recv_sem=recv_sem.at[(v >> 8) & 255],
            device_id=(there, (v >> 16) & 15),
            device_id_type=MESH,
        )

    def arrived(index):
        pltpu.make_async_copy(slot(index), slot(index), recv_sem.at[index]).wait()

    has0 = (row == 0) | ((column >= row) & (row + column >= 16))
    has1 = (column < 15) & ((row <= 1) | ((column + 1 >= row) & (row + column >= 16)))
    here = pl.ds(pl.multiple_of(half * 384, 128), 384)
    other = pl.ds(pl.multiple_of(384 - half * 384, 128), 384)

    def rows(index):
        return buf[pl.ds(pl.multiple_of(index * SIZE, SIZE), 384), :]

    def first_term():
        right = jnp.where(row + column == 0, 0, RIGHT0)
        acc[:, here] = nt_dot(rows(0), rows(right))

        @pl.loop(0, CHUNKS)
        def _(j):
            arrived(SIB + j)

        acc[:, other] = nt_dot(rows(0), rows(SIB))

    @pl.loop(0, sends)
    def _(i):
        v = table[i]

        @pl.when((v & (1 << 25)) != 0)
        def _():
            arrived(v & 255)

        @pl.when((v & (1 << 26)) != 0)
        def _():
            copy(v, i).start()

        @pl.when((v & (1 << 27)) != 0)
        def _():
            first_term()

    @pl.when(has1)
    def _():
        left = jnp.where(column == 0, RIGHT1, LEFT)
        for columns, right in ((here, RIGHT1), (other, SIB + CHUNKS)):
            if right != RIGHT1:

                @pl.loop(0, CHUNKS)
                def _(j):
                    arrived(SIB + CHUNKS + j)

            term = nt_dot(rows(left), rows(right))

            @pl.when(has0)
            def _():
                out_ref[:, columns] = (acc[:, columns] + term).astype(jnp.bfloat16)

            @pl.when(jnp.logical_not(has0))
            def _():
                out_ref[:, columns] = term.astype(jnp.bfloat16)

    @pl.when(has0 & jnp.logical_not(has1))
    def _():
        out_ref[...] = acc[...].astype(jnp.bfloat16)

    @pl.when(jnp.logical_not(has0 | has1))
    def _():
        out_ref[...] = jnp.zeros_like(out_ref)

    @pl.loop(0, sends)
    def _(i):
        v = table[i]

        @pl.when((v & (1 << 26)) != 0)
        def _():
            copy(v, i).wait_send()


def per_device(upper_store, block_mask):
    return pl.pallas_call(
        kernel,
        out_shape=jax.ShapeDtypeStruct((384, 768), jnp.bfloat16),
        in_specs=[pl.BlockSpec(memory_space=pl.ANY)] * 2,
        out_specs=pl.BlockSpec(memory_space=pltpu.VMEM),
        scratch_shapes=[
            pltpu.VMEM((SLOTS * SIZE, 768), jnp.bfloat16),
            pltpu.VMEM((384, 768), jnp.float32),
            pltpu.SMEM((3, 6), jnp.int32),
            pltpu.SMEM((MAX_SENDS,), jnp.int32),
            pltpu.SMEM((MAX_FROM,), jnp.int32),
            pltpu.SMEM((3,), jnp.int32),
            pltpu.SemaphoreType.DMA((2,)),
            pltpu.SemaphoreType.DMA((MAX_SENDS,)),
            pltpu.SemaphoreType.DMA((SLOTS,)),
        ],
        compiler_params=pltpu.CompilerParams(
            collective_id=0, has_side_effects=True, vmem_limit_bytes=60 * 2**20
        ),
        name="cannon_steps",
    )(upper_store, block_mask)


def solution(mesh):
    spec = P("brow", "bcol")
    return jax.shard_map(per_device, mesh=mesh, in_specs=(spec, spec), out_specs=spec, check_vma=False)
```

time: 39.1 us -> 39.2 us (level)
  no operation moved by 1% of the time
where the time goes in v5:
time: 39.2 us; the launch traced here: 39 us
  Pallas kernels  37.1 us (95%)
  local copies, waits for them, and re-layouts  1.92 us (5%)
    pallas_call x1, Pallas kernels, per_device(): pl.pallas_call(kernel, out_shape=jax.ShapeDtypeStruct((384, 768), jnp.bfl...  37.1 us
    unnamed x1, local copies, waits for them, and re-layouts  1.92 us

profile of v5, /device:TPU:430, one launch (start us, length us, event | category | flops | bytes accessed | tf_op | source)
XLA Modules:
  0.0 39.0 jit_solution(13649463807016505953)
XLA Ops:
  0.0 37.1 %cannon_steps.1 = bf16[384,768]{1,0:T(8,128)(2,1)} custom-call(bf16[384,768]{1,0:T(8,128)(2,1)} %upper_ref.1, s32[3,6]{1,0:T(4,128)} %mask_hbm.1), custom_call_target="tpu_custom_call" | custom-call | tf_op jit(solution)/shard_map/cannon_steps/pallas_call | solution.py:426
  37.1 1.9 %copy.4 = bf16[384,768]{1,0:T(8,128)(2,1)} copy(bf16[384,768]{1,0:T(8,128)(2,1)} %cannon_steps.1) | data formatting | bytes 1179648
